TPU v7x, 256 devices: a whole 4x4x8 slice. The times are simulated.
256 devices in a mesh: win: 4 (over z_lo), row: 8 (over z_hi, x), col: 8 (over y, core).
Axes of the slice: x: 4, y: 4, z: 8 (z_hi: 2, z_lo: 4; z = z_hi * 4 + z_lo), core: 2. Of those that a mesh axis runs over, the one named last changes fastest.
Arguments:
- record: bfloat16 [32, 512, 12000], P('win', ('row', 'col')), may hold values from -6 to 6
- window_weight: float32 [32], P('win'), may hold values from 0.25 to 4
Outputs:
- corr: bfloat16 [8, 4, 16, 8, 64, 4000], P('row', 'win', None, None, 'col')
All inputs are finite; a program needn't handle non-finite values.
Results may differ from a plain program's by a relative error of at most 0.0081.
Values may be sent and summed in bfloat16 or wider, within the bound.
No kernel may reach another device: no remote copies, remote signals or barrier semaphores. Data moves between devices by JAX's collectives and lax.ppermute only.
A program may use at most 192 MiB of HBM per device.

v0:
```python
import math

import jax
import jax.numpy as jnp
from jax import lax
from jax.sharding import PartitionSpec as P

BINS = 512
LAGS = 4000
FIRST_BIN = 60
SMOOTH = 64


def time_taper(length):
    index = jnp.arange(length, dtype=jnp.int32)
    edge = jnp.minimum(index, length - 1 - index).astype(jnp.float32)
    ramp = max(length // 20, 1)
    return jnp.where(edge < ramp, 0.5 - 0.5 * jnp.cos(jnp.pi * (edge + 0.5) / ramp), 1.0)


def band_taper(bins):
    index = jnp.arange(bins, dtype=jnp.int32)
    edge = jnp.minimum(index, bins - 1 - index).astype(jnp.float32)
    ramp = max(bins // 16, 1)
    return jnp.where(edge < ramp, 0.5 - 0.5 * jnp.cos(jnp.pi * (edge + 1.0) / (ramp + 1.0)), 1.0)


def fourier_table(length, bins, first):
    times = jnp.arange(length, dtype=jnp.int32)
    freqs = jnp.arange(bins, dtype=jnp.int32) + first
    phase = jnp.mod(times[:, None] * freqs[None, :], length).astype(jnp.float32)
    angle = 2.0 * jnp.pi / length * phase
    return jnp.concatenate([jnp.cos(angle), -jnp.sin(angle)], axis=1).astype(jnp.bfloat16)


def lag_table(length, bins, first, lags):
    shifts = jnp.arange(lags, dtype=jnp.int32) - lags // 2
    freqs = jnp.arange(bins, dtype=jnp.int32) + first
    phase = jnp.mod(freqs[:, None] * shifts[None, :], length).astype(jnp.float32)
    angle = 2.0 * jnp.pi / length * phase
    return jnp.concatenate([jnp.cos(angle), -jnp.sin(angle)], axis=0).astype(jnp.bfloat16)


def smoother(bins, half):
    index = jnp.arange(bins, dtype=jnp.int32)
    inside = (jnp.abs(index[:, None] - index[None, :]) <= half).astype(jnp.float32)
    return inside / jnp.sum(inside, axis=0, keepdims=True)


def whiten(record, weights):
    windows, channels, length = record.shape
    values = record.astype(jnp.float32)
    centered = ((values - jnp.mean(values, axis=2, keepdims=True)) * time_taper(length)).astype(
        jnp.bfloat16
    )
    table = fourier_table(length, BINS, FIRST_BIN)
    spectrum = jnp.dot(centered.reshape(-1, length), table, preferred_element_type=jnp.float32) * (
        1.0 / math.sqrt(length)
    )
    real_part = spectrum[:, :BINS]
    imag_part = spectrum[:, BINS:]
    power = real_part * real_part + imag_part * imag_part
    smoothed = jnp.dot(
        power,
        smoother(BINS, SMOOTH),
        precision=lax.Precision.HIGHEST,
        preferred_element_type=jnp.float32,
    )
    gain = band_taper(BINS)[None, :] / jnp.sqrt(smoothed + 1e-05)
    whitened = (spectrum * jnp.concatenate([gain, gain], axis=1)).reshape(
        windows, channels, 2 * BINS
    )
    plain = whitened.astype(jnp.bfloat16)
    weighted = (whitened * weights[:, None, None]).astype(jnp.bfloat16)
    return (plain, weighted)


def cross(rows, cols):
    row_re = rows[..., :BINS]
    row_im = rows[..., BINS:]
    col_re = cols[..., :BINS]
    col_im = cols[..., BINS:]
    real_part = jnp.einsum(
        "wif,wjf->ijf", row_re, col_re, preferred_element_type=jnp.float32
    ) + jnp.einsum("wif,wjf->ijf", row_im, col_im, preferred_element_type=jnp.float32)
    imag_part = jnp.einsum(
        "wif,wjf->ijf", row_im, col_re, preferred_element_type=jnp.float32
    ) - jnp.einsum("wif,wjf->ijf", row_re, col_im, preferred_element_type=jnp.float32)
    return jnp.concatenate([real_part, imag_part], axis=2)


def regroup(gathered, outer, inner, local_windows):
    width = gathered.shape[2]
    split = gathered.reshape(outer, inner, local_windows, gathered.shape[1], width)
    return split.transpose(0, 2, 1, 3, 4).reshape(
        outer * local_windows, inner * gathered.shape[1], width
    )


def shards(record, window_weight):
    local_windows, channels, length = record.shape
    plain, weighted = whiten(record, window_weight)
    win_count = lax.axis_size("win")
    row_count = lax.axis_size("row")
    col_count = lax.axis_size("col")
    win_place = lax.axis_index("win")
    quarter_rows = channels * col_count // win_count
    every_rows = lax.all_gather(weighted, ("win", "col"), axis=0, tiled=True)
    row_block = regroup(every_rows, win_count, col_count, local_windows)
    rows = lax.dynamic_slice_in_dim(row_block, win_place * quarter_rows, quarter_rows, 1)
    every_cols = lax.all_gather(plain, ("win", "row"), axis=0, tiled=True)
    cols = regroup(every_cols, win_count, row_count, local_windows)
    summed = cross(rows, cols)
    stacked = summed.astype(jnp.bfloat16)
    table = lag_table(length, BINS, FIRST_BIN, LAGS)
    scale = 1.0 / math.sqrt(BINS * local_windows * win_count)
    lagged = (
        jnp.dot(stacked.reshape(-1, 2 * BINS), table, preferred_element_type=jnp.float32) * scale
    )
    return lagged.astype(jnp.bfloat16).reshape(1, 1, quarter_rows, row_count, channels, LAGS)


def solution(mesh):
    placed = (P("win", ("row", "col"), None), P("win"))
    return jax.shard_map(
        shards,
        mesh=mesh,
        in_specs=placed,
        out_specs=P("row", "win", None, None, "col", None),
        check_vma=False,
    )
```

profile of v0, /device:TPU:6, one launch (start us, length us, event | category | flops | bytes accessed | tf_op | source)
XLA Modules:
  0.0 459.0 jit_solution(145965661989781347)
XLA Ops:
  6.5 0.0 all-gather.5.cloned.1.call-start
  6.5 0.2 subtract_select_fusion
  6.7 0.1 convert_reduce_fusion.1
  6.9 0.0 copy-start.3
  6.9 103.7 %cosine_convert_fusion = (bf16[12000,512]{1,0:T(8,128)(2,1)}, bf16[12000,512]{1,0:T(8,128)(2,1)}) fusion(s32[512]{0:T(512)S(1)} %iota_add_fusion.1), kind=kLoop, calls=%fused_computation.8 | loop fusion | flops 73728000 | bytes 24578048 | tf_op jit(solution)/shard_map/convert.8
  110.6 0.0 copy-done.3
  110.6 0.3 convert_reduce_fusion
  110.9 10.4 %fusion.28 = f32[64,1024]{1,0:T(8,128)S(1)} fusion(bf16[12000,512]{1,0:T(8,128)(2,1)} %get-tuple-element.12, bf16[12000,512]{1,0:T(8,128)(2,1)} %get-tuple-element.11, bf16[8,8,12000]{2,1,0:T(8,128)(2,1)S(1)} %copy-done.3, f32[12000]{0:T(1024)S(1)} %subtract_select_fusion, f32[8,8]{1,0:T(8,128)S(1)} %broadcast_multiply_fusion), kind=kOutput, calls=%fused_computation.42 | convolution fusion | flops 1625153536 | bytes 26422400 | tf_op jit(solution)/shard_map/dot_general | solution.py:57
  121.3 0.0 copy-start.4
  121.3 0.8 fusion.34
  122.1 0.0 copy-done.4
  122.1 0.7 multiply_convert_fusion.1
  122.8 0.0 all-gather.5.cloned.1.call-update
  122.9 0.2 all-gather.3.cloned.1.call-start
  123.1 0.7 fusion.38
  123.8 0.0 all-gather.3.cloned.1.call-update
  123.8 36.4 %cosine_convert_fusion.1 = (bf16[512,4000]{1,0:T(8,128)(2,1)}, bf16[512,4000]{1,0:T(8,128)(2,1)}) fusion(s32[4000]{0:T(1024)S(1)} %iota_add_fusion, s32[512]{0:T(512)S(1)} %iota_add_fusion.1), kind=kLoop, calls=%fused_computation.21 | loop fusion | flops 24576000 | bytes 8210048 | tf_op jit(solution)/shard_map/convert
  160.3 29.0 %all-gather.5.cloned.1.call-done = bf16[256,8,1024]{2,1,0:T(8,128)(2,1)} async-done(((bf16[8,8,1024]{2,1,0:T(8,128)(2,1)}), bf16[256,8,1024]{2,1,0:T(8,128)(2,1)}) %all-gather.5.cloned.1.call-update) | async-done | bytes 4194320 | tf_op jit(solution)/shard_map/all_gather | solution.py:108
  189.3 2.6 copy.30
  191.9 0.1 constant_dynamic-slice_fusion
  192.1 2.2 copy.37
  194.3 188.8 %all-gather.3.cloned.1.call-done = bf16[256,8,1024]{2,1,0:T(8,128)(2,1)} async-done(((bf16[8,8,1024]{2,1,0:T(8,128)(2,1)}), bf16[256,8,1024]{2,1,0:T(8,128)(2,1)}) %all-gather.3.cloned.1.call-update) | async-done | bytes 4194320 | tf_op jit(solution)/shard_map/all_gather | solution.py:111
  383.0 2.6 copy.28
  385.7 2.6 fusion.48
  388.3 7.4 %copy.38 = bf16[32,64,512]{1,0,2:T(8,128)(2,1)} copy(bf16[32,64,512]{2,1,0:T(8,128)(2,1)} %get-tuple-element.6) | data formatting | bytes 4194304
  395.7 3.1 copy.39
  398.8 7.4 %copy.40 = bf16[32,64,512]{1,0,2:T(8,128)(2,1)} copy(bf16[32,64,512]{2,1,0:T(8,128)(2,1)} %get-tuple-element.5) | data formatting | bytes 4194304
  406.2 0.0 copy-start.1
  406.2 0.0 copy-start.2
  406.2 3.6 fusion.49
  409.8 0.0 copy-done.1
  409.8 0.5 copy-done.2
  410.3 0.0 copy-start
  410.3 3.2 fusion.50
  413.5 0.0 copy-done
  413.5 2.6 fusion.22
  416.1 2.5 copy.33
  418.6 6.0 %fusion.23 = bf16[16,64,512]{1,0,2:T(8,128)(2,1)} fusion(f32[512,64,16]{1,2,0:T(8,128)} %fusion.50, bf16[32,16,512]{0,1,2:T(8,128)(2,1)S(1)} %copy.37, bf16[32,64,512]{1,0,2:T(8,128)(2,1)} %copy.40), kind=kOutput, calls=%fused_computation.36 | convolution fusion | flops 34603008 | bytes 5767168 | tf_op jit(solution)/shard_map/wif,wjf->ijf/dot_general | solution.py:88
  424.6 2.5 copy.34
  427.1 13.3 %multiply_convert_fusion = bf16[1024,4000]{0,1:T(8,128)(2,1)} fusion(bf16[512,4000]{1,0:T(8,128)(2,1)} %get-tuple-element.10, bf16[512,4000]{1,0:T(8,128)(2,1)} %get-tuple-element.9, bf16[1024,512]{1,0:T(8,128)(2,1)S(1)} %bitcast.39, bf16[1024,512]{1,0:T(8,128)(2,1)S(1)} %bitcast.38), kind=kOutput, calls=%fused_computation.13 | convolution fusion | flops 8417378304 | bytes 18481152 | tf_op jit(solution)/shard_map/dot_general | solution.py:118
  440.5 11.7 %copy.35 = bf16[1024,4000]{1,0:T(8,128)(2,1)} copy(bf16[1024,4000]{0,1:T(8,128)(2,1)} %multiply_convert_fusion) | data formatting | bytes 16384000 | tf_op jit(solution)/shard_map/convert_element_type | solution.py:120
  (4 shorter events, 0.1 us)
Async XLA Ops:
  6.5 182.8 %all-gather.5.cloned.1.call-start = ((), (), s32[]{:S(2)}) async-start(), calls=%async_computation.1 | async-start | bytes 4325376 | tf_op jit(solution)/shard_map/all_gather | solution.py:108
  6.9 103.7 %copy-start.3 = (bf16[8,8,12000]{2,1,0:T(8,128)(2,1)S(1)}, bf16[8,8,12000]{2,1,0:T(8,128)(2,1)}, u32[]{:S(2)}) copy-start(bf16[8,8,12000]{2,1,0:T(8,128)(2,1)} %param.2) | copy-start | bytes 4608004
  121.3 0.8 copy-start.4
  122.9 260.2 %all-gather.3.cloned.1.call-start = ((), (), s32[]{:S(2)}) async-start(), calls=%async_computation | async-start | bytes 4325376 | tf_op jit(solution)/shard_map/all_gather | solution.py:111
  406.2 3.6 copy-start.1
  406.2 4.1 copy-start.2
  410.3 3.2 copy-start
Sparse Core Ops, SparseCore 0:
  123.0 66.2 all-gather.4
  191.1 191.9 all-gather.2
where the time goes:
time: 460 us; the launch traced here: 459 us
  waiting for transfers between devices  218 us (47%)
  other arithmetic  142 us (31%)
  local copies, waits for them, and re-layouts  45.4 us (10%)
  matrix products  39.8 us (9%)
  between operations  13.5 us (3%)
    all_gather x1, waiting for transfers between devices, shards(): every_cols = lax.all_gather(plain, ('win', 'row'), axis=0, tiled=True)  189 us
    another operation x2, other arithmetic  140 us
    all_gather x1, waiting for transfers between devices, shards(): every_rows = lax.all_gather(weighted, ('win', 'col'), axis=0, tiled=True)  29 us
    unnamed x14, local copies, waits for them, and re-layouts  20.7 us
    dot_general x1, matrix products, shards(): jnp.dot(stacked.reshape(-1, 2 * BINS), table, preferred_element_type=jnp....  13.3 us
    convert_element_type x1, local copies, waits for them, and re-layouts, shards(): lagged.astype(jnp.bfloat16)  11.7 us
    dot_general x1, matrix products, whiten(): jnp.dot(centered.reshape(-1, length), table, preferred_element_type=jnp.f...  10.4 us
  transfers between devices with their start and end apart: 2, of which 2 were waited for; matrix products, arithmetic and copies ran while one was open for 9% of the time, Pallas kernels for 0%

commit v1 on v0

v1 whole, which is shorter than its diff:
```python
import math

import jax
import jax.numpy as jnp
import ml_dtypes
import numpy as np
from jax import lax
from jax.experimental import pallas as pl
from jax.experimental.pallas import tpu as pltpu
from jax.sharding import PartitionSpec as P

SAMPLES = 12000
QUARTER = 3000
BINS = 512
LAGS = 4000
LAGS_PAD = 4096
FIRST_BIN = 60
SMOOTH = 64
AXES = ("win", "row", "col")
OFFSETS = (0, -1, 1, -2, 2, -3, 3, -4)
BINS_AT = np.concatenate([np.arange(0, 512, 4), np.arange(2, 512, 4), np.arange(1, 512, 2)])
PHASE = 2.0 * np.pi / SAMPLES


def bf16(values):
    return values.astype(np.float32).astype(ml_dtypes.bfloat16)


def time_taper():
    index = np.arange(SAMPLES)
    edge = np.minimum(index, SAMPLES - 1 - index).astype(np.float64)
    ramp = max(SAMPLES // 20, 1)
    return np.where(edge < ramp, 0.5 - 0.5 * np.cos(np.pi * (edge + 0.5) / ramp), 1.0).astype(
        np.float32
    )


def band_taper():
    index = np.arange(BINS)
    edge = np.minimum(index, BINS - 1 - index).astype(np.float64)
    ramp = max(BINS // 16, 1)
    return np.where(edge < ramp, 0.5 - 0.5 * np.cos(np.pi * (edge + 1.0) / (ramp + 1.0)), 1.0).astype(
        np.float32
    )


def waves(bins):
    angle = PHASE * np.mod(np.arange(QUARTER)[:, None] * (bins + FIRST_BIN)[None, :], SAMPLES)
    return np.cos(angle), np.sin(angle)


def even_table(bins):
    cos, sin = waves(bins)
    return bf16(np.concatenate([cos, -sin], axis=1))


def odd_table(bins):
    cos, sin = waves(bins)
    turn = np.where((bins + FIRST_BIN) % 4 == 1, 1.0, -1.0)[None, :]
    first = np.concatenate([cos, -sin], axis=1)
    second = np.concatenate([-turn * sin, -turn * cos], axis=1)
    return bf16(np.concatenate([first, second], axis=0))


def lag_table():
    shifts = np.arange(LAGS) - LAGS // 2
    angle = PHASE * np.mod((BINS_AT + FIRST_BIN)[:, None] * shifts[None, :], SAMPLES)
    table = np.zeros((2 * BINS, LAGS_PAD))
    table[:BINS, :LAGS] = np.cos(angle)
    table[BINS:, :LAGS] = -np.sin(angle)
    return bf16(table)


def smoother():
    index = np.arange(BINS)
    inside = (np.abs(index[:, None] - index[None, :]) <= SMOOTH).astype(np.float32)
    mean = inside / np.sum(inside, axis=0, keepdims=True, dtype=np.float32)
    return mean[BINS_AT][:, BINS_AT]


def whiten(record, weights):
    windows, channels, length = record.shape
    values = record.reshape(windows * channels, length).astype(jnp.float32)
    centered = (values - jnp.mean(values, axis=1, keepdims=True)) * time_taper()[None, :]
    centered = centered.astype(jnp.bfloat16).astype(jnp.float32)
    part = [centered[:, QUARTER * q : QUARTER * (q + 1)] for q in range(4)]
    sum02, dif02 = part[0] + part[2], part[0] - part[2]
    sum13, dif13 = part[1] + part[3], part[1] - part[3]
    even0 = (sum02 + sum13).astype(jnp.bfloat16)
    even2 = (sum02 - sum13).astype(jnp.bfloat16)
    odd = jnp.concatenate([dif02, dif13], axis=1).astype(jnp.bfloat16)

    def product(left, table):
        return jnp.dot(left, table, preferred_element_type=jnp.float32)

    spec0 = product(even0, even_table(BINS_AT[:128]))
    spec2 = product(even2, even_table(BINS_AT[128:256]))
    spec1 = product(odd, odd_table(BINS_AT[256:]))
    scale = 1.0 / math.sqrt(length)
    real_part = jnp.concatenate([spec0[:, :128], spec2[:, :128], spec1[:, :256]], axis=1) * scale
    imag_part = jnp.concatenate([spec0[:, 128:], spec2[:, 128:], spec1[:, 256:]], axis=1) * scale
    power = real_part * real_part + imag_part * imag_part
    smoothed = jnp.dot(
        power,
        smoother(),
        precision=lax.Precision.HIGHEST,
        preferred_element_type=jnp.float32,
    )
    gain = band_taper()[BINS_AT][None, :] / jnp.sqrt(smoothed + 1e-05)
    whitened = jnp.concatenate([real_part * gain, imag_part * gain], axis=1)
    whitened = whitened.reshape(windows, channels, 2 * BINS)
    plain = whitened.astype(jnp.bfloat16)
    weighted = (whitened * weights[:, None, None]).astype(jnp.bfloat16)
    return plain, weighted


def device_at(x, y, z, core):
    return ((z % 4) * 8 + (z // 4) * 4 + x) * 8 + y * 2 + core


def shift(value, dx=0, dy=0, dz=0, dcore=0):
    pairs = [
        (
            device_at(x, y, z, core),
            device_at((x + dx) % 4, (y + dy) % 4, (z + dz) % 8, (core + dcore) % 2),
        )
        for x in range(4)
        for y in range(4)
        for z in range(8)
        for core in range(2)
    ]
    return lax.ppermute(value, AXES, pairs)


def ring_z(own):
    blocks = [own]
    up = down = own
    for step in range(1, 5):
        up = shift(up, dz=1)
        blocks.append(up)
        if step < 4:
            down = shift(down, dz=-1)
            blocks.append(down)
    return blocks


def spread_x(own):
    return [own, shift(own, dx=1), shift(own, dx=-1), shift(own, dx=2)]


def gather_cols(plain):
    half = plain.shape[0] // 2
    first = spread_x(jnp.stack(ring_z(plain[:half])))
    second = ring_z(jnp.stack(spread_x(plain[half:])))
    return jnp.stack(first), jnp.stack(second)


def gather_rows(weighted, y, z_low):
    held = jnp.stack([weighted] + [shift(weighted, dy=k) for k in (1, 2, 3)])

    def for_offset(k):
        return lax.dynamic_index_in_dim(held, (y - z_low - k) % 4, 0, keepdims=False)

    moved = [for_offset(0)]
    for k in (1, 2, 3):
        moved.append(lax.ppermute(for_offset(k), "win", [(i, (i + k) % 4) for i in range(4)]))
    mine = jnp.stack(moved)
    return mine, shift(mine, dcore=1)


def pair_kernel(place, first, second, mine, other, table, out, z_re, z_im, z_sum, stack):
    chunk = pl.program_id(0)

    @pl.when(chunk == 0)
    def _():
        core = place[16]
        for k in range(4):
            group = place[12 + k]
            for ref, at in ((mine, core), (other, 1 - core)):
                for w in range(8):
                    value = ref[k, w].astype(jnp.float32)
                    re, im = value[:, :BINS], value[:, BINS:]
                    z_re[group * 8 + w, at] = re
                    z_im[group * 8 + w, at] = im
                    z_sum[group * 8 + w, at] = re + im

    def cross_block(lane, block):
        lane_im = pl.multiple_of(lane + BINS, 128)
        core, base = block // 2, (block % 2) * 4

        def group_step(group, sums):
            sums = list(sums)
            at = [place[4 + group], place[8 + group]]
            for w in range(8):
                source, v = (first, w) if w < 4 else (second, w - 4)
                yr, yi = [], []
                for high in range(2):
                    where = (0, at[high], v) if w < 4 else (at[high], 0, v)
                    yr.append(source[(*where, slice(None), pl.ds(lane, 128))].astype(jnp.float32))
                    yi.append(source[(*where, slice(None), pl.ds(lane_im, 128))].astype(jnp.float32))
                dif = [yr[0] - yi[0], yr[1] - yi[1]]
                window = group * 8 + w
                for i in range(4):
                    row = pl.ds(base + i, 1)
                    zr = jnp.broadcast_to(z_re[window, core, row, pl.ds(lane, 128)], (8, 128))
                    zi = jnp.broadcast_to(z_im[window, core, row, pl.ds(lane, 128)], (8, 128))
                    zs = jnp.broadcast_to(z_sum[window, core, row, pl.ds(lane, 128)], (8, 128))
                    for high in range(2):
                        n = (i * 2 + high) * 3
                        sums[n] = sums[n] + zr * yr[high]
                        sums[n + 1] = sums[n + 1] + zi * yi[high]
                        sums[n + 2] = sums[n + 2] + zs * dif[high]
            return tuple(sums)

        sums = lax.fori_loop(0, 4, group_step, (jnp.zeros((8, 128), jnp.float32),) * 24)
        for i in range(4):
            re, im = [], []
            for high in range(2):
                p, q, r = sums[(i * 2 + high) * 3 : (i * 2 + high) * 3 + 3]
                re.append(p + q)
                im.append(r - p + q)
            row = pl.ds((block * 4 + i) * 16, 16)
            stack[row, pl.ds(lane, 128)] = jnp.concatenate(re, axis=0).astype(jnp.bfloat16)
            stack[row, pl.ds(lane_im, 128)] = jnp.concatenate(im, axis=0).astype(jnp.bfloat16)

    def cross(tile, carry):
        lane = pl.multiple_of(tile * 128, 128)
        for block in range(4):
            cross_block(lane, block)
        return carry

    lax.fori_loop(0, 4, cross, 0)
    width = 512
    for tile in range(LAGS_PAD // width):
        start = tile * width
        keep = min(width, LAGS - start)
        value = jnp.dot(
            stack[...], table[:, start : start + width], preferred_element_type=jnp.float32
        )
        value = value * (1.0 / 128.0)
        value = value.reshape(16, 2, 1, 8, width).astype(jnp.bfloat16)
        out[:, :, :, :, start : start + keep] = value[..., :keep]


def pair_correlations(place, first, second, mine, other):
    whole = pl.BlockSpec(memory_space=pltpu.VMEM)
    return pl.pallas_call(
        pair_kernel,
        out_shape=jax.ShapeDtypeStruct((16, 2, 4, 8, LAGS), jnp.bfloat16),
        grid_spec=pltpu.PrefetchScalarGridSpec(
            num_scalar_prefetch=1,
            grid=(4,),
            in_specs=[
                pl.BlockSpec((1, 8, 4, 8, 2 * BINS), lambda j, place: (j, 0, 0, 0, 0)),
                pl.BlockSpec((8, 1, 4, 8, 2 * BINS), lambda j, place: (0, j, 0, 0, 0)),
                whole,
                whole,
                whole,
            ],
            out_specs=pl.BlockSpec((16, 2, 1, 8, LAGS), lambda j, place: (0, 0, place[j], 0, 0)),
            scratch_shapes=[
                pltpu.VMEM((32, 2, 8, BINS), jnp.float32),
                pltpu.VMEM((32, 2, 8, BINS), jnp.float32),
                pltpu.VMEM((32, 2, 8, BINS), jnp.float32),
                pltpu.VMEM((256, 2 * BINS), jnp.bfloat16),
            ],
        ),
        compiler_params=pltpu.CompilerParams(vmem_limit_bytes=48 * 1024 * 1024),
        cost_estimate=pl.CostEstimate(
            flops=2 * 1024 * 1024 * LAGS, bytes_accessed=24 * 2**20, transcendentals=0
        ),
    )(place, first, second, mine, other, lag_table())


def shards(record, window_weight):
    plain, weighted = whiten(record, window_weight)
    z_low = lax.axis_index("win")
    row = lax.axis_index("row")
    col = lax.axis_index("col")
    z_high, x = row // 4, row % 4
    z = z_high * 4 + z_low
    mine, other = gather_rows(weighted, col // 2, z_low)
    first, second = gather_cols(plain)
    slots = np.zeros(8, np.int32)
    for slot, offset in enumerate(OFFSETS):
        slots[offset % 8] = slot
    slot_of = jnp.asarray(slots)[(jnp.arange(8) - z) % 8]
    place = jnp.concatenate(
        [
            (x + jnp.array([0, -1, 1, 2])) % 4,
            slot_of,
            (z_low - jnp.arange(4)) % 4,
            jnp.stack([col % 2]),
        ]
    ).astype(jnp.int32)
    corr = pair_correlations(place, first, second, mine, other)
    return corr.reshape(1, 1, 16, 8, 8, LAGS)


def solution(mesh):
    placed = (P("win", ("row", "col"), None), P("win"))
    return jax.shard_map(
        shards,
        mesh=mesh,
        in_specs=placed,
        out_specs=P("row", "win", None, None, "col", None),
        check_vma=False,
    )
```

time: 460 us -> 127 us (0.28)
  waiting for transfers between devices: 218 us -> 40.3 us
  other arithmetic: 142 us -> 3.91 us
  local copies, waits for them, and re-layouts: 45.4 us -> 3.12 us
  starting transfers between devices: 0.22 us -> 41.1 us
  matrix products: 39.8 us -> 3.74 us
  Pallas kernels: 0 us -> 33.6 us
  between operations: 13.5 us -> 0.46 us
    all_gather x2 -> x0, waiting for transfers between devices: 218 us -> none  [the longest x1 189 us: shards(): every_cols = lax.all_gather(plain, ('win', 'row'), axis=0, tiled=True)]
    another operation x2 -> x4, other arithmetic: 140 us -> 0.43 us  [the longest x1 0.26 us: gather_cols(): return (jnp.stack(first), jnp.stack(second))]
    ppermute x0 -> x27, starting transfers between devices: none -> 41.1 us  [the longest x24 41 us: shift(): return lax.ppermute(value, AXES, pairs)]
    ppermute x0 -> x27, waiting for transfers between devices: none -> 40.3 us  [the longest x24 37.7 us: shift(): return lax.ppermute(value, AXES, pairs)]
    dot_general x7 -> x5, matrix products: 39.8 us -> 3.74 us  [the longest x4 2.96 us: product(): return jnp.dot(left, table, preferred_element_type=jnp.float32)]
    pallas_call x0 -> x1, Pallas kernels: none -> 33.6 us  [pair_correlations(): pl.pallas_call(pair_kernel, out_shape=jax.ShapeDtypeStruct((16, 2, 4, 8,...]
    unnamed x14 -> x33, local copies, waits for them, and re-layouts: 20.7 us -> 2.29 us
    convert_element_type x1 -> x0, local copies, waits for them, and re-layouts: 11.7 us -> none  [shards(): lagged.astype(jnp.bfloat16)]
  transfers between devices with their start and end apart: 2 -> 27, of which waited for: 2 -> 11; matrix products, arithmetic and copies ran while one was open for 9% -> 1% of each run, Pallas kernels for 0% -> 0%
where the time goes in v1:
time: 127 us; the launch traced here: 126 us
  starting transfers between devices  41.1 us (32%)
  waiting for transfers between devices  40.3 us (32%)
  Pallas kernels  33.6 us (26%)
  other arithmetic  3.91 us (3%)
  matrix products  3.74 us (3%)
  local copies, waits for them, and re-layouts  3.12 us (2%)
    ppermute x24, starting transfers between devices, shift(): return lax.ppermute(value, AXES, pairs)  41 us
    ppermute x24, waiting for transfers between devices, shift(): return lax.ppermute(value, AXES, pairs)  37.7 us
    pallas_call x1, Pallas kernels, pair_correlations(): pl.pallas_call(pair_kernel, out_shape=jax.ShapeDtypeStruct((16, 2, 4, 8,...  33.6 us
    dot_general x4, matrix products, product(): return jnp.dot(left, table, preferred_element_type=jnp.float32)  2.96 us
    ppermute x3, waiting for transfers between devices, gather_rows(): lax.ppermute(for_offset(k), 'win', [(i, (i + k) % 4) for i in range(4)])  2.59 us
  transfers between devices with their start and end apart: 27, of which 11 were waited for; matrix products, arithmetic and copies ran while one was open for 1% of the time, Pallas kernels for 0%

profile of v1, /device:TPU:6, one launch (start us, length us, event | category | flops | bytes accessed | tf_op | source)
XLA Modules:
  0.0 126.2 jit_solution(2754910186644972531)
XLA Ops:
  0.0 1.8 %convert_reduce_fusion = f32[8,8]{1,0:T(8,128)S(1)} fusion(bf16[8,8,12000]{2,1,0:T(8,128)(2,1)} %param.11), kind=kLoop, calls=%fused_computation.1 | loop fusion | flops 1535936 | bytes 1536256 | tf_op jit(solution)/shard_map/reduce_sum | solution.py:84
  1.9 0.1 div.38
  1.9 0.0 copy-start.8
  2.0 1.3 %fusion.3 = f32[64,12000]{1,0:T(8,128)S(1)} fusion(bf16[8,8,12000]{2,1,0:T(8,128)(2,1)S(1)} %copy-done.1, f32[12000]{0:T(1024)} %constant.153, f32[64]{0:T(128)S(1)} %div.38), kind=kLoop, calls=%fused_computation.7 | loop fusion | flops 3840000 | bytes 4656256 | tf_op jit(solution)/shard_map/convert_element_type | solution.py:85
  3.3 0.1 copy-done.9
  3.4 0.9 fusion.7
  4.2 0.0 copy-done.8
  4.2 0.9 fusion.6
  5.1 0.2 copy-done.3
  5.3 0.6 fusion.8
  6.0 1.3 copy-done.2
  7.2 0.6 convolution_add_fusion.1
  7.8 0.0 copy-start.7
  7.8 0.0 copy-start
  7.9 0.5 copy-done.4
  8.4 0.8 fusion.13
  9.2 0.1 fusion.10
  9.3 3.1 %collective-permute-start.22 = (bf16[8,8,1024]{2,1,0:T(8,128)(2,1)S(1)}, bf16[8,8,1024]{2,1,0:T(8,128)(2,1)S(1)}, u32[]{:S(2)}, u32[]{:S(2)}) collective-permute-start(bf16[8,8,1024]{2,1,0:T(8,128)(2,1)S(1)} %fusion.10), channel_id=1, source_target_pairs={{0,6},{1,7},{64,70},{65,71},{128,134},{129,135},{192,198},{193,199... | collective-permute-start | bytes 393224 | tf_op jit(solution)/shard_map/ppermute | solution.py:132
  12.4 0.6 collective-permute-start.21
  13.1 0.9 collective-permute-start.11
  14.0 2.4 %collective-permute-start.10 = (bf16[4,8,1024]{2,1,0:T(8,128)(2,1)S(1)}, bf16[4,8,1024]{2,1,0:T(8,128)(2,1)S(1)}, u32[]{:S(2)}, u32[]{:S(2)}) collective-permute-start(bf16[4,8,1024]{2,1,0:T(8,128)(2,1)S(1)} %get-tuple-element.10), channel_id=1, source_target_pairs={{0,8},{1,9},{64,72},{65,73},{128,136},{129,137},{192,200},{193,201... | collective-permute-start | bytes 196616 | tf_op jit(solution)/shard_map/ppermute | solution.py:132
  16.4 0.2 collective-permute-start.12
  16.6 0.1 fusion.9
  16.8 0.6 gather_fusion
  17.5 0.1 pad_add_fusion.place
  17.6 1.1 collective-permute-done.11
  18.7 1.0 collective-permute-start.20
  19.6 1.9 %collective-permute-start = (bf16[4,8,1024]{2,1,0:T(8,128)(2,1)S(1)}, bf16[4,8,1024]{2,1,0:T(8,128)(2,1)S(1)}, u32[]{:S(2)}, u32[]{:S(2)}) collective-permute-start(bf16[4,8,1024]{2,1,0:T(8,128)(2,1)S(1)} %get-tuple-element.11), channel_id=1, source_target_pairs={{0,64},{1,65},{64,128},{65,129},{128,192},{129,193},{192,32},{193,... | collective-permute-start | bytes 196616 | tf_op jit(solution)/shard_map/ppermute | solution.py:132
  21.5 0.6 collective-permute-done.12
  22.2 5.9 %collective-permute-start.1 = (bf16[4,8,1024]{2,1,0:T(8,128)(2,1)S(1)}, bf16[4,8,1024]{2,1,0:T(8,128)(2,1)S(1)}, u32[]{:S(2)}, u32[]{:S(2)}) collective-permute-start(bf16[4,8,1024]{2,1,0:T(8,128)(2,1)S(1)} %get-tuple-element.11), channel_id=1, source_target_pairs={{0,224},{1,225},{64,0},{65,1},{128,64},{129,65},{192,128},{193,129... | collective-permute-start | bytes 196616 | tf_op jit(solution)/shard_map/ppermute | solution.py:132
  28.1 0.0 collective-permute-done
  28.1 0.1 collective-permute-start.13
  28.2 1.8 %collective-permute-done.1 = bf16[4,8,1024]{2,1,0:T(8,128)(2,1)S(1)} collective-permute-done((bf16[4,8,1024]{2,1,0:T(8,128)(2,1)S(1)}, bf16[4,8,1024]{2,1,0:T(8,128)(2,1)S(1)}, u32[]{:S(2)}, u32[]{:S(2)}) %collective-permute-start.1) | collective-permute-done | bytes 65568 | tf_op jit(solution)/shard_map/ppermute | solution.py:132
  29.9 3.6 %collective-permute-start.14 = (bf16[4,4,8,1024]{3,2,1,0:T(8,128)(2,1)S(1)}, bf16[4,4,8,1024]{3,2,1,0:T(8,128)(2,1)S(1)}, u32[]{:S(2)}, u32[]{:S(2)}) collective-permute-start(bf16[4,4,8,1024]{3,2,1,0:T(8,128)(2,1)S(1)} %pad_maximum_fusion.4), channel_id=1, source_target_pairs={{0,224},{1,225},{64,0},{65,1},{128,64},{129,65},{192,128},{193,129... | collective-permute-start | bytes 786440 | tf_op jit(solution)/shard_map/ppermute | solution.py:132
  33.5 0.0 collective-permute-done.22
  33.6 0.1 collective-permute-start.2
  33.6 0.0 collective-permute-done.21
  33.7 3.2 %collective-permute-start.3 = (bf16[4,8,1024]{2,1,0:T(8,128)(2,1)S(1)}, bf16[4,8,1024]{2,1,0:T(8,128)(2,1)S(1)}, u32[]{:S(2)}, u32[]{:S(2)}) collective-permute-start(bf16[4,8,1024]{2,1,0:T(8,128)(2,1)S(1)} %collective-permute-done.1), channel_id=1, source_target_pairs={{0,224},{1,225},{64,0},{65,1},{128,64},{129,65},{192,128},{193,129... | collective-permute-start | bytes 196616 | tf_op jit(solution)/shard_map/ppermute | solution.py:132
  36.9 0.0 collective-permute-done.20
  36.9 0.1 pad_maximum_fusion.1
  37.0 0.1 collective-permute-start.25
  37.1 2.0 %collective-permute-done.2 = bf16[4,8,1024]{2,1,0:T(8,128)(2,1)S(1)} collective-permute-done((bf16[4,8,1024]{2,1,0:T(8,128)(2,1)S(1)}, bf16[4,8,1024]{2,1,0:T(8,128)(2,1)S(1)}, u32[]{:S(2)}, u32[]{:S(2)}) %collective-permute-start.2) | collective-permute-done | bytes 65568 | tf_op jit(solution)/shard_map/ppermute | solution.py:132
  39.1 0.0 collective-permute-start.24
  39.1 0.3 collective-permute-start.4
  39.4 5.2 %collective-permute-done.4 = bf16[4,8,1024]{2,1,0:T(8,128)(2,1)S(1)} collective-permute-done((bf16[4,8,1024]{2,1,0:T(8,128)(2,1)S(1)}, bf16[4,8,1024]{2,1,0:T(8,128)(2,1)S(1)}, u32[]{:S(2)}, u32[]{:S(2)}) %collective-permute-start.4) | collective-permute-done | bytes 65568 | tf_op jit(solution)/shard_map/ppermute | solution.py:132
  44.7 2.1 %collective-permute-start.5 = (bf16[4,8,1024]{2,1,0:T(8,128)(2,1)S(1)}, bf16[4,8,1024]{2,1,0:T(8,128)(2,1)S(1)}, u32[]{:S(2)}, u32[]{:S(2)}) collective-permute-start(bf16[4,8,1024]{2,1,0:T(8,128)(2,1)S(1)} %collective-permute-done.3), channel_id=1, source_target_pairs={{0,224},{1,225},{64,0},{65,1},{128,64},{129,65},{192,128},{193,129... | collective-permute-start | bytes 196616 | tf_op jit(solution)/shard_map/ppermute | solution.py:132
  46.8 2.2 %collective-permute-done.5 = bf16[4,8,1024]{2,1,0:T(8,128)(2,1)S(1)} collective-permute-done((bf16[4,8,1024]{2,1,0:T(8,128)(2,1)S(1)}, bf16[4,8,1024]{2,1,0:T(8,128)(2,1)S(1)}, u32[]{:S(2)}, u32[]{:S(2)}) %collective-permute-start.5) | collective-permute-done | bytes 65568 | tf_op jit(solution)/shard_map/ppermute | solution.py:132
  49.0 0.4 collective-permute-start.6
  49.4 5.1 %collective-permute-done.6 = bf16[4,8,1024]{2,1,0:T(8,128)(2,1)S(1)} collective-permute-done((bf16[4,8,1024]{2,1,0:T(8,128)(2,1)S(1)}, bf16[4,8,1024]{2,1,0:T(8,128)(2,1)S(1)}, u32[]{:S(2)}, u32[]{:S(2)}) %collective-permute-start.6) | collective-permute-done | bytes 65568 | tf_op jit(solution)/shard_map/ppermute | solution.py:132
  54.5 1.7 %collective-permute-start.9 = (bf16[8,4,8,1024]{3,2,1,0:T(8,128)(2,1)S(1)}, bf16[8,4,8,1024]{3,2,1,0:T(8,128)(2,1)S(1)}, u32[]{:S(2)}, u32[]{:S(2)}) collective-permute-start(bf16[8,4,8,1024]{3,2,1,0:T(8,128)(2,1)S(1)} %bitcast_dynamic-update-slice_fusion.8), channel_id=1, source_target_pairs={{0,16},{1,17},{64,80},{65,81},{128,144},{129,145},{192,208},{193,2... | collective-permute-start | bytes 1572872 | tf_op jit(solution)/shard_map/ppermute | solution.py:132
  56.2 2.6 %collective-permute-start.8 = (bf16[8,4,8,1024]{3,2,1,0:T(8,128)(2,1)S(1)}, bf16[8,4,8,1024]{3,2,1,0:T(8,128)(2,1)S(1)}, u32[]{:S(2)}, u32[]{:S(2)}) collective-permute-start(bf16[8,4,8,1024]{3,2,1,0:T(8,128)(2,1)S(1)} %bitcast_dynamic-update-slice_fusion.8), channel_id=1, source_target_pairs={{0,24},{1,25},{64,88},{65,89},{128,152},{129,153},{192,216},{193,2... | collective-permute-start | bytes 1572872 | tf_op jit(solution)/shard_map/ppermute | solution.py:132
  58.8 2.6 %collective-permute-done.23 = bf16[8,8,1024]{2,1,0:T(8,128)(2,1)S(1)} collective-permute-done((bf16[8,8,1024]{2,1,0:T(8,128)(2,1)S(1)}, bf16[8,8,1024]{2,1,0:T(8,128)(2,1)S(1)}, u32[]{:S(2)}, u32[]{:S(2)}) %collective-permute-start.23) | collective-permute-done | bytes 131104 | tf_op jit(solution)/shard_map/ppermute | solution.py:166
  61.4 4.2 %collective-permute-start.7 = (bf16[8,4,8,1024]{3,2,1,0:T(8,128)(2,1)S(1)}, bf16[8,4,8,1024]{3,2,1,0:T(8,128)(2,1)S(1)}, u32[]{:S(2)}, u32[]{:S(2)}) collective-permute-start(bf16[8,4,8,1024]{3,2,1,0:T(8,128)(2,1)S(1)} %bitcast_dynamic-update-slice_fusion.8), channel_id=1, source_target_pairs={{0,8},{1,9},{64,72},{65,73},{128,136},{129,137},{192,200},{193,201... | collective-permute-start | bytes 1572872 | tf_op jit(solution)/shard_map/ppermute | solution.py:132
  65.7 0.1 pad_maximum_fusion.2.mine
  65.7 0.1 collective-permute-start.15
  65.8 3.2 %collective-permute-start.16 = (bf16[4,4,8,1024]{3,2,1,0:T(8,128)(2,1)S(1)}, bf16[4,4,8,1024]{3,2,1,0:T(8,128)(2,1)S(1)}, u32[]{:S(2)}, u32[]{:S(2)}) collective-permute-start(bf16[4,4,8,1024]{3,2,1,0:T(8,128)(2,1)S(1)} %collective-permute-done.14), channel_id=1, source_target_pairs={{0,224},{1,225},{64,0},{65,1},{128,64},{129,65},{192,128},{193,129... | collective-permute-start | bytes 786440 | tf_op jit(solution)/shard_map/ppermute | solution.py:132
  69.1 4.3 %collective-permute-done.15 = bf16[4,4,8,1024]{3,2,1,0:T(8,128)(2,1)S(1)} collective-permute-done((bf16[4,4,8,1024]{3,2,1,0:T(8,128)(2,1)S(1)}, bf16[4,4,8,1024]{3,2,1,0:T(8,128)(2,1)S(1)}, u32[]{:S(2)}, u32[]{:S(2)}) %collective-permute-start.15) | collective-permute-done | bytes 262176 | tf_op jit(solution)/shard_map/ppermute | solution.py:132
  73.4 0.1 collective-permute-start.17
  73.6 3.3 %collective-permute-start.18 = (bf16[4,4,8,1024]{3,2,1,0:T(8,128)(2,1)S(1)}, bf16[4,4,8,1024]{3,2,1,0:T(8,128)(2,1)S(1)}, u32[]{:S(2)}, u32[]{:S(2)}) collective-permute-start(bf16[4,4,8,1024]{3,2,1,0:T(8,128)(2,1)S(1)} %collective-permute-done.16), channel_id=1, source_target_pairs={{0,224},{1,225},{64,0},{65,1},{128,64},{129,65},{192,128},{193,129... | collective-permute-start | bytes 786440 | tf_op jit(solution)/shard_map/ppermute | solution.py:132
  76.9 0.3 pad_maximum_fusion.first
  77.1 6.3 %collective-permute-done.17 = bf16[4,4,8,1024]{3,2,1,0:T(8,128)(2,1)S(1)} collective-permute-done((bf16[4,4,8,1024]{3,2,1,0:T(8,128)(2,1)S(1)}, bf16[4,4,8,1024]{3,2,1,0:T(8,128)(2,1)S(1)}, u32[]{:S(2)}, u32[]{:S(2)}) %collective-permute-start.17) | collective-permute-done | bytes 262176 | tf_op jit(solution)/shard_map/ppermute | solution.py:132
  83.4 0.0 collective-permute-start.19
  83.5 9.1 %collective-permute-done.19 = bf16[4,4,8,1024]{3,2,1,0:T(8,128)(2,1)S(1)} collective-permute-done((bf16[4,4,8,1024]{3,2,1,0:T(8,128)(2,1)S(1)}, bf16[4,4,8,1024]{3,2,1,0:T(8,128)(2,1)S(1)}, u32[]{:S(2)}, u32[]{:S(2)}) %collective-permute-start.19) | collective-permute-done | bytes 262176 | tf_op jit(solution)/shard_map/ppermute | solution.py:132
  92.6 33.6 %shard_map.109 = bf16[16,2,4,8,4000]{4,3,2,1,0:T(8,128)(2,1)} custom-call(s32[17]{0:T(128)S(1)} %pad_add_fusion.place, bf16[4,8,4,8,1024]{4,3,2,1,0:T(8,128)(2,1)S(1)} %pad_maximum_fusion.first, bf16[8,4,4,8,1024]{4,3,2,1,0:T(8,128)(2,1)S(1)} %bitcast_dynamic-update-slice_fusion.second, bf16[4,8,8,1024]{3,2,1,0:T(8,128)(2,1)S(1)} %pad_maximum_fusion.2.mine, ...), custom_call_target="tpu_custom_call" | custom-call | flops 8388608000 | bytes 25165824 | tf_op jit(solution)/shard_map/pallas_call | solution.py:247
  (52 shorter events, 0.4 us)
Async XLA Ops:
  0.0 1.9 %copy-start.1 = (bf16[8,8,12000]{2,1,0:T(8,128)(2,1)S(1)}, bf16[8,8,12000]{2,1,0:T(8,128)(2,1)}, u32[]{:S(2)}) copy-start(bf16[8,8,12000]{2,1,0:T(8,128)(2,1)} %param.11) | copy-start | bytes 4608004
  1.9 1.4 %copy-start.9 = (bf16[3000,256]{1,0:T(8,128)(2,1)S(1)}, bf16[3000,256]{1,0:T(8,128)(2,1)}, u32[]{:S(2)}) copy-start(bf16[3000,256]{1,0:T(8,128)(2,1)} %constant.145.clone) | copy-start | bytes 4608004
  1.9 2.3 %copy-start.8 = (bf16[3000,256]{1,0:T(8,128)(2,1)S(1)}, bf16[3000,256]{1,0:T(8,128)(2,1)}, u32[]{:S(2)}) copy-start(bf16[3000,256]{1,0:T(8,128)(2,1)} %constant.144.clone) | copy-start | bytes 4608004
  3.4 2.0 %copy-start.3 = (bf16[3000,512]{1,0:T(8,128)(2,1)S(1)}, bf16[3000,512]{1,0:T(8,128)(2,1)}, u32[]{:S(2)}) copy-start(bf16[3000,512]{1,0:T(8,128)(2,1)} %constant.154) | copy-start | bytes 9216004
  5.3 1.9 %copy-start.2 = (bf16[3000,512]{1,0:T(8,128)(2,1)S(1)}, bf16[3000,512]{1,0:T(8,128)(2,1)}, u32[]{:S(2)}) copy-start(bf16[3000,512]{1,0:T(8,128)(2,1)} %constant.155) | copy-start | bytes 9216004
  7.2 1.2 copy-start.4
  7.2 1.2 copy-start.6
  7.8 1.4 %copy-start.5 = (f32[8]{0:T(128)S(1)}, f32[8]{0:T(128)}, u32[]{:S(2)}) copy-start(f32[8]{0:T(128)} %param.12) | copy-start | bytes 100
  7.8 9.0 %copy-start.7 = (s32[4]{0:T(128)S(1)}, s32[4]{0:T(128)}, u32[]{:S(2)}) copy-start(s32[4]{0:T(128)} %constant.150.clone) | copy-start | bytes 52
  7.8 9.0 %copy-start = (s32[8]{0:T(128)S(1)}, s32[8]{0:T(128)}, u32[]{:S(2)}) copy-start(s32[8]{0:T(128)} %constant.149.clone) | copy-start | bytes 100
  9.3 24.2 %collective-permute-start.22 = (bf16[8,8,1024]{2,1,0:T(8,128)(2,1)S(1)}, bf16[8,8,1024]{2,1,0:T(8,128)(2,1)S(1)}, u32[]{:S(2)}, u32[]{:S(2)}) collective-permute-start(bf16[8,8,1024]{2,1,0:T(8,128)(2,1)S(1)} %fusion.10), channel_id=1, source_target_pairs={{0,6},{1,7},{64,70},{65,71},{128,134},{129,135},{192,198},{193,199... | collective-permute-start | bytes 393224 | tf_op jit(solution)/shard_map/ppermute | solution.py:132
  12.4 21.2 %collective-permute-start.21 = (bf16[8,8,1024]{2,1,0:T(8,128)(2,1)S(1)}, bf16[8,8,1024]{2,1,0:T(8,128)(2,1)S(1)}, u32[]{:S(2)}, u32[]{:S(2)}) collective-permute-start(bf16[8,8,1024]{2,1,0:T(8,128)(2,1)S(1)} %fusion.10), channel_id=1, source_target_pairs={{0,4},{1,5},{64,68},{65,69},{128,132},{129,133},{192,196},{193,197... | collective-permute-start | bytes 393224 | tf_op jit(solution)/shard_map/ppermute | solution.py:132
  13.1 5.6 %collective-permute-start.11 = (bf16[4,8,1024]{2,1,0:T(8,128)(2,1)S(1)}, bf16[4,8,1024]{2,1,0:T(8,128)(2,1)S(1)}, u32[]{:S(2)}, u32[]{:S(2)}) collective-permute-start(bf16[4,8,1024]{2,1,0:T(8,128)(2,1)S(1)} %get-tuple-element.10), channel_id=1, source_target_pairs={{0,24},{1,25},{64,88},{65,89},{128,152},{129,153},{192,216},{193,2... | collective-permute-start | bytes 196616 | tf_op jit(solution)/shard_map/ppermute | solution.py:132
  14.0 5.6 %collective-permute-start.10 = (bf16[4,8,1024]{2,1,0:T(8,128)(2,1)S(1)}, bf16[4,8,1024]{2,1,0:T(8,128)(2,1)S(1)}, u32[]{:S(2)}, u32[]{:S(2)}) collective-permute-start(bf16[4,8,1024]{2,1,0:T(8,128)(2,1)S(1)} %get-tuple-element.10), channel_id=1, source_target_pairs={{0,8},{1,9},{64,72},{65,73},{128,136},{129,137},{192,200},{193,201... | collective-permute-start | bytes 196616 | tf_op jit(solution)/shard_map/ppermute | solution.py:132
  16.4 5.8 %collective-permute-start.12 = (bf16[4,8,1024]{2,1,0:T(8,128)(2,1)S(1)}, bf16[4,8,1024]{2,1,0:T(8,128)(2,1)S(1)}, u32[]{:S(2)}, u32[]{:S(2)}) collective-permute-start(bf16[4,8,1024]{2,1,0:T(8,128)(2,1)S(1)} %get-tuple-element.10), channel_id=1, source_target_pairs={{0,16},{1,17},{64,80},{65,81},{128,144},{129,145},{192,208},{193,2... | collective-permute-start | bytes 196616 | tf_op jit(solution)/shard_map/ppermute | solution.py:132
  18.7 18.2 %collective-permute-start.20 = (bf16[8,8,1024]{2,1,0:T(8,128)(2,1)S(1)}, bf16[8,8,1024]{2,1,0:T(8,128)(2,1)S(1)}, u32[]{:S(2)}, u32[]{:S(2)}) collective-permute-start(bf16[8,8,1024]{2,1,0:T(8,128)(2,1)S(1)} %fusion.10), channel_id=1, source_target_pairs={{0,2},{1,3},{64,66},{65,67},{128,130},{129,131},{192,194},{193,195... | collective-permute-start | bytes 393224 | tf_op jit(solution)/shard_map/ppermute | solution.py:132
  19.6 8.5 %collective-permute-start = (bf16[4,8,1024]{2,1,0:T(8,128)(2,1)S(1)}, bf16[4,8,1024]{2,1,0:T(8,128)(2,1)S(1)}, u32[]{:S(2)}, u32[]{:S(2)}) collective-permute-start(bf16[4,8,1024]{2,1,0:T(8,128)(2,1)S(1)} %get-tuple-element.11), channel_id=1, source_target_pairs={{0,64},{1,65},{64,128},{65,129},{128,192},{129,193},{192,32},{193,... | collective-permute-start | bytes 196616 | tf_op jit(solution)/shard_map/ppermute | solution.py:132
  22.2 7.8 %collective-permute-start.1 = (bf16[4,8,1024]{2,1,0:T(8,128)(2,1)S(1)}, bf16[4,8,1024]{2,1,0:T(8,128)(2,1)S(1)}, u32[]{:S(2)}, u32[]{:S(2)}) collective-permute-start(bf16[4,8,1024]{2,1,0:T(8,128)(2,1)S(1)} %get-tuple-element.11), channel_id=1, source_target_pairs={{0,224},{1,225},{64,0},{65,1},{128,64},{129,65},{192,128},{193,129... | collective-permute-start | bytes 196616 | tf_op jit(solution)/shard_map/ppermute | solution.py:132
  28.1 37.6 %collective-permute-start.13 = (bf16[4,4,8,1024]{3,2,1,0:T(8,128)(2,1)S(1)}, bf16[4,4,8,1024]{3,2,1,0:T(8,128)(2,1)S(1)}, u32[]{:S(2)}, u32[]{:S(2)}) collective-permute-start(bf16[4,4,8,1024]{3,2,1,0:T(8,128)(2,1)S(1)} %pad_maximum_fusion.4), channel_id=1, source_target_pairs={{0,64},{1,65},{64,128},{65,129},{128,192},{129,193},{192,32},{193,... | collective-permute-start | bytes 786440 | tf_op jit(solution)/shard_map/ppermute | solution.py:132
  29.9 35.9 %collective-permute-start.14 = (bf16[4,4,8,1024]{3,2,1,0:T(8,128)(2,1)S(1)}, bf16[4,4,8,1024]{3,2,1,0:T(8,128)(2,1)S(1)}, u32[]{:S(2)}, u32[]{:S(2)}) collective-permute-start(bf16[4,4,8,1024]{3,2,1,0:T(8,128)(2,1)S(1)} %pad_maximum_fusion.4), channel_id=1, source_target_pairs={{0,224},{1,225},{64,0},{65,1},{128,64},{129,65},{192,128},{193,129... | collective-permute-start | bytes 786440 | tf_op jit(solution)/shard_map/ppermute | solution.py:132
  33.6 5.6 %collective-permute-start.2 = (bf16[4,8,1024]{2,1,0:T(8,128)(2,1)S(1)}, bf16[4,8,1024]{2,1,0:T(8,128)(2,1)S(1)}, u32[]{:S(2)}, u32[]{:S(2)}) collective-permute-start(bf16[4,8,1024]{2,1,0:T(8,128)(2,1)S(1)} %collective-permute-done), channel_id=1, source_target_pairs={{0,64},{1,65},{64,128},{65,129},{128,192},{129,193},{192,32},{193,... | collective-permute-start | bytes 196616 | tf_op jit(solution)/shard_map/ppermute | solution.py:132
  33.7 5.5 %collective-permute-start.3 = (bf16[4,8,1024]{2,1,0:T(8,128)(2,1)S(1)}, bf16[4,8,1024]{2,1,0:T(8,128)(2,1)S(1)}, u32[]{:S(2)}, u32[]{:S(2)}) collective-permute-start(bf16[4,8,1024]{2,1,0:T(8,128)(2,1)S(1)} %collective-permute-done.1), channel_id=1, source_target_pairs={{0,224},{1,225},{64,0},{65,1},{128,64},{129,65},{192,128},{193,129... | collective-permute-start | bytes 196616 | tf_op jit(solution)/shard_map/ppermute | solution.py:132
  37.0 17.5 %collective-permute-start.25 = (bf16[8,8,1024]{2,1,0:T(8,128)(2,1)S(1)}, bf16[8,8,1024]{2,1,0:T(8,128)(2,1)S(1)}, u32[]{:S(2)}, u32[]{:S(2)}) collective-permute-start(bf16[8,8,1024]{2,1,0:T(8,128)(2,1)S(1)} %get-tuple-element.6), channel_id=1, source_target_pairs={{0,192},{64,0},{128,64},{192,128},{1,193},{65,1},{129,65},{193,129... | collective-permute-start | bytes 393224 | tf_op jit(solution)/shard_map/ppermute | solution.py:166
  39.1 17.1 %collective-permute-start.24 = (bf16[8,8,1024]{2,1,0:T(8,128)(2,1)S(1)}, bf16[8,8,1024]{2,1,0:T(8,128)(2,1)S(1)}, u32[]{:S(2)}, u32[]{:S(2)}) collective-permute-start(bf16[8,8,1024]{2,1,0:T(8,128)(2,1)S(1)} %get-tuple-element.7), channel_id=1, source_target_pairs={{0,128},{64,192},{128,0},{192,64},{1,129},{65,193},{129,1},{193,65... | collective-permute-start | bytes 393224 | tf_op jit(solution)/shard_map/ppermute | solution.py:166
  39.1 5.6 %collective-permute-start.4 = (bf16[4,8,1024]{2,1,0:T(8,128)(2,1)S(1)}, bf16[4,8,1024]{2,1,0:T(8,128)(2,1)S(1)}, u32[]{:S(2)}, u32[]{:S(2)}) collective-permute-start(bf16[4,8,1024]{2,1,0:T(8,128)(2,1)S(1)} %collective-permute-done.2), channel_id=1, source_target_pairs={{0,64},{1,65},{64,128},{65,129},{128,192},{129,193},{192,32},{193,... | collective-permute-start | bytes 196616 | tf_op jit(solution)/shard_map/ppermute | solution.py:132
  44.7 4.3 %collective-permute-start.5 = (bf16[4,8,1024]{2,1,0:T(8,128)(2,1)S(1)}, bf16[4,8,1024]{2,1,0:T(8,128)(2,1)S(1)}, u32[]{:S(2)}, u32[]{:S(2)}) collective-permute-start(bf16[4,8,1024]{2,1,0:T(8,128)(2,1)S(1)} %collective-permute-done.3), channel_id=1, source_target_pairs={{0,224},{1,225},{64,0},{65,1},{128,64},{129,65},{192,128},{193,129... | collective-permute-start | bytes 196616 | tf_op jit(solution)/shard_map/ppermute | solution.py:132
  49.0 5.5 %collective-permute-start.6 = (bf16[4,8,1024]{2,1,0:T(8,128)(2,1)S(1)}, bf16[4,8,1024]{2,1,0:T(8,128)(2,1)S(1)}, u32[]{:S(2)}, u32[]{:S(2)}) collective-permute-start(bf16[4,8,1024]{2,1,0:T(8,128)(2,1)S(1)} %collective-permute-done.4), channel_id=1, source_target_pairs={{0,64},{1,65},{64,128},{65,129},{128,192},{129,193},{192,32},{193,... | collective-permute-start | bytes 196616 | tf_op jit(solution)/shard_map/ppermute | solution.py:132
  54.5 6.9 %collective-permute-start.23 = (bf16[8,8,1024]{2,1,0:T(8,128)(2,1)S(1)}, bf16[8,8,1024]{2,1,0:T(8,128)(2,1)S(1)}, u32[]{:S(2)}, u32[]{:S(2)}) collective-permute-start(bf16[8,8,1024]{2,1,0:T(8,128)(2,1)S(1)} %get-tuple-element.8), channel_id=1, source_target_pairs={{0,64},{64,128},{128,192},{192,0},{1,65},{65,129},{129,193},{193,1... | collective-permute-start | bytes 393224 | tf_op jit(solution)/shard_map/ppermute | solution.py:166
  54.5 19.0 %collective-permute-start.9 = (bf16[8,4,8,1024]{3,2,1,0:T(8,128)(2,1)S(1)}, bf16[8,4,8,1024]{3,2,1,0:T(8,128)(2,1)S(1)}, u32[]{:S(2)}, u32[]{:S(2)}) collective-permute-start(bf16[8,4,8,1024]{3,2,1,0:T(8,128)(2,1)S(1)} %bitcast_dynamic-update-slice_fusion.8), channel_id=1, source_target_pairs={{0,16},{1,17},{64,80},{65,81},{128,144},{129,145},{192,208},{193,2... | collective-permute-start | bytes 1572872 | tf_op jit(solution)/shard_map/ppermute | solution.py:132
  56.2 20.7 %collective-permute-start.8 = (bf16[8,4,8,1024]{3,2,1,0:T(8,128)(2,1)S(1)}, bf16[8,4,8,1024]{3,2,1,0:T(8,128)(2,1)S(1)}, u32[]{:S(2)}, u32[]{:S(2)}) collective-permute-start(bf16[8,4,8,1024]{3,2,1,0:T(8,128)(2,1)S(1)} %bitcast_dynamic-update-slice_fusion.8), channel_id=1, source_target_pairs={{0,24},{1,25},{64,88},{65,89},{128,152},{129,153},{192,216},{193,2... | collective-permute-start | bytes 1572872 | tf_op jit(solution)/shard_map/ppermute | solution.py:132
  61.4 15.4 %collective-permute-start.7 = (bf16[8,4,8,1024]{3,2,1,0:T(8,128)(2,1)S(1)}, bf16[8,4,8,1024]{3,2,1,0:T(8,128)(2,1)S(1)}, u32[]{:S(2)}, u32[]{:S(2)}) collective-permute-start(bf16[8,4,8,1024]{3,2,1,0:T(8,128)(2,1)S(1)} %bitcast_dynamic-update-slice_fusion.8), channel_id=1, source_target_pairs={{0,8},{1,9},{64,72},{65,73},{128,136},{129,137},{192,200},{193,201... | collective-permute-start | bytes 1572872 | tf_op jit(solution)/shard_map/ppermute | solution.py:132
  65.7 7.7 %collective-permute-start.15 = (bf16[4,4,8,1024]{3,2,1,0:T(8,128)(2,1)S(1)}, bf16[4,4,8,1024]{3,2,1,0:T(8,128)(2,1)S(1)}, u32[]{:S(2)}, u32[]{:S(2)}) collective-permute-start(bf16[4,4,8,1024]{3,2,1,0:T(8,128)(2,1)S(1)} %collective-permute-done.13), channel_id=1, source_target_pairs={{0,64},{1,65},{64,128},{65,129},{128,192},{129,193},{192,32},{193,... | collective-permute-start | bytes 786440 | tf_op jit(solution)/shard_map/ppermute | solution.py:132
  65.8 7.6 %collective-permute-start.16 = (bf16[4,4,8,1024]{3,2,1,0:T(8,128)(2,1)S(1)}, bf16[4,4,8,1024]{3,2,1,0:T(8,128)(2,1)S(1)}, u32[]{:S(2)}, u32[]{:S(2)}) collective-permute-start(bf16[4,4,8,1024]{3,2,1,0:T(8,128)(2,1)S(1)} %collective-permute-done.14), channel_id=1, source_target_pairs={{0,224},{1,225},{64,0},{65,1},{128,64},{129,65},{192,128},{193,129... | collective-permute-start | bytes 786440 | tf_op jit(solution)/shard_map/ppermute | solution.py:132
  73.4 19.2 %collective-permute-start.26 = (bf16[4,8,8,1024]{3,2,1,0:T(8,128)(2,1)S(1)}, bf16[4,8,8,1024]{3,2,1,0:T(8,128)(2,1)S(1)}, u32[]{:S(2)}, u32[]{:S(2)}) collective-permute-start(bf16[4,8,8,1024]{3,2,1,0:T(8,128)(2,1)S(1)} %pad_maximum_fusion.2.mine), channel_id=1, source_target_pairs={{0,1},{1,0},{64,65},{65,64},{128,129},{129,128},{192,193},{193,192... | collective-permute-start | bytes 1572872 | tf_op jit(solution)/shard_map/ppermute | solution.py:132
  73.4 10.0 %collective-permute-start.17 = (bf16[4,4,8,1024]{3,2,1,0:T(8,128)(2,1)S(1)}, bf16[4,4,8,1024]{3,2,1,0:T(8,128)(2,1)S(1)}, u32[]{:S(2)}, u32[]{:S(2)}) collective-permute-start(bf16[4,4,8,1024]{3,2,1,0:T(8,128)(2,1)S(1)} %collective-permute-done.15), channel_id=1, source_target_pairs={{0,64},{1,65},{64,128},{65,129},{128,192},{129,193},{192,32},{193,... | collective-permute-start | bytes 786440 | tf_op jit(solution)/shard_map/ppermute | solution.py:132
  73.6 9.9 %collective-permute-start.18 = (bf16[4,4,8,1024]{3,2,1,0:T(8,128)(2,1)S(1)}, bf16[4,4,8,1024]{3,2,1,0:T(8,128)(2,1)S(1)}, u32[]{:S(2)}, u32[]{:S(2)}) collective-permute-start(bf16[4,4,8,1024]{3,2,1,0:T(8,128)(2,1)S(1)} %collective-permute-done.16), channel_id=1, source_target_pairs={{0,224},{1,225},{64,0},{65,1},{128,64},{129,65},{192,128},{193,129... | collective-permute-start | bytes 786440 | tf_op jit(solution)/shard_map/ppermute | solution.py:132
  83.4 9.1 %collective-permute-start.19 = (bf16[4,4,8,1024]{3,2,1,0:T(8,128)(2,1)S(1)}, bf16[4,4,8,1024]{3,2,1,0:T(8,128)(2,1)S(1)}, u32[]{:S(2)}, u32[]{:S(2)}) collective-permute-start(bf16[4,4,8,1024]{3,2,1,0:T(8,128)(2,1)S(1)} %collective-permute-done.17), channel_id=1, source_target_pairs={{0,64},{1,65},{64,128},{65,129},{128,192},{129,193},{192,32},{193,... | collective-permute-start | bytes 786440 | tf_op jit(solution)/shard_map/ppermute | solution.py:132

commit v2 on v1

v2 whole, which is shorter than its diff:
```python
import math

import jax
import jax.numpy as jnp
import ml_dtypes
import numpy as np
from jax import lax
from jax.experimental import pallas as pl
from jax.experimental.pallas import tpu as pltpu
from jax.sharding import PartitionSpec as P

SAMPLES = 12000
QUARTER = 3000
BINS = 512
LAGS = 4000
LAGS_PAD = 4096
FIRST_BIN = 60
SMOOTH = 64
AXES = ("win", "row", "col")
BINS_AT = np.concatenate([np.arange(0, 512, 4), np.arange(2, 512, 4), np.arange(1, 512, 2)])
PHASE = 2.0 * np.pi / SAMPLES


def bf16(values):
    return values.astype(np.float32).astype(ml_dtypes.bfloat16)


def time_taper():
    index = np.arange(SAMPLES)
    edge = np.minimum(index, SAMPLES - 1 - index).astype(np.float64)
    ramp = max(SAMPLES // 20, 1)
    return np.where(edge < ramp, 0.5 - 0.5 * np.cos(np.pi * (edge + 0.5) / ramp), 1.0).astype(
        np.float32
    )


def band_taper():
    index = np.arange(BINS)
    edge = np.minimum(index, BINS - 1 - index).astype(np.float64)
    ramp = max(BINS // 16, 1)
    return np.where(edge < ramp, 0.5 - 0.5 * np.cos(np.pi * (edge + 1.0) / (ramp + 1.0)), 1.0).astype(
        np.float32
    )


def waves(bins):
    angle = PHASE * np.mod(np.arange(QUARTER)[:, None] * (bins + FIRST_BIN)[None, :], SAMPLES)
    return np.cos(angle), np.sin(angle)


def even_table(bins):
    cos, sin = waves(bins)
    return bf16(np.concatenate([cos, -sin], axis=1))


def odd_table(bins):
    cos, sin = waves(bins)
    turn = np.where((bins + FIRST_BIN) % 4 == 1, 1.0, -1.0)[None, :]
    first = np.concatenate([cos, -sin], axis=1)
    second = np.concatenate([-turn * sin, -turn * cos], axis=1)
    return bf16(np.concatenate([first, second], axis=0))


def lag_table():
    shifts = np.arange(LAGS) - LAGS // 2
    angle = PHASE * np.mod((BINS_AT + FIRST_BIN)[:, None] * shifts[None, :], SAMPLES)
    table = np.zeros((2 * BINS, LAGS_PAD))
    table[:BINS, :LAGS] = np.cos(angle)
    table[BINS:, :LAGS] = -np.sin(angle)
    return bf16(table / 128.0)


def smoother():
    index = np.arange(BINS)
    inside = (np.abs(index[:, None] - index[None, :]) <= SMOOTH).astype(np.float32)
    mean = inside / np.sum(inside, axis=0, keepdims=True, dtype=np.float32)
    return mean[BINS_AT][:, BINS_AT]


def whiten(record, weights):
    windows, channels, length = record.shape
    values = record.reshape(windows * channels, length).astype(jnp.float32)
    centered = (values - jnp.mean(values, axis=1, keepdims=True)) * time_taper()[None, :]
    centered = centered.astype(jnp.bfloat16).astype(jnp.float32)
    part = [centered[:, QUARTER * q : QUARTER * (q + 1)] for q in range(4)]
    sum02, dif02 = part[0] + part[2], part[0] - part[2]
    sum13, dif13 = part[1] + part[3], part[1] - part[3]
    even0 = (sum02 + sum13).astype(jnp.bfloat16)
    even2 = (sum02 - sum13).astype(jnp.bfloat16)
    odd = jnp.concatenate([dif02, dif13], axis=1).astype(jnp.bfloat16)

    def product(left, table):
        return jnp.dot(left, table, preferred_element_type=jnp.float32)

    spec0 = product(even0, even_table(BINS_AT[:128]))
    spec2 = product(even2, even_table(BINS_AT[128:256]))
    spec1 = product(odd, odd_table(BINS_AT[256:]))
    scale = 1.0 / math.sqrt(length)
    real_part = jnp.concatenate([spec0[:, :128], spec2[:, :128], spec1[:, :256]], axis=1) * scale
    imag_part = jnp.concatenate([spec0[:, 128:], spec2[:, 128:], spec1[:, 256:]], axis=1) * scale
    power = real_part * real_part + imag_part * imag_part
    smoothed = jnp.dot(
        power,
        smoother(),
        precision=lax.Precision.HIGHEST,
        preferred_element_type=jnp.float32,
    )
    gain = band_taper()[BINS_AT][None, :] / jnp.sqrt(smoothed + 1e-05)
    whitened = jnp.concatenate([real_part * gain, imag_part * gain], axis=1)
    whitened = whitened.reshape(windows, channels, 2 * BINS)
    plain = whitened.astype(jnp.bfloat16)
    weighted = (whitened * weights[:, None, None]).astype(jnp.bfloat16)
    return plain, weighted


def device_at(x, y, z, core):
    return ((z % 4) * 8 + (z // 4) * 4 + x) * 8 + y * 2 + core


def shift(value, dx=0, dy=0, dz=0, dcore=0):
    pairs = [
        (
            device_at(x, y, z, core),
            device_at((x + dx) % 4, (y + dy) % 4, (z + dz) % 8, (core + dcore) % 2),
        )
        for x in range(4)
        for y in range(4)
        for z in range(8)
        for core in range(2)
    ]
    return lax.ppermute(value, AXES, pairs)


def own_only(value, k):
    return lax.ppermute(value, "win", [(i, (i + k) % 4) for i in range(4)])


def together(*values):
    return lax.optimization_barrier(values)


def first_step(plain, weighted):
    return together(
        shift(plain, dz=4),
        shift(plain, dx=2),
        shift(plain, dz=1),
        shift(plain, dz=-1),
        shift(weighted, dy=1),
        shift(weighted, dy=2),
        shift(weighted, dy=3),
    )


def second_step(plain, weighted, arrived, y, z_low):
    opposite, across, below, above, *sides = arrived
    near = jnp.stack([plain, below, above, opposite])
    held = jnp.stack([weighted, *sides])

    def for_offset(k):
        return lax.dynamic_index_in_dim(held, (y - z_low - k) % 4, 0, keepdims=False)

    sent = together(
        shift(near, dx=1),
        shift(near, dx=-1),
        shift(jnp.stack([below, opposite, across]), dz=1),
        shift(jnp.stack([above, opposite, across]), dz=-1),
        shift(opposite, dx=2),
        own_only(for_offset(1), 1),
        own_only(for_offset(2), 2),
        own_only(for_offset(3), 3),
    )
    left, right, up, down, across_opposite, *rows = sent
    far = jnp.concatenate([up[:2], down[:2]])
    across_near = jnp.stack([across, up[2], down[2], across_opposite])
    mine = jnp.stack([for_offset(0), *rows])
    return near, far, left, right, across_near, mine


def third_step(far, across_near):
    left, right, up, down = together(
        shift(far, dx=1),
        shift(far, dx=-1),
        shift(across_near[1::2], dz=1),
        shift(across_near[2:], dz=-1),
    )
    return jnp.stack([left, right, jnp.concatenate([up, down])])


NEAR = (0, -1, 1, 4)
FAR = (-2, 3, 2, -3)
XS, HIGH_NEAR, GROUP_NEAR, HIGH_FAR, GROUP_FAR, ROWS, CORE = 0, 4, 8, 12, 16, 20, 24


def load_rows(place, mine, other, z_re, z_im, z_sum):
    core = place[CORE]
    for k in range(4):
        group = place[ROWS + k]
        for ref, at in ((mine, core), (other, 1 - core)):
            for w in range(8):
                value = ref[k, w].astype(jnp.float32)
                re, im = value[:, :BINS], value[:, BINS:]
                for tile in range(4):
                    lanes = slice(tile * 128, tile * 128 + 128)
                    z_re[group * 8 + w, at, tile] = re[:, lanes]
                    z_im[group * 8 + w, at, tile] = im[:, lanes]
                    z_sum[group * 8 + w, at, tile] = re[:, lanes] + im[:, lanes]


def add_cross(turn, block, high_at, group_at, place, z_re, z_im, z_sum, total):
    tile, n = turn // 4, turn % 4
    lane = pl.ds(pl.multiple_of(tile * 128, 128), 128)
    lane_im = pl.ds(pl.multiple_of(tile * 128 + BINS, 128), 128)
    high, group = place[high_at + n], place[group_at + n]
    for core, base in ((0, 0), (0, 4), (1, 0), (1, 4)):
        sums = [None] * 12
        for w in range(8):
            yr = block[0, n, w, :, lane].astype(jnp.float32)
            yi = block[0, n, w, :, lane_im].astype(jnp.float32)
            dif = yr - yi
            window = group * 8 + w
            for i in range(4):
                row = pl.ds(base + i, 8, stride=0)
                terms = (
                    z_re[window, core, tile, row, :] * yr,
                    z_im[window, core, tile, row, :] * yi,
                    z_sum[window, core, tile, row, :] * dif,
                )
                for m, term in enumerate(terms):
                    at = i * 3 + m
                    sums[at] = term if w == 0 else sums[at] + term
        for i in range(4):
            p, q, r = sums[i * 3 : i * 3 + 3]
            total[high, core * 8 + base + i, :, lane] += p + q
            total[high, core * 8 + base + i, :, lane_im] += r - p + q


def near_kernel(place, block, mine, other, total, z_re, z_im, z_sum):
    step = pl.program_id(0)

    @pl.when(step == 0)
    def _():
        load_rows(place, mine, other, z_re, z_im, z_sum)

    @pl.when(step != 1)
    def _():
        total[...] = jnp.zeros_like(total)

    high_at = jnp.where(step == 1, HIGH_FAR, HIGH_NEAR)
    group_at = jnp.where(step == 1, GROUP_FAR, GROUP_NEAR)

    def turn(at, carry):
        add_cross(at, block, high_at, group_at, place, z_re, z_im, z_sum, total.at[0])
        return carry

    lax.fori_loop(0, 16, turn, 0)


WHOLE = pl.BlockSpec(memory_space=pltpu.VMEM)
BLOCK = (1, 4, 8, 8, 2 * BINS)
TOTAL = (1, 2, 16, 8, 2 * BINS)
ROW_SCRATCH = [pltpu.VMEM((32, 2, 4, 8, 128), jnp.float32)] * 3


def near_totals(place, blocks, mine, other):
    return pl.pallas_call(
        near_kernel,
        out_shape=jax.ShapeDtypeStruct((4, *TOTAL[1:]), jnp.float32),
        grid_spec=pltpu.PrefetchScalarGridSpec(
            num_scalar_prefetch=1,
            grid=(5,),
            in_specs=[
                pl.BlockSpec(BLOCK, lambda j, place: (j, 0, 0, 0, 0)),
                WHOLE,
                WHOLE,
            ],
            out_specs=pl.BlockSpec(TOTAL, lambda j, place: (jnp.maximum(j - 1, 0), 0, 0, 0, 0)),
            scratch_shapes=ROW_SCRATCH,
        ),
        compiler_params=pltpu.CompilerParams(vmem_limit_bytes=32 * 1024 * 1024),
        cost_estimate=pl.CostEstimate(
            flops=12 * 10**9, bytes_accessed=8 * 2**20, transcendentals=0
        ),
    )(place, blocks, mine, other)


def far_kernel(
    place, block, before, mine, other, source, out, z_re, z_im, z_sum, total, now, later, table, ready
):
    step = pl.program_id(0)
    fetch = pltpu.make_async_copy(source, table, ready)

    def settle(source, target):
        for i in range(16):
            rows = jnp.concatenate([source[0, i], source[1, i]], axis=0)
            target[pl.ds(i * 16, 16), :] = rows.astype(jnp.bfloat16)

    @pl.when(step == 0)
    def _():
        fetch.start()
        load_rows(place, mine, other, z_re, z_im, z_sum)
        settle(before.at[0], now)

    def lag_all():
        for tile in range(8):
            start = tile * 512
            keep = min(512, LAGS - start)
            value = jnp.dot(
                now[...], table[:, start : start + 512], preferred_element_type=jnp.float32
            )
            value = value.reshape(16, 2, 1, 8, 512).astype(jnp.bfloat16)
            out[:, :, :, :, start : start + keep] = value[..., :keep]

    @pl.when(step < 3)
    def _():
        total[...] = before[step + 1]

        def turn(at, carry):
            add_cross(at, block, HIGH_FAR, GROUP_FAR, place, z_re, z_im, z_sum, total)
            return carry

        lax.fori_loop(0, 16, turn, 0)
        settle(total, later)

    @pl.when(step == 0)
    def _():
        fetch.wait()

    lag_all()

    @pl.when(step < 3)
    def _():
        now[...] = later[...]


def correlations(place, blocks, before, mine, other):
    last = lambda j: jnp.minimum(j, 2)
    return pl.pallas_call(
        far_kernel,
        out_shape=jax.ShapeDtypeStruct((16, 2, 4, 8, LAGS), jnp.bfloat16),
        grid_spec=pltpu.PrefetchScalarGridSpec(
            num_scalar_prefetch=1,
            grid=(4,),
            in_specs=[
                pl.BlockSpec(BLOCK, lambda j, place: (last(j), 0, 0, 0, 0)),
                pl.BlockSpec((4, *TOTAL[1:]), lambda j, place: (0, 0, 0, 0, 0)),
                WHOLE,
                WHOLE,
                pl.BlockSpec(memory_space=pl.ANY),
            ],
            out_specs=pl.BlockSpec((16, 2, 1, 8, LAGS), lambda j, place: (0, 0, place[j], 0, 0)),
            scratch_shapes=[
                *ROW_SCRATCH,
                pltpu.VMEM(TOTAL[1:], jnp.float32),
                pltpu.VMEM((256, 2 * BINS), jnp.bfloat16),
                pltpu.VMEM((256, 2 * BINS), jnp.bfloat16),
                pltpu.VMEM((2 * BINS, LAGS_PAD), jnp.bfloat16),
                pltpu.SemaphoreType.DMA(()),
            ],
        ),
        compiler_params=pltpu.CompilerParams(vmem_limit_bytes=48 * 1024 * 1024),
        cost_estimate=pl.CostEstimate(
            flops=2 * 1024 * 1024 * LAGS, bytes_accessed=24 * 2**20, transcendentals=0
        ),
    )(place, blocks, before, mine, other, lag_table())


def shards(record, window_weight):
    plain, weighted = whiten(record, window_weight)
    z_low = lax.axis_index("win")
    row = lax.axis_index("row")
    col = lax.axis_index("col")
    x, z = row % 4, (row // 4) * 4 + z_low
    near_z = (z + jnp.array(NEAR)) % 8
    far_z = (z + jnp.array(FAR)) % 8
    place = jnp.concatenate(
        [
            (x + jnp.array([0, -1, 1, 2])) % 4,
            near_z // 4,
            near_z % 4,
            far_z // 4,
            far_z % 4,
            (z_low - jnp.arange(4)) % 4,
            jnp.stack([col % 2]),
        ]
    ).astype(jnp.int32)
    arrived = first_step(plain, weighted)
    near, far, left, right, across, mine = second_step(plain, weighted, arrived, col // 2, z_low)
    other = shift(mine, dcore=1)
    rest = third_step(far, across)
    before = near_totals(place, jnp.stack([near, far, left, right, across]), mine, other)
    corr = correlations(place, rest, before, mine, other)
    return corr.reshape(1, 1, 16, 8, 8, LAGS)


def solution(mesh):
    placed = (P("win", ("row", "col"), None), P("win"))
    return jax.shard_map(
        shards,
        mesh=mesh,
        in_specs=placed,
        out_specs=P("row", "win", None, None, "col", None),
        check_vma=False,
    )
```

time: 127 us -> 112 us (0.88)
  the two profiles are of different devices: /device:TPU:6 before, /device:TPU:64 now
where the time goes in v2:
time: 112 us
  Pallas kernels  36.8 us (33%)
  starting transfers between devices  33.4 us (30%)
  waiting for transfers between devices  25.8 us (23%)
  other arithmetic  6.42 us (6%)
  local copies, waits for them, and re-layouts  5.54 us (5%)
  matrix products  3.72 us (3%)
    ppermute x17, starting transfers between devices, shift(): return lax.ppermute(value, AXES, pairs)  28.7 us
    pallas_call x1, Pallas kernels, correlations(): pl.pallas_call(far_kernel, out_shape=jax.ShapeDtypeStruct((16, 2, 4, 8, L...  22.5 us
    ppermute x17, waiting for transfers between devices, shift(): return lax.ppermute(value, AXES, pairs)  16.1 us
    pallas_call x1, Pallas kernels, near_totals(): pl.pallas_call(near_kernel, out_shape=jax.ShapeDtypeStruct((4, *TOTAL[1:]...  14.3 us
    ppermute x3, waiting for transfers between devices, own_only(): return lax.ppermute(value, 'win', [(i, (i + k) % 4) for i in range(4)])  9.68 us
    ppermute x3, starting transfers between devices, own_only(): return lax.ppermute(value, 'win', [(i, (i + k) % 4) for i in range(4)])  4.7 us
    unnamed x32, local copies, waits for them, and re-layouts  4.56 us
    dot_general x4, matrix products, product(): return jnp.dot(left, table, preferred_element_type=jnp.float32)  2.93 us
  transfers between devices with their start and end apart: 20, of which 10 were waited for; matrix products, arithmetic and copies ran while one was open for 3% of the time, Pallas kernels for 0%

profile of v2, /device:TPU:64, one launch (start us, length us, event | category | flops | bytes accessed | tf_op | source)
XLA Modules:
  0.0 112.2 jit_solution(1109794783779661921)
XLA Ops:
  0.0 1.7 %convert_reduce_fusion = f32[8,8]{1,0:T(8,128)S(1)} fusion(bf16[8,8,12000]{2,1,0:T(8,128)(2,1)} %param.12), kind=kLoop, calls=%fused_computation | loop fusion | flops 1535936 | bytes 1536256 | tf_op jit(solution)/shard_map/reduce_sum | solution.py:83
  1.7 0.1 div.65
  1.8 1.9 %fusion.3 = f32[64,12000]{1,0:T(8,128)S(1)} fusion(bf16[8,8,12000]{2,1,0:T(8,128)(2,1)} %param.12, f32[12000]{0:T(1024)} %constant.182, f32[64]{0:T(128)S(1)} %div.65), kind=kLoop, calls=%fused_computation.6 | loop fusion | flops 3840000 | bytes 4656256 | tf_op jit(solution)/shard_map/convert_element_type | solution.py:84
  3.8 0.0 copy-start.2
  3.8 0.9 fusion.7
  4.6 0.0 copy-done.13
  4.6 0.0 copy-start.1
  4.6 0.9 fusion.6
  5.5 0.2 copy-done.2
  5.7 0.6 fusion.8
  6.3 0.4 copy-done.1
  6.8 0.6 convolution_add_fusion.1
  7.4 0.0 copy-start.10
  7.4 0.6 copy-done.3
  8.0 0.8 fusion.13
  8.8 0.2 collective-permute-start.3
  9.0 1.9 %collective-permute-start.2 = (bf16[8,8,1024]{2,1,0:T(8,128)(2,1)S(1)}, bf16[8,8,1024]{2,1,0:T(8,128)(2,1)S(1)}, u32[]{:S(2)}, u32[]{:S(2)}) collective-permute-start(bf16[8,8,1024]{2,1,0:T(8,128)(2,1)S(1)} %get-tuple-element.54), channel_id=1, source_target_pairs={{0,64},{1,65},{64,128},{65,129},{128,192},{129,193},{192,32},{193,... | collective-permute-start | bytes 393224 | tf_op jit(solution)/shard_map/ppermute | solution.py:131
  10.9 3.0 %collective-permute-start.1 = (bf16[8,8,1024]{2,1,0:T(8,128)(2,1)S(1)}, bf16[8,8,1024]{2,1,0:T(8,128)(2,1)S(1)}, u32[]{:S(2)}, u32[]{:S(2)}) collective-permute-start(bf16[8,8,1024]{2,1,0:T(8,128)(2,1)S(1)} %get-tuple-element.54), channel_id=1, source_target_pairs={{0,16},{1,17},{64,80},{65,81},{128,144},{129,145},{192,208},{193,2... | collective-permute-start | bytes 393224 | tf_op jit(solution)/shard_map/ppermute | solution.py:131
  13.9 5.4 %collective-permute-start = (bf16[8,8,1024]{2,1,0:T(8,128)(2,1)S(1)}, bf16[8,8,1024]{2,1,0:T(8,128)(2,1)S(1)}, u32[]{:S(2)}, u32[]{:S(2)}) collective-permute-start(bf16[8,8,1024]{2,1,0:T(8,128)(2,1)S(1)} %get-tuple-element.54), channel_id=1, source_target_pairs={{0,32},{1,33},{64,96},{65,97},{128,160},{129,161},{192,224},{193,2... | collective-permute-start | bytes 393224 | tf_op jit(solution)/shard_map/ppermute | solution.py:131
  19.3 0.1 fusion.9
  19.4 0.0 copy-start.11
  19.4 3.1 %collective-permute-start.6 = (bf16[8,8,1024]{2,1,0:T(8,128)(2,1)S(1)}, bf16[8,8,1024]{2,1,0:T(8,128)(2,1)S(1)}, u32[]{:S(2)}, u32[]{:S(2)}) collective-permute-start(bf16[8,8,1024]{2,1,0:T(8,128)(2,1)S(1)} %fusion.9), channel_id=1, source_target_pairs={{0,6},{1,7},{64,70},{65,71},{128,134},{129,135},{192,198},{193,199... | collective-permute-start | bytes 393224 | tf_op jit(solution)/shard_map/ppermute | solution.py:131
  22.5 0.1 fusion.10
  22.7 0.7 collective-permute-start.5
  23.4 0.0 collective-permute-done.2
  23.4 1.0 collective-permute-start.4
  24.4 0.0 collective-permute-done.1
  24.4 0.0 collective-permute-done
  24.4 2.8 %collective-permute-done.6 = bf16[8,8,1024]{2,1,0:T(8,128)(2,1)S(1)} collective-permute-done((bf16[8,8,1024]{2,1,0:T(8,128)(2,1)S(1)}, bf16[8,8,1024]{2,1,0:T(8,128)(2,1)S(1)}, u32[]{:S(2)}, u32[]{:S(2)}) %collective-permute-start.6) | collective-permute-done | bytes 131104 | tf_op jit(solution)/shard_map/ppermute | solution.py:131
  27.2 2.4 %collective-permute-done.5 = bf16[8,8,1024]{2,1,0:T(8,128)(2,1)S(1)} collective-permute-done((bf16[8,8,1024]{2,1,0:T(8,128)(2,1)S(1)}, bf16[8,8,1024]{2,1,0:T(8,128)(2,1)S(1)}, u32[]{:S(2)}, u32[]{:S(2)}) %collective-permute-start.5) | collective-permute-done | bytes 131104 | tf_op jit(solution)/shard_map/ppermute | solution.py:131
  29.6 1.3 %collective-permute-done.4 = bf16[8,8,1024]{2,1,0:T(8,128)(2,1)S(1)} collective-permute-done((bf16[8,8,1024]{2,1,0:T(8,128)(2,1)S(1)}, bf16[8,8,1024]{2,1,0:T(8,128)(2,1)S(1)}, u32[]{:S(2)}, u32[]{:S(2)}) %collective-permute-start.4) | collective-permute-done | bytes 131104 | tf_op jit(solution)/shard_map/ppermute | solution.py:131
  30.9 0.5 collective-permute-start.11
  31.4 0.1 pad_maximum_fusion.1
  31.5 2.8 %collective-permute-start.8 = (bf16[4,8,8,1024]{3,2,1,0:T(8,128)(2,1)S(1)}, bf16[4,8,8,1024]{3,2,1,0:T(8,128)(2,1)S(1)}, u32[]{:S(2)}, u32[]{:S(2)}) collective-permute-start(bf16[4,8,8,1024]{3,2,1,0:T(8,128)(2,1)S(1)} %pad_maximum_fusion.1), channel_id=1, source_target_pairs={{0,24},{1,25},{64,88},{65,89},{128,152},{129,153},{192,216},{193,2... | collective-permute-start | bytes 1572872 | tf_op jit(solution)/shard_map/ppermute | solution.py:131
  34.4 0.0 collective-permute-start.7
  34.4 0.1 pad_maximum_fusion.2
  34.4 0.7 constant_dynamic-slice_fusion
  35.1 1.0 collective-permute-start.14
  36.2 3.6 %collective-permute-start.13 = (bf16[8,8,1024]{2,1,0:T(8,128)(2,1)S(1)}, bf16[8,8,1024]{2,1,0:T(8,128)(2,1)}, u32[]{:S(2)}, u32[]{:S(2)}) collective-permute-start(bf16[8,8,1024]{2,1,0:T(8,128)(2,1)S(1)} %get-tuple-element.49), channel_id=1, source_target_pairs={{0,128},{64,192},{128,0},{192,64},{1,129},{65,193},{129,1},{193,65... | collective-permute-start | bytes 393224 | tf_op jit(solution)/shard_map/ppermute | solution.py:135
  39.7 0.9 pad_maximum_fusion.6
  40.7 0.1 collective-permute-done.14
  40.7 0.7 copy-done.4
  41.4 4.7 %collective-permute-start.9 = (bf16[3,8,8,1024]{3,2,1,0:T(8,128)(2,1)}, bf16[3,8,8,1024]{3,2,1,0:T(8,128)(2,1)S(1)}, u32[]{:S(2)}, u32[]{:S(2)}) collective-permute-start(bf16[3,8,8,1024]{3,2,1,0:T(8,128)(2,1)} %get-tuple-element.52), channel_id=1, source_target_pairs={{0,64},{1,65},{64,128},{65,129},{128,192},{129,193},{192,32},{193,... | collective-permute-start | bytes 1179656 | tf_op jit(solution)/shard_map/ppermute | solution.py:131
  46.1 0.8 collective-permute-done.13
  46.9 0.1 collective-permute-start.12
  47.0 0.1 concatenate.23.place
  47.2 8.9 %collective-permute-done.12 = bf16[8,8,1024]{2,1,0:T(8,128)(2,1)S(1)} collective-permute-done((bf16[8,8,1024]{2,1,0:T(8,128)(2,1)}, bf16[8,8,1024]{2,1,0:T(8,128)(2,1)S(1)}, u32[]{:S(2)}, u32[]{:S(2)}) %collective-permute-start.12) | collective-permute-done | bytes 131104 | tf_op jit(solution)/shard_map/ppermute | solution.py:135
  56.0 0.0 collective-permute-done.9
  56.1 0.0 collective-permute-done.8
  56.1 0.6 copy-done.6
  56.8 3.0 %collective-permute-start.16 = (bf16[4,8,8,1024]{3,2,1,0:T(8,128)(2,1)S(1)}, bf16[4,8,8,1024]{3,2,1,0:T(8,128)(2,1)S(1)}, u32[]{:S(2)}, u32[]{:S(2)}) collective-permute-start(bf16[4,8,8,1024]{3,2,1,0:T(8,128)(2,1)S(1)} %pad_maximum_fusion.3), channel_id=1, source_target_pairs={{0,24},{1,25},{64,88},{65,89},{128,152},{129,153},{192,216},{193,2... | collective-permute-start | bytes 1572872 | tf_op jit(solution)/shard_map/ppermute | solution.py:131
  59.9 0.1 collective-permute-start.18
  60.0 0.1 pad_maximum_fusion.4
  60.1 2.1 %collective-permute-start.17 = (bf16[2,8,8,1024]{3,2,1,0:T(8,128)(2,1)S(1)}, bf16[2,8,8,1024]{3,2,1,0:T(8,128)(2,1)S(1)}, u32[]{:S(2)}, u32[]{:S(2)}) collective-permute-start(bf16[2,8,8,1024]{3,2,1,0:T(8,128)(2,1)S(1)} %slice.61), channel_id=1, source_target_pairs={{0,64},{1,65},{64,128},{65,129},{128,192},{129,193},{192,32},{193,... | collective-permute-start | bytes 786440 | tf_op jit(solution)/shard_map/ppermute | solution.py:131
  62.2 1.0 pad_maximum_fusion.5.mine
  63.2 0.1 collective-permute-start.19
  63.4 2.9 %collective-permute-done.18 = bf16[2,8,8,1024]{3,2,1,0:T(8,128)(2,1)S(1)} collective-permute-done((bf16[2,8,8,1024]{3,2,1,0:T(8,128)(2,1)S(1)}, bf16[2,8,8,1024]{3,2,1,0:T(8,128)(2,1)S(1)}, u32[]{:S(2)}, u32[]{:S(2)}) %collective-permute-start.18) | collective-permute-done | bytes 262176 | tf_op jit(solution)/shard_map/ppermute | solution.py:131
  66.3 0.2 collective-permute-done.17
  66.5 3.1 %collective-permute-done.16 = bf16[4,8,8,1024]{3,2,1,0:T(8,128)(2,1)S(1)} collective-permute-done((bf16[4,8,8,1024]{3,2,1,0:T(8,128)(2,1)S(1)}, bf16[4,8,8,1024]{3,2,1,0:T(8,128)(2,1)S(1)}, u32[]{:S(2)}, u32[]{:S(2)}) %collective-permute-start.16) | collective-permute-done | bytes 524320 | tf_op jit(solution)/shard_map/ppermute | solution.py:131
  69.6 3.4 %collective-permute-done.15 = bf16[4,8,8,1024]{3,2,1,0:T(8,128)(2,1)S(1)} collective-permute-done((bf16[4,8,8,1024]{3,2,1,0:T(8,128)(2,1)S(1)}, bf16[4,8,8,1024]{3,2,1,0:T(8,128)(2,1)S(1)}, u32[]{:S(2)}, u32[]{:S(2)}) %collective-permute-start.15) | collective-permute-done | bytes 524320 | tf_op jit(solution)/shard_map/ppermute | solution.py:131
  73.1 0.2 pad_maximum_fusion.block
  73.3 14.3 %shard_map.118.before = f32[4,2,16,8,1024]{4,3,2,1,0:T(8,128)S(1)} custom-call(s32[25]{0:T(128)S(1)} %concatenate.23.place, bf16[5,4,8,8,1024]{4,3,2,1,0:T(8,128)(2,1)S(1)} %bitcast_dynamic-update-slice_fusion.block, bf16[4,8,8,1024]{3,2,1,0:T(8,128)(2,1)S(1)} %pad_maximum_fusion.5.mine, bf16[4,8,8,1024]{3,2,1,0:T(8,128)(2,1)S(1)} %collective-permute-done.19.other), custom_call_target="tpu_custom_call" | custom-call | flops 12000000000 | bytes 8388608 | tf_op jit(solution)/shard_map/pallas_call | solution.py:265
  87.6 2.0 %copy-done = f32[4,2,16,8,1024]{4,3,2,1,0:T(8,128)} copy-done((f32[4,2,16,8,1024]{4,3,2,1,0:T(8,128)}, f32[4,2,16,8,1024]{4,3,2,1,0:T(8,128)S(1)}, u32[]{:S(2)}) %copy-start) | copy-done | bytes 4194328
  89.6 22.5 %shard_map.119 = bf16[16,2,4,8,4000]{4,3,2,1,0:T(8,128)(2,1)} custom-call(s32[25]{0:T(128)S(1)} %concatenate.23.place, bf16[3,4,8,8,1024]{4,3,2,1,0:T(8,128)(2,1)S(1)} %pad_maximum_fusion.block, f32[4,2,16,8,1024]{4,3,2,1,0:T(8,128)} %copy-done, bf16[4,8,8,1024]{3,2,1,0:T(8,128)(2,1)S(1)} %pad_maximum_fusion.5.mine, ...), custom_call_target="tpu_custom_call" | custom-call | flops 8388608000 | bytes 25165824 | tf_op jit(solution)/shard_map/pallas_call | solution.py:337
  (47 shorter events, 0.5 us)
Async XLA Ops:
  1.7 2.0 %copy-start.14 = (bf16[3000,256]{1,0:T(8,128)(2,1)S(1)}, bf16[3000,256]{1,0:T(8,128)(2,1)}, u32[]{:S(2)}) copy-start(bf16[3000,256]{1,0:T(8,128)(2,1)} %constant.173.clone) | copy-start | bytes 4608004
  1.8 2.8 %copy-start.13 = (bf16[3000,256]{1,0:T(8,128)(2,1)S(1)}, bf16[3000,256]{1,0:T(8,128)(2,1)}, u32[]{:S(2)}) copy-start(bf16[3000,256]{1,0:T(8,128)(2,1)} %constant.172.clone) | copy-start | bytes 4608004
  3.8 2.0 %copy-start.2 = (bf16[3000,512]{1,0:T(8,128)(2,1)S(1)}, bf16[3000,512]{1,0:T(8,128)(2,1)}, u32[]{:S(2)}) copy-start(bf16[3000,512]{1,0:T(8,128)(2,1)} %constant.183) | copy-start | bytes 9216004
  4.6 2.1 %copy-start.1 = (bf16[3000,512]{1,0:T(8,128)(2,1)S(1)}, bf16[3000,512]{1,0:T(8,128)(2,1)}, u32[]{:S(2)}) copy-start(bf16[3000,512]{1,0:T(8,128)(2,1)} %constant.184) | copy-start | bytes 9216004
  6.8 1.2 %copy-start.3 = (f32[512,512]{1,0:T(8,128)S(1)}, f32[512,512]{1,0:T(8,128)}, u32[]{:S(2)}) copy-start(f32[512,512]{1,0:T(8,128)} %constant.175.clone) | copy-start | bytes 3145732
  6.8 1.2 %copy-start.9 = (f32[512]{0:T(512)S(1)}, f32[512]{0:T(512)}, u32[]{:S(2)}) copy-start(f32[512]{0:T(512)} %constant.185) | copy-start | bytes 6148
  6.8 12.6 %copy-start.8 = (f32[8]{0:T(128)S(1)}, f32[8]{0:T(128)}, u32[]{:S(2)}) copy-start(f32[8]{0:T(128)} %param.13) | copy-start | bytes 100
  7.4 15.3 %copy-start.12 = (s32[4]{0:T(128)S(1)}, s32[4]{0:T(128)}, u32[]{:S(2)}) copy-start(s32[4]{0:T(128)} %constant.177.clone) | copy-start | bytes 52
  7.4 17.0 %copy-start.10 = (s32[4]{0:T(128)S(1)}, s32[4]{0:T(128)}, u32[]{:S(2)}) copy-start(s32[4]{0:T(128)} %constant.179.clone) | copy-start | bytes 52
  8.8 13.9 %collective-permute-start.3 = (bf16[8,8,1024]{2,1,0:T(8,128)(2,1)S(1)}, bf16[8,8,1024]{2,1,0:T(8,128)(2,1)S(1)}, u32[]{:S(2)}, u32[]{:S(2)}) collective-permute-start(bf16[8,8,1024]{2,1,0:T(8,128)(2,1)S(1)} %get-tuple-element.54), channel_id=1, source_target_pairs={{0,224},{1,225},{64,0},{65,1},{128,64},{129,65},{192,128},{193,129... | collective-permute-start | bytes 393224 | tf_op jit(solution)/shard_map/ppermute | solution.py:131
  9.0 14.4 %collective-permute-start.2 = (bf16[8,8,1024]{2,1,0:T(8,128)(2,1)S(1)}, bf16[8,8,1024]{2,1,0:T(8,128)(2,1)S(1)}, u32[]{:S(2)}, u32[]{:S(2)}) collective-permute-start(bf16[8,8,1024]{2,1,0:T(8,128)(2,1)S(1)} %get-tuple-element.54), channel_id=1, source_target_pairs={{0,64},{1,65},{64,128},{65,129},{128,192},{129,193},{192,32},{193,... | collective-permute-start | bytes 393224 | tf_op jit(solution)/shard_map/ppermute | solution.py:131
  10.9 13.5 %collective-permute-start.1 = (bf16[8,8,1024]{2,1,0:T(8,128)(2,1)S(1)}, bf16[8,8,1024]{2,1,0:T(8,128)(2,1)S(1)}, u32[]{:S(2)}, u32[]{:S(2)}) collective-permute-start(bf16[8,8,1024]{2,1,0:T(8,128)(2,1)S(1)} %get-tuple-element.54), channel_id=1, source_target_pairs={{0,16},{1,17},{64,80},{65,81},{128,144},{129,145},{192,208},{193,2... | collective-permute-start | bytes 393224 | tf_op jit(solution)/shard_map/ppermute | solution.py:131
  13.9 10.5 %collective-permute-start = (bf16[8,8,1024]{2,1,0:T(8,128)(2,1)S(1)}, bf16[8,8,1024]{2,1,0:T(8,128)(2,1)S(1)}, u32[]{:S(2)}, u32[]{:S(2)}) collective-permute-start(bf16[8,8,1024]{2,1,0:T(8,128)(2,1)S(1)} %get-tuple-element.54), channel_id=1, source_target_pairs={{0,32},{1,33},{64,96},{65,97},{128,160},{129,161},{192,224},{193,2... | collective-permute-start | bytes 393224 | tf_op jit(solution)/shard_map/ppermute | solution.py:131
  19.4 26.7 %copy-start.11 = (s32[4]{0:T(128)S(1)}, s32[4]{0:T(128)}, u32[]{:S(2)}) copy-start(s32[4]{0:T(128)} %constant.178.clone) | copy-start | bytes 52
  19.4 7.8 %collective-permute-start.6 = (bf16[8,8,1024]{2,1,0:T(8,128)(2,1)S(1)}, bf16[8,8,1024]{2,1,0:T(8,128)(2,1)S(1)}, u32[]{:S(2)}, u32[]{:S(2)}) collective-permute-start(bf16[8,8,1024]{2,1,0:T(8,128)(2,1)S(1)} %fusion.9), channel_id=1, source_target_pairs={{0,6},{1,7},{64,70},{65,71},{128,134},{129,135},{192,198},{193,199... | collective-permute-start | bytes 393224 | tf_op jit(solution)/shard_map/ppermute | solution.py:131
  22.7 6.9 %collective-permute-start.5 = (bf16[8,8,1024]{2,1,0:T(8,128)(2,1)S(1)}, bf16[8,8,1024]{2,1,0:T(8,128)(2,1)S(1)}, u32[]{:S(2)}, u32[]{:S(2)}) collective-permute-start(bf16[8,8,1024]{2,1,0:T(8,128)(2,1)S(1)} %fusion.9), channel_id=1, source_target_pairs={{0,4},{1,5},{64,68},{65,69},{128,132},{129,133},{192,196},{193,197... | collective-permute-start | bytes 393224 | tf_op jit(solution)/shard_map/ppermute | solution.py:131
  23.4 7.5 %collective-permute-start.4 = (bf16[8,8,1024]{2,1,0:T(8,128)(2,1)S(1)}, bf16[8,8,1024]{2,1,0:T(8,128)(2,1)S(1)}, u32[]{:S(2)}, u32[]{:S(2)}) collective-permute-start(bf16[8,8,1024]{2,1,0:T(8,128)(2,1)S(1)} %fusion.9), channel_id=1, source_target_pairs={{0,2},{1,3},{64,66},{65,67},{128,130},{129,131},{192,194},{193,195... | collective-permute-start | bytes 393224 | tf_op jit(solution)/shard_map/ppermute | solution.py:131
  30.9 9.7 %collective-permute-start.11 = (bf16[8,8,1024]{2,1,0:T(8,128)(2,1)S(1)}, bf16[8,8,1024]{2,1,0:T(8,128)(2,1)S(1)}, u32[]{:S(2)}, u32[]{:S(2)}) collective-permute-start(bf16[8,8,1024]{2,1,0:T(8,128)(2,1)S(1)} %collective-permute-done), channel_id=1, source_target_pairs={{0,16},{1,17},{64,80},{65,81},{128,144},{129,145},{192,208},{193,2... | collective-permute-start | bytes 393224 | tf_op jit(solution)/shard_map/ppermute | solution.py:131
  31.5 24.5 %collective-permute-start.8 = (bf16[4,8,8,1024]{3,2,1,0:T(8,128)(2,1)S(1)}, bf16[4,8,8,1024]{3,2,1,0:T(8,128)(2,1)S(1)}, u32[]{:S(2)}, u32[]{:S(2)}) collective-permute-start(bf16[4,8,8,1024]{3,2,1,0:T(8,128)(2,1)S(1)} %pad_maximum_fusion.1), channel_id=1, source_target_pairs={{0,24},{1,25},{64,88},{65,89},{128,152},{129,153},{192,216},{193,2... | collective-permute-start | bytes 1572872 | tf_op jit(solution)/shard_map/ppermute | solution.py:131
  34.4 21.7 %collective-permute-start.7 = (bf16[4,8,8,1024]{3,2,1,0:T(8,128)(2,1)S(1)}, bf16[4,8,8,1024]{3,2,1,0:T(8,128)(2,1)S(1)}, u32[]{:S(2)}, u32[]{:S(2)}) collective-permute-start(bf16[4,8,8,1024]{3,2,1,0:T(8,128)(2,1)S(1)} %pad_maximum_fusion.1), channel_id=1, source_target_pairs={{0,8},{1,9},{64,72},{65,73},{128,136},{129,137},{192,200},{193,201... | collective-permute-start | bytes 1572872 | tf_op jit(solution)/shard_map/ppermute | solution.py:131
  35.1 5.6 %collective-permute-start.14 = (bf16[8,8,1024]{2,1,0:T(8,128)(2,1)S(1)}, bf16[8,8,1024]{2,1,0:T(8,128)(2,1)S(1)}, u32[]{:S(2)}, u32[]{:S(2)}) collective-permute-start(bf16[8,8,1024]{2,1,0:T(8,128)(2,1)S(1)} %get-tuple-element.48), channel_id=1, source_target_pairs={{0,192},{64,0},{128,64},{192,128},{1,193},{65,1},{129,65},{193,129... | collective-permute-start | bytes 393224 | tf_op jit(solution)/shard_map/ppermute | solution.py:135
  36.2 10.8 %collective-permute-start.13 = (bf16[8,8,1024]{2,1,0:T(8,128)(2,1)S(1)}, bf16[8,8,1024]{2,1,0:T(8,128)(2,1)}, u32[]{:S(2)}, u32[]{:S(2)}) collective-permute-start(bf16[8,8,1024]{2,1,0:T(8,128)(2,1)S(1)} %get-tuple-element.49), channel_id=1, source_target_pairs={{0,128},{64,192},{128,0},{192,64},{1,129},{65,193},{129,1},{193,65... | collective-permute-start | bytes 393224 | tf_op jit(solution)/shard_map/ppermute | solution.py:135
  40.7 15.4 %collective-permute-start.10 = (bf16[3,8,8,1024]{3,2,1,0:T(8,128)(2,1)}, bf16[3,8,8,1024]{3,2,1,0:T(8,128)(2,1)S(1)}, u32[]{:S(2)}, u32[]{:S(2)}) collective-permute-start(bf16[3,8,8,1024]{3,2,1,0:T(8,128)(2,1)} %get-tuple-element.51), channel_id=1, source_target_pairs={{0,224},{1,225},{64,0},{65,1},{128,64},{129,65},{192,128},{193,129... | collective-permute-start | bytes 1179656 | tf_op jit(solution)/shard_map/ppermute | solution.py:131
  40.7 0.7 copy-start.4
  41.4 14.6 %collective-permute-start.9 = (bf16[3,8,8,1024]{3,2,1,0:T(8,128)(2,1)}, bf16[3,8,8,1024]{3,2,1,0:T(8,128)(2,1)S(1)}, u32[]{:S(2)}, u32[]{:S(2)}) collective-permute-start(bf16[3,8,8,1024]{3,2,1,0:T(8,128)(2,1)} %get-tuple-element.52), channel_id=1, source_target_pairs={{0,64},{1,65},{64,128},{65,129},{128,192},{129,193},{192,32},{193,... | collective-permute-start | bytes 1179656 | tf_op jit(solution)/shard_map/ppermute | solution.py:131
  46.9 9.1 %collective-permute-start.12 = (bf16[8,8,1024]{2,1,0:T(8,128)(2,1)}, bf16[8,8,1024]{2,1,0:T(8,128)(2,1)S(1)}, u32[]{:S(2)}, u32[]{:S(2)}) collective-permute-start(bf16[8,8,1024]{2,1,0:T(8,128)(2,1)} %get-tuple-element.50), channel_id=1, source_target_pairs={{0,64},{64,128},{128,192},{192,0},{1,65},{65,129},{129,193},{193,1... | collective-permute-start | bytes 393224 | tf_op jit(solution)/shard_map/ppermute | solution.py:135
  47.2 15.0 %copy-start.5 = (bf16[8,8,1024]{2,1,0:T(8,128)(2,1)S(1)}, bf16[8,8,1024]{2,1,0:T(8,128)(2,1)}, u32[]{:S(2)}) copy-start(bf16[8,8,1024]{2,1,0:T(8,128)(2,1)} %copy-done.4) | copy-start | bytes 393220
  56.0 0.7 copy-start.6
  56.7 5.5 %copy-start.7 = (bf16[8,8,1024]{2,1,0:T(8,128)(2,1)S(1)}, bf16[8,8,1024]{2,1,0:T(8,128)(2,1)}, u32[]{:S(2)}) copy-start(bf16[8,8,1024]{2,1,0:T(8,128)(2,1)} %copy-done.6) | copy-start | bytes 393220
  56.8 12.8 %collective-permute-start.16 = (bf16[4,8,8,1024]{3,2,1,0:T(8,128)(2,1)S(1)}, bf16[4,8,8,1024]{3,2,1,0:T(8,128)(2,1)S(1)}, u32[]{:S(2)}, u32[]{:S(2)}) collective-permute-start(bf16[4,8,8,1024]{3,2,1,0:T(8,128)(2,1)S(1)} %pad_maximum_fusion.3), channel_id=1, source_target_pairs={{0,24},{1,25},{64,88},{65,89},{128,152},{129,153},{192,216},{193,2... | collective-permute-start | bytes 1572872 | tf_op jit(solution)/shard_map/ppermute | solution.py:131
  59.9 13.2 %collective-permute-start.15 = (bf16[4,8,8,1024]{3,2,1,0:T(8,128)(2,1)S(1)}, bf16[4,8,8,1024]{3,2,1,0:T(8,128)(2,1)S(1)}, u32[]{:S(2)}, u32[]{:S(2)}) collective-permute-start(bf16[4,8,8,1024]{3,2,1,0:T(8,128)(2,1)S(1)} %pad_maximum_fusion.3), channel_id=1, source_target_pairs={{0,8},{1,9},{64,72},{65,73},{128,136},{129,137},{192,200},{193,201... | collective-permute-start | bytes 1572872 | tf_op jit(solution)/shard_map/ppermute | solution.py:131
  59.9 6.4 %collective-permute-start.18 = (bf16[2,8,8,1024]{3,2,1,0:T(8,128)(2,1)S(1)}, bf16[2,8,8,1024]{3,2,1,0:T(8,128)(2,1)S(1)}, u32[]{:S(2)}, u32[]{:S(2)}) collective-permute-start(bf16[2,8,8,1024]{3,2,1,0:T(8,128)(2,1)S(1)} %pad_maximum_fusion.11), channel_id=1, source_target_pairs={{0,224},{1,225},{64,0},{65,1},{128,64},{129,65},{192,128},{193,129... | collective-permute-start | bytes 786440 | tf_op jit(solution)/shard_map/ppermute | solution.py:131
  60.1 6.4 %collective-permute-start.17 = (bf16[2,8,8,1024]{3,2,1,0:T(8,128)(2,1)S(1)}, bf16[2,8,8,1024]{3,2,1,0:T(8,128)(2,1)S(1)}, u32[]{:S(2)}, u32[]{:S(2)}) collective-permute-start(bf16[2,8,8,1024]{3,2,1,0:T(8,128)(2,1)S(1)} %slice.61), channel_id=1, source_target_pairs={{0,64},{1,65},{64,128},{65,129},{128,192},{129,193},{192,32},{193,... | collective-permute-start | bytes 786440 | tf_op jit(solution)/shard_map/ppermute | solution.py:131
  63.2 10.1 %collective-permute-start.19 = (bf16[4,8,8,1024]{3,2,1,0:T(8,128)(2,1)S(1)}, bf16[4,8,8,1024]{3,2,1,0:T(8,128)(2,1)S(1)}, u32[]{:S(2)}, u32[]{:S(2)}) collective-permute-start(bf16[4,8,8,1024]{3,2,1,0:T(8,128)(2,1)S(1)} %pad_maximum_fusion.5.mine), channel_id=1, source_target_pairs={{0,1},{1,0},{64,65},{65,64},{128,129},{129,128},{192,193},{193,192... | collective-permute-start | bytes 1572872 | tf_op jit(solution)/shard_map/ppermute | solution.py:131
  87.6 2.0 %copy-start = (f32[4,2,16,8,1024]{4,3,2,1,0:T(8,128)}, f32[4,2,16,8,1024]{4,3,2,1,0:T(8,128)S(1)}, u32[]{:S(2)}) copy-start(f32[4,2,16,8,1024]{4,3,2,1,0:T(8,128)S(1)} %shard_map.118.before) | copy-start | bytes 12582916

commit v3 on v2

--- a/solution.py
+++ b/solution.py
@@ -131,8 +131,17 @@
     return lax.ppermute(value, AXES, pairs)
 
 
-def own_only(value, k):
-    return lax.ppermute(value, "win", [(i, (i + k) % 4) for i in range(4)])
+def turn_rows(value, m):
+    pairs = []
+    for x in range(4):
+        for high in range(2):
+            for y in range(4):
+                for low in range(4):
+                    for core in range(2):
+                        k = 2 * core + m
+                        source = device_at(x, y, high * 4 + low, core)
+                        pairs.append((source, device_at(x, (low - k) % 4, high * 4 + y, core)))
+    return lax.ppermute(value, AXES, pairs)
 
 
 def together(*values):
@@ -140,40 +149,32 @@
 
 
 def first_step(plain, weighted):
+    both = jnp.stack([weighted, shift(weighted, dcore=1)])
     return together(
         shift(plain, dz=4),
         shift(plain, dx=2),
         shift(plain, dz=1),
         shift(plain, dz=-1),
-        shift(weighted, dy=1),
-        shift(weighted, dy=2),
-        shift(weighted, dy=3),
-    )
-
-
-def second_step(plain, weighted, arrived, y, z_low):
-    opposite, across, below, above, *sides = arrived
+        turn_rows(both, 0),
+        turn_rows(both, 1),
+    )
+
+
+def second_step(plain, arrived):
+    opposite, across, below, above, *turned = arrived
     near = jnp.stack([plain, below, above, opposite])
-    held = jnp.stack([weighted, *sides])
-
-    def for_offset(k):
-        return lax.dynamic_index_in_dim(held, (y - z_low - k) % 4, 0, keepdims=False)
-
-    sent = together(
+    mine = jnp.stack(turned)
+    other, left, right, up, down, across_opposite = together(
+        shift(mine, dcore=1),
         shift(near, dx=1),
         shift(near, dx=-1),
         shift(jnp.stack([below, opposite, across]), dz=1),
         shift(jnp.stack([above, opposite, across]), dz=-1),
         shift(opposite, dx=2),
-        own_only(for_offset(1), 1),
-        own_only(for_offset(2), 2),
-        own_only(for_offset(3), 3),
-    )
-    left, right, up, down, across_opposite, *rows = sent
+    )
     far = jnp.concatenate([up[:2], down[:2]])
     across_near = jnp.stack([across, up[2], down[2], across_opposite])
-    mine = jnp.stack([for_offset(0), *rows])
-    return near, far, left, right, across_near, mine
+    return near, far, left, right, across_near, mine, other
 
 
 def third_step(far, across_near):
@@ -194,10 +195,12 @@
 def load_rows(place, mine, other, z_re, z_im, z_sum):
     core = place[CORE]
     for k in range(4):
+        ref, m = (mine, k) if k < 2 else (other, k - 2)
         group = place[ROWS + k]
-        for ref, at in ((mine, core), (other, 1 - core)):
+        for n in range(2):
+            at = core if (k < 2) == (n == 0) else 1 - core
             for w in range(8):
-                value = ref[k, w].astype(jnp.float32)
+                value = ref[m, n, w].astype(jnp.float32)
                 re, im = value[:, :BINS], value[:, BINS:]
                 for tile in range(4):
                     lanes = slice(tile * 128, tile * 128 + 128)
@@ -379,13 +382,12 @@
             near_z % 4,
             far_z // 4,
             far_z % 4,
-            (z_low - jnp.arange(4)) % 4,
+            (col // 2 + (2 * (col % 2) + jnp.arange(4))) % 4,
             jnp.stack([col % 2]),
         ]
     ).astype(jnp.int32)
     arrived = first_step(plain, weighted)
-    near, far, left, right, across, mine = second_step(plain, weighted, arrived, col // 2, z_low)
-    other = shift(mine, dcore=1)
+    near, far, left, right, across, mine, other = second_step(plain, arrived)
     rest = third_step(far, across)
     before = near_totals(place, jnp.stack([near, far, left, right, across]), mine, other)
     corr = correlations(place, rest, before, mine, other)

time: 112 us -> 131 us (1.17)
  the two profiles are of different devices: /device:TPU:64 before, /device:TPU:6 now
where the time goes in v3:
time: 131 us; the launch traced here: 129 us
  starting transfers between devices  39.3 us (30%)
  Pallas kernels  36.8 us (28%)
  waiting for transfers between devices  36.1 us (28%)
  local copies, waits for them, and re-layouts  7.23 us (6%)
  other arithmetic  5.46 us (4%)
  matrix products  3.72 us (3%)
    ppermute x15, starting transfers between devices, shift(): return lax.ppermute(value, AXES, pairs)  35.5 us
    pallas_call x1, Pallas kernels, correlations(): pl.pallas_call(far_kernel, out_shape=jax.ShapeDtypeStruct((16, 2, 4, 8, L...  22.5 us
    ppermute x2, waiting for transfers between devices, turn_rows(): return lax.ppermute(value, AXES, pairs)  19.4 us
    ppermute x15, waiting for transfers between devices, shift(): return lax.ppermute(value, AXES, pairs)  16.6 us
    pallas_call x1, Pallas kernels, near_totals(): pl.pallas_call(near_kernel, out_shape=jax.ShapeDtypeStruct((4, *TOTAL[1:]...  14.3 us
    ppermute x2, starting transfers between devices, turn_rows(): return lax.ppermute(value, AXES, pairs)  3.76 us
    unnamed x24, local copies, waits for them, and re-layouts  3.25 us
    dot_general x4, matrix products, product(): return jnp.dot(left, table, preferred_element_type=jnp.float32)  2.93 us
  transfers between devices with their start and end apart: 17, of which 5 were waited for; matrix products, arithmetic and copies ran while one was open for 1% of the time, Pallas kernels for 11%

profile of v3, /device:TPU:6, one launch (start us, length us, event | category | flops | bytes accessed | tf_op | source)
XLA Modules:
  0.0 129.1 jit_solution(17394107846342640714)
XLA Ops:
  0.0 1.7 %convert_reduce_fusion = f32[8,8]{1,0:T(8,128)S(1)} fusion(bf16[8,8,12000]{2,1,0:T(8,128)(2,1)} %param.12), kind=kLoop, calls=%fused_computation | loop fusion | flops 1535936 | bytes 1536256 | tf_op jit(solution)/shard_map/reduce_sum | solution.py:83
  1.7 0.1 div.68
  1.8 1.9 %fusion.3 = f32[64,12000]{1,0:T(8,128)S(1)} fusion(bf16[8,8,12000]{2,1,0:T(8,128)(2,1)} %param.12, f32[12000]{0:T(1024)} %constant.151, f32[64]{0:T(128)S(1)} %div.68), kind=kLoop, calls=%fused_computation.6 | loop fusion | flops 3840000 | bytes 4656256 | tf_op jit(solution)/shard_map/convert_element_type | solution.py:84
  3.8 0.0 copy-start.2
  3.8 0.9 fusion.7
  4.6 0.0 copy-done.9
  4.6 0.0 copy-start.1
  4.6 0.9 fusion.6
  5.5 0.2 copy-done.2
  5.7 0.6 fusion.8
  6.3 0.4 copy-done.1
  6.8 0.6 convolution_add_fusion.1
  7.4 0.0 copy-start.7
  7.4 0.6 copy-done.3
  8.0 0.8 fusion.13
  8.8 0.0 copy-start.8
  8.8 5.9 %collective-permute-start.3 = (bf16[8,8,1024]{2,1,0:T(8,128)(2,1)S(1)}, bf16[8,8,1024]{2,1,0:T(8,128)(2,1)S(1)}, u32[]{:S(2)}, u32[]{:S(2)}) collective-permute-start(bf16[8,8,1024]{2,1,0:T(8,128)(2,1)S(1)} %get-tuple-element.44), channel_id=1, source_target_pairs={{0,224},{1,225},{64,0},{65,1},{128,64},{129,65},{192,128},{193,129... | collective-permute-start | bytes 393224 | tf_op jit(solution)/shard_map/ppermute | solution.py:131
  14.8 0.0 collective-permute-start.2
  14.8 1.4 %collective-permute-start.1 = (bf16[8,8,1024]{2,1,0:T(8,128)(2,1)S(1)}, bf16[8,8,1024]{2,1,0:T(8,128)(2,1)S(1)}, u32[]{:S(2)}, u32[]{:S(2)}) collective-permute-start(bf16[8,8,1024]{2,1,0:T(8,128)(2,1)S(1)} %get-tuple-element.44), channel_id=1, source_target_pairs={{0,16},{1,17},{64,80},{65,81},{128,144},{129,145},{192,208},{193,2... | collective-permute-start | bytes 393224 | tf_op jit(solution)/shard_map/ppermute | solution.py:131
  16.2 0.1 fusion.10
  16.3 0.1 collective-permute-start.4
  16.4 0.1 fusion.9
  16.5 1.2 collective-permute-done.4
  17.7 3.1 %collective-permute-start.6 = (bf16[2,8,8,1024]{3,2,1,0:T(8,128)(2,1)S(1)}, bf16[2,8,8,1024]{3,2,1,0:T(8,128)(2,1)S(1)}, u32[]{:S(2)}, u32[]{:S(2)}) collective-permute-start(bf16[2,8,8,1024]{3,2,1,0:T(8,128)(2,1)S(1)} %pad_maximum_fusion.10), channel_id=1, source_target_pairs={{0,6},{1,3},{64,0},{65,5},{128,2},{129,7},{192,4},{193,1},{2,70},{... | collective-permute-start | bytes 786440 | tf_op jit(solution)/shard_map/ppermute | solution.py:144
  20.8 0.7 collective-permute-start.5
  21.5 0.0 collective-permute-done.3
  21.5 3.4 %collective-permute-start = (bf16[8,8,1024]{2,1,0:T(8,128)(2,1)S(1)}, bf16[8,8,1024]{2,1,0:T(8,128)(2,1)S(1)}, u32[]{:S(2)}, u32[]{:S(2)}) collective-permute-start(bf16[8,8,1024]{2,1,0:T(8,128)(2,1)S(1)} %get-tuple-element.44), channel_id=1, source_target_pairs={{0,32},{1,33},{64,96},{65,97},{128,160},{129,161},{192,224},{193,2... | collective-permute-start | bytes 393224 | tf_op jit(solution)/shard_map/ppermute | solution.py:131
  25.0 0.0 collective-permute-done.2
  25.0 0.0 collective-permute-done.1
  25.0 6.7 %collective-permute-done = bf16[8,8,1024]{2,1,0:T(8,128)(2,1)S(1)} collective-permute-done((bf16[8,8,1024]{2,1,0:T(8,128)(2,1)S(1)}, bf16[8,8,1024]{2,1,0:T(8,128)(2,1)S(1)}, u32[]{:S(2)}, u32[]{:S(2)}) %collective-permute-start) | collective-permute-done | bytes 131104 | tf_op jit(solution)/shard_map/ppermute | solution.py:131
  31.7 19.4 %collective-permute-done.6 = bf16[2,8,8,1024]{3,2,1,0:T(8,128)(2,1)S(1)} collective-permute-done((bf16[2,8,8,1024]{3,2,1,0:T(8,128)(2,1)S(1)}, bf16[2,8,8,1024]{3,2,1,0:T(8,128)(2,1)S(1)}, u32[]{:S(2)}, u32[]{:S(2)}) %collective-permute-start.6) | collective-permute-done | bytes 262176 | tf_op jit(solution)/shard_map/ppermute | solution.py:144
  51.1 0.0 collective-permute-done.5
  51.1 2.1 %collective-permute-start.12 = (bf16[8,8,1024]{2,1,0:T(8,128)(2,1)S(1)}, bf16[8,8,1024]{2,1,0:T(8,128)(2,1)S(1)}, u32[]{:S(2)}, u32[]{:S(2)}) collective-permute-start(bf16[8,8,1024]{2,1,0:T(8,128)(2,1)S(1)} %collective-permute-done), channel_id=1, source_target_pairs={{0,16},{1,17},{64,80},{65,81},{128,144},{129,145},{192,208},{193,2... | collective-permute-start | bytes 393224 | tf_op jit(solution)/shard_map/ppermute | solution.py:131
  53.2 0.1 pad_maximum_fusion.2
  53.3 0.9 collective-permute-start.9
  54.2 2.4 %collective-permute-start.8 = (bf16[4,8,8,1024]{3,2,1,0:T(8,128)(2,1)S(1)}, bf16[4,8,8,1024]{3,2,1,0:T(8,128)(2,1)S(1)}, u32[]{:S(2)}, u32[]{:S(2)}) collective-permute-start(bf16[4,8,8,1024]{3,2,1,0:T(8,128)(2,1)S(1)} %pad_maximum_fusion.2), channel_id=1, source_target_pairs={{0,8},{1,9},{64,72},{65,73},{128,136},{129,137},{192,200},{193,201... | collective-permute-start | bytes 1572872 | tf_op jit(solution)/shard_map/ppermute | solution.py:131
  56.6 0.1 pad_maximum_fusion.1.mine
  56.7 0.1 collective-permute-start.7
  56.8 1.0 pad_maximum_fusion.5
  57.7 9.3 %collective-permute-start.11 = (bf16[3,8,8,1024]{3,2,1,0:T(8,128)(2,1)}, bf16[3,8,8,1024]{3,2,1,0:T(8,128)(2,1)}, u32[]{:S(2)}, u32[]{:S(2)}) collective-permute-start(bf16[3,8,8,1024]{3,2,1,0:T(8,128)(2,1)} %get-tuple-element.41), channel_id=1, source_target_pairs={{0,224},{1,225},{64,0},{65,1},{128,64},{129,65},{192,128},{193,129... | collective-permute-start | bytes 1179656 | tf_op jit(solution)/shard_map/ppermute | solution.py:131
  67.1 0.0 collective-permute-done.12
  67.1 3.8 %collective-permute-start.10 = (bf16[3,8,8,1024]{3,2,1,0:T(8,128)(2,1)}, bf16[3,8,8,1024]{3,2,1,0:T(8,128)(2,1)}, u32[]{:S(2)}, u32[]{:S(2)}) collective-permute-start(bf16[3,8,8,1024]{3,2,1,0:T(8,128)(2,1)} %get-tuple-element.42), channel_id=1, source_target_pairs={{0,64},{1,65},{64,128},{65,129},{128,192},{129,193},{192,32},{193,... | collective-permute-start | bytes 1179656 | tf_op jit(solution)/shard_map/ppermute | solution.py:131
  70.9 0.1 concatenate.23.place
  71.0 8.6 %collective-permute-done.11 = bf16[3,8,8,1024]{3,2,1,0:T(8,128)(2,1)} collective-permute-done((bf16[3,8,8,1024]{3,2,1,0:T(8,128)(2,1)}, bf16[3,8,8,1024]{3,2,1,0:T(8,128)(2,1)}, u32[]{:S(2)}, u32[]{:S(2)}) %collective-permute-start.11) | collective-permute-done | bytes 393248 | tf_op jit(solution)/shard_map/ppermute | solution.py:131
  79.6 0.1 collective-permute-done.10
  79.7 0.0 collective-permute-done.9
  79.7 0.0 collective-permute-done.8
  79.7 0.0 collective-permute-done.7.other
  79.8 0.9 slice.60
  80.7 1.0 slice.58
  81.6 0.9 slice.59
  82.6 1.0 slice.57
  83.6 0.1 collective-permute-start.14
  83.7 3.2 %collective-permute-start.13 = (bf16[4,8,8,1024]{3,2,1,0:T(8,128)(2,1)S(1)}, bf16[4,8,8,1024]{3,2,1,0:T(8,128)(2,1)S(1)}, u32[]{:S(2)}, u32[]{:S(2)}) collective-permute-start(bf16[4,8,8,1024]{3,2,1,0:T(8,128)(2,1)S(1)} %pad_maximum_fusion.3), channel_id=1, source_target_pairs={{0,8},{1,9},{64,72},{65,73},{128,136},{129,137},{192,200},{193,201... | collective-permute-start | bytes 1572872 | tf_op jit(solution)/shard_map/ppermute | solution.py:131
  86.9 1.9 %collective-permute-start.16 = (bf16[2,8,8,1024]{3,2,1,0:T(8,128)(2,1)S(1)}, bf16[2,8,8,1024]{3,2,1,0:T(8,128)(2,1)S(1)}, u32[]{:S(2)}, u32[]{:S(2)}) collective-permute-start(bf16[2,8,8,1024]{3,2,1,0:T(8,128)(2,1)S(1)} %pad_maximum_fusion.11), channel_id=1, source_target_pairs={{0,224},{1,225},{64,0},{65,1},{128,64},{129,65},{192,128},{193,129... | collective-permute-start | bytes 786440 | tf_op jit(solution)/shard_map/ppermute | solution.py:131
  88.9 0.1 pad_maximum_fusion.4
  89.0 0.7 collective-permute-start.15
  89.9 14.3 %shard_map.118.before = f32[4,2,16,8,1024]{4,3,2,1,0:T(8,128)S(1)} custom-call(s32[25]{0:T(128)S(1)} %concatenate.23.place, bf16[5,4,8,8,1024]{4,3,2,1,0:T(8,128)(2,1)S(1)} %bitcast_dynamic-update-slice_fusion.block, bf16[2,2,8,8,1024]{4,3,2,1,0:T(8,128)(2,1)S(1)} %pad_maximum_fusion.1.mine, bf16[2,2,8,8,1024]{4,3,2,1,0:T(8,128)(2,1)S(1)} %collective-permute-done.7.other), custom_call_target="tpu_custom_call" | custom-call | flops 12000000000 | bytes 8388608 | tf_op jit(solution)/shard_map/pallas_call | solution.py:268
  104.2 2.0 %copy-done = f32[4,2,16,8,1024]{4,3,2,1,0:T(8,128)} copy-done((f32[4,2,16,8,1024]{4,3,2,1,0:T(8,128)}, f32[4,2,16,8,1024]{4,3,2,1,0:T(8,128)S(1)}, u32[]{:S(2)}) %copy-start) | copy-done | bytes 4194328
  106.1 0.0 collective-permute-done.16
  106.1 0.0 collective-permute-done.15
  106.1 0.0 collective-permute-done.14
  106.2 0.2 pad_maximum_fusion.block
  106.4 22.5 %shard_map.119 = bf16[16,2,4,8,4000]{4,3,2,1,0:T(8,128)(2,1)} custom-call(s32[25]{0:T(128)S(1)} %concatenate.23.place, bf16[3,4,8,8,1024]{4,3,2,1,0:T(8,128)(2,1)S(1)} %pad_maximum_fusion.block, f32[4,2,16,8,1024]{4,3,2,1,0:T(8,128)} %copy-done, bf16[2,2,8,8,1024]{4,3,2,1,0:T(8,128)(2,1)S(1)} %pad_maximum_fusion.1.mine, ...), custom_call_target="tpu_custom_call" | custom-call | flops 8388608000 | bytes 25165824 | tf_op jit(solution)/shard_map/pallas_call | solution.py:340
  (32 shorter events, 0.5 us)
Async XLA Ops:
  1.7 2.0 %copy-start.10 = (bf16[3000,256]{1,0:T(8,128)(2,1)S(1)}, bf16[3000,256]{1,0:T(8,128)(2,1)}, u32[]{:S(2)}) copy-start(bf16[3000,256]{1,0:T(8,128)(2,1)} %constant.142.clone) | copy-start | bytes 4608004
  1.8 2.8 %copy-start.9 = (bf16[3000,256]{1,0:T(8,128)(2,1)S(1)}, bf16[3000,256]{1,0:T(8,128)(2,1)}, u32[]{:S(2)}) copy-start(bf16[3000,256]{1,0:T(8,128)(2,1)} %constant.141.clone) | copy-start | bytes 4608004
  3.8 2.0 %copy-start.2 = (bf16[3000,512]{1,0:T(8,128)(2,1)S(1)}, bf16[3000,512]{1,0:T(8,128)(2,1)}, u32[]{:S(2)}) copy-start(bf16[3000,512]{1,0:T(8,128)(2,1)} %constant.152) | copy-start | bytes 9216004
  4.6 2.1 %copy-start.1 = (bf16[3000,512]{1,0:T(8,128)(2,1)S(1)}, bf16[3000,512]{1,0:T(8,128)(2,1)}, u32[]{:S(2)}) copy-start(bf16[3000,512]{1,0:T(8,128)(2,1)} %constant.153) | copy-start | bytes 9216004
  6.8 1.2 copy-start.3
  6.8 1.2 copy-start.5
  6.8 9.4 %copy-start.4 = (f32[8]{0:T(128)S(1)}, f32[8]{0:T(128)}, u32[]{:S(2)}) copy-start(f32[8]{0:T(128)} %param.13) | copy-start | bytes 100
  7.4 14.1 %copy-start.6 = (s32[4]{0:T(128)S(1)}, s32[4]{0:T(128)}, u32[]{:S(2)}) copy-start(s32[4]{0:T(128)} %constant.147.clone) | copy-start | bytes 52
  7.4 14.1 %copy-start.7 = (s32[4]{0:T(128)S(1)}, s32[4]{0:T(128)}, u32[]{:S(2)}) copy-start(s32[4]{0:T(128)} %constant.146.clone) | copy-start | bytes 52
  8.8 62.1 %copy-start.8 = (s32[4]{0:T(128)S(1)}, s32[4]{0:T(128)}, u32[]{:S(2)}) copy-start(s32[4]{0:T(128)} %constant.148.clone) | copy-start | bytes 52
  8.8 12.7 %collective-permute-start.3 = (bf16[8,8,1024]{2,1,0:T(8,128)(2,1)S(1)}, bf16[8,8,1024]{2,1,0:T(8,128)(2,1)S(1)}, u32[]{:S(2)}, u32[]{:S(2)}) collective-permute-start(bf16[8,8,1024]{2,1,0:T(8,128)(2,1)S(1)} %get-tuple-element.44), channel_id=1, source_target_pairs={{0,224},{1,225},{64,0},{65,1},{128,64},{129,65},{192,128},{193,129... | collective-permute-start | bytes 393224 | tf_op jit(solution)/shard_map/ppermute | solution.py:131
  14.8 10.2 %collective-permute-start.2 = (bf16[8,8,1024]{2,1,0:T(8,128)(2,1)S(1)}, bf16[8,8,1024]{2,1,0:T(8,128)(2,1)S(1)}, u32[]{:S(2)}, u32[]{:S(2)}) collective-permute-start(bf16[8,8,1024]{2,1,0:T(8,128)(2,1)S(1)} %get-tuple-element.44), channel_id=1, source_target_pairs={{0,64},{1,65},{64,128},{65,129},{128,192},{129,193},{192,32},{193,... | collective-permute-start | bytes 393224 | tf_op jit(solution)/shard_map/ppermute | solution.py:131
  14.8 10.2 %collective-permute-start.1 = (bf16[8,8,1024]{2,1,0:T(8,128)(2,1)S(1)}, bf16[8,8,1024]{2,1,0:T(8,128)(2,1)S(1)}, u32[]{:S(2)}, u32[]{:S(2)}) collective-permute-start(bf16[8,8,1024]{2,1,0:T(8,128)(2,1)S(1)} %get-tuple-element.44), channel_id=1, source_target_pairs={{0,16},{1,17},{64,80},{65,81},{128,144},{129,145},{192,208},{193,2... | collective-permute-start | bytes 393224 | tf_op jit(solution)/shard_map/ppermute | solution.py:131
  16.3 1.4 %collective-permute-start.4 = (bf16[8,8,1024]{2,1,0:T(8,128)(2,1)S(1)}, bf16[8,8,1024]{2,1,0:T(8,128)(2,1)S(1)}, u32[]{:S(2)}, u32[]{:S(2)}) collective-permute-start(bf16[8,8,1024]{2,1,0:T(8,128)(2,1)S(1)} %fusion.10), channel_id=1, source_target_pairs={{0,1},{1,0},{64,65},{65,64},{128,129},{129,128},{192,193},{193,192... | collective-permute-start | bytes 393224 | tf_op jit(solution)/shard_map/ppermute | solution.py:131
  17.7 33.4 %collective-permute-start.6 = (bf16[2,8,8,1024]{3,2,1,0:T(8,128)(2,1)S(1)}, bf16[2,8,8,1024]{3,2,1,0:T(8,128)(2,1)S(1)}, u32[]{:S(2)}, u32[]{:S(2)}) collective-permute-start(bf16[2,8,8,1024]{3,2,1,0:T(8,128)(2,1)S(1)} %pad_maximum_fusion.10), channel_id=1, source_target_pairs={{0,6},{1,3},{64,0},{65,5},{128,2},{129,7},{192,4},{193,1},{2,70},{... | collective-permute-start | bytes 786440 | tf_op jit(solution)/shard_map/ppermute | solution.py:144
  20.8 30.3 %collective-permute-start.5 = (bf16[2,8,8,1024]{3,2,1,0:T(8,128)(2,1)S(1)}, bf16[2,8,8,1024]{3,2,1,0:T(8,128)(2,1)S(1)}, u32[]{:S(2)}, u32[]{:S(2)}) collective-permute-start(bf16[2,8,8,1024]{3,2,1,0:T(8,128)(2,1)S(1)} %pad_maximum_fusion.10), channel_id=1, source_target_pairs={{0,0},{1,5},{64,2},{65,7},{128,4},{129,1},{192,6},{193,3},{2,64},{... | collective-permute-start | bytes 786440 | tf_op jit(solution)/shard_map/ppermute | solution.py:144
  21.5 10.1 %collective-permute-start = (bf16[8,8,1024]{2,1,0:T(8,128)(2,1)S(1)}, bf16[8,8,1024]{2,1,0:T(8,128)(2,1)S(1)}, u32[]{:S(2)}, u32[]{:S(2)}) collective-permute-start(bf16[8,8,1024]{2,1,0:T(8,128)(2,1)S(1)} %get-tuple-element.44), channel_id=1, source_target_pairs={{0,32},{1,33},{64,96},{65,97},{128,160},{129,161},{192,224},{193,2... | collective-permute-start | bytes 393224 | tf_op jit(solution)/shard_map/ppermute | solution.py:131
  51.1 16.0 %collective-permute-start.12 = (bf16[8,8,1024]{2,1,0:T(8,128)(2,1)S(1)}, bf16[8,8,1024]{2,1,0:T(8,128)(2,1)S(1)}, u32[]{:S(2)}, u32[]{:S(2)}) collective-permute-start(bf16[8,8,1024]{2,1,0:T(8,128)(2,1)S(1)} %collective-permute-done), channel_id=1, source_target_pairs={{0,16},{1,17},{64,80},{65,81},{128,144},{129,145},{192,208},{193,2... | collective-permute-start | bytes 393224 | tf_op jit(solution)/shard_map/ppermute | solution.py:131
  53.3 26.4 %collective-permute-start.9 = (bf16[4,8,8,1024]{3,2,1,0:T(8,128)(2,1)S(1)}, bf16[4,8,8,1024]{3,2,1,0:T(8,128)(2,1)S(1)}, u32[]{:S(2)}, u32[]{:S(2)}) collective-permute-start(bf16[4,8,8,1024]{3,2,1,0:T(8,128)(2,1)S(1)} %pad_maximum_fusion.2), channel_id=1, source_target_pairs={{0,24},{1,25},{64,88},{65,89},{128,152},{129,153},{192,216},{193,2... | collective-permute-start | bytes 1572872 | tf_op jit(solution)/shard_map/ppermute | solution.py:131
  54.2 25.5 %collective-permute-start.8 = (bf16[4,8,8,1024]{3,2,1,0:T(8,128)(2,1)S(1)}, bf16[4,8,8,1024]{3,2,1,0:T(8,128)(2,1)S(1)}, u32[]{:S(2)}, u32[]{:S(2)}) collective-permute-start(bf16[4,8,8,1024]{3,2,1,0:T(8,128)(2,1)S(1)} %pad_maximum_fusion.2), channel_id=1, source_target_pairs={{0,8},{1,9},{64,72},{65,73},{128,136},{129,137},{192,200},{193,201... | collective-permute-start | bytes 1572872 | tf_op jit(solution)/shard_map/ppermute | solution.py:131
  56.7 23.1 %collective-permute-start.7 = (bf16[2,2,8,8,1024]{4,3,2,1,0:T(8,128)(2,1)S(1)}, bf16[2,2,8,8,1024]{4,3,2,1,0:T(8,128)(2,1)S(1)}, u32[]{:S(2)}, u32[]{:S(2)}) collective-permute-start(bf16[2,2,8,8,1024]{4,3,2,1,0:T(8,128)(2,1)S(1)} %pad_maximum_fusion.1.mine), channel_id=1, source_target_pairs={{0,1},{1,0},{64,65},{65,64},{128,129},{129,128},{192,193},{193,192... | collective-permute-start | bytes 1572872 | tf_op jit(solution)/shard_map/ppermute | solution.py:131
  57.7 21.9 %collective-permute-start.11 = (bf16[3,8,8,1024]{3,2,1,0:T(8,128)(2,1)}, bf16[3,8,8,1024]{3,2,1,0:T(8,128)(2,1)}, u32[]{:S(2)}, u32[]{:S(2)}) collective-permute-start(bf16[3,8,8,1024]{3,2,1,0:T(8,128)(2,1)} %get-tuple-element.41), channel_id=1, source_target_pairs={{0,224},{1,225},{64,0},{65,1},{128,64},{129,65},{192,128},{193,129... | collective-permute-start | bytes 1179656 | tf_op jit(solution)/shard_map/ppermute | solution.py:131
  67.1 12.7 %collective-permute-start.10 = (bf16[3,8,8,1024]{3,2,1,0:T(8,128)(2,1)}, bf16[3,8,8,1024]{3,2,1,0:T(8,128)(2,1)}, u32[]{:S(2)}, u32[]{:S(2)}) collective-permute-start(bf16[3,8,8,1024]{3,2,1,0:T(8,128)(2,1)} %get-tuple-element.42), channel_id=1, source_target_pairs={{0,64},{1,65},{64,128},{65,129},{128,192},{129,193},{192,32},{193,... | collective-permute-start | bytes 1179656 | tf_op jit(solution)/shard_map/ppermute | solution.py:131
  83.6 22.6 %collective-permute-start.14 = (bf16[4,8,8,1024]{3,2,1,0:T(8,128)(2,1)S(1)}, bf16[4,8,8,1024]{3,2,1,0:T(8,128)(2,1)S(1)}, u32[]{:S(2)}, u32[]{:S(2)}) collective-permute-start(bf16[4,8,8,1024]{3,2,1,0:T(8,128)(2,1)S(1)} %pad_maximum_fusion.3), channel_id=1, source_target_pairs={{0,24},{1,25},{64,88},{65,89},{128,152},{129,153},{192,216},{193,2... | collective-permute-start | bytes 1572872 | tf_op jit(solution)/shard_map/ppermute | solution.py:131
  83.7 22.5 %collective-permute-start.13 = (bf16[4,8,8,1024]{3,2,1,0:T(8,128)(2,1)S(1)}, bf16[4,8,8,1024]{3,2,1,0:T(8,128)(2,1)S(1)}, u32[]{:S(2)}, u32[]{:S(2)}) collective-permute-start(bf16[4,8,8,1024]{3,2,1,0:T(8,128)(2,1)S(1)} %pad_maximum_fusion.3), channel_id=1, source_target_pairs={{0,8},{1,9},{64,72},{65,73},{128,136},{129,137},{192,200},{193,201... | collective-permute-start | bytes 1572872 | tf_op jit(solution)/shard_map/ppermute | solution.py:131
  86.9 19.2 %collective-permute-start.16 = (bf16[2,8,8,1024]{3,2,1,0:T(8,128)(2,1)S(1)}, bf16[2,8,8,1024]{3,2,1,0:T(8,128)(2,1)S(1)}, u32[]{:S(2)}, u32[]{:S(2)}) collective-permute-start(bf16[2,8,8,1024]{3,2,1,0:T(8,128)(2,1)S(1)} %pad_maximum_fusion.11), channel_id=1, source_target_pairs={{0,224},{1,225},{64,0},{65,1},{128,64},{129,65},{192,128},{193,129... | collective-permute-start | bytes 786440 | tf_op jit(solution)/shard_map/ppermute | solution.py:131
  89.0 17.2 %collective-permute-start.15 = (bf16[2,8,8,1024]{3,2,1,0:T(8,128)(2,1)S(1)}, bf16[2,8,8,1024]{3,2,1,0:T(8,128)(2,1)S(1)}, u32[]{:S(2)}, u32[]{:S(2)}) collective-permute-start(bf16[2,8,8,1024]{3,2,1,0:T(8,128)(2,1)S(1)} %slice.61), channel_id=1, source_target_pairs={{0,64},{1,65},{64,128},{65,129},{128,192},{129,193},{192,32},{193,... | collective-permute-start | bytes 786440 | tf_op jit(solution)/shard_map/ppermute | solution.py:131
  104.2 2.0 %copy-start = (f32[4,2,16,8,1024]{4,3,2,1,0:T(8,128)}, f32[4,2,16,8,1024]{4,3,2,1,0:T(8,128)S(1)}, u32[]{:S(2)}) copy-start(f32[4,2,16,8,1024]{4,3,2,1,0:T(8,128)S(1)} %shard_map.118.before) | copy-start | bytes 12582916

commit v4 on v2

--- a/solution.py
+++ b/solution.py
@@ -154,36 +154,60 @@
 def second_step(plain, weighted, arrived, y, z_low):
     opposite, across, below, above, *sides = arrived
     near = jnp.stack([plain, below, above, opposite])
-    held = jnp.stack([weighted, *sides])
+    held = [weighted, *sides]
 
     def for_offset(k):
-        return lax.dynamic_index_in_dim(held, (y - z_low - k) % 4, 0, keepdims=False)
-
-    sent = together(
+        at = (y - z_low - k) % 4
+        low = jnp.where(at == 0, held[0], held[1])
+        high = jnp.where(at == 2, held[2], held[3])
+        return jnp.where(at < 2, low, high)
+
+    mine = jnp.stack([for_offset(0)] + [own_only(for_offset(k), k) for k in (1, 2, 3)])
+    return near, together(
+        mine,
+        shift(mine, dcore=1),
         shift(near, dx=1),
         shift(near, dx=-1),
         shift(jnp.stack([below, opposite, across]), dz=1),
         shift(jnp.stack([above, opposite, across]), dz=-1),
         shift(opposite, dx=2),
-        own_only(for_offset(1), 1),
-        own_only(for_offset(2), 2),
-        own_only(for_offset(3), 3),
-    )
-    left, right, up, down, across_opposite, *rows = sent
-    far = jnp.concatenate([up[:2], down[:2]])
-    across_near = jnp.stack([across, up[2], down[2], across_opposite])
-    mine = jnp.stack([for_offset(0), *rows])
-    return near, far, left, right, across_near, mine
-
-
-def third_step(far, across_near):
-    left, right, up, down = together(
+    )
+
+
+def repack_kernel(up, down, across_opposite, far, up_out, down_out, done):
+    pairs = (
+        (up.at[0:2], far.at[0:2]),
+        (down.at[0:2], far.at[2:4]),
+        (up.at[2], up_out.at[0]),
+        (across_opposite, up_out.at[1]),
+        (down.at[2], down_out.at[0]),
+        (across_opposite, down_out.at[1]),
+    )
+    copies = [
+        pltpu.make_async_copy(source, target, done.at[n])
+        for n, (source, target) in enumerate(pairs)
+    ]
+    for copy in copies:
+        copy.start()
+    for copy in copies:
+        copy.wait()
+
+
+def third_step(up, down, across_opposite):
+    block = up.shape[1:]
+    far, up_out, down_out = pl.pallas_call(
+        repack_kernel,
+        out_shape=[jax.ShapeDtypeStruct((n, *block), jnp.bfloat16) for n in (4, 2, 2)],
+        in_specs=[pl.BlockSpec(memory_space=pl.ANY)] * 3,
+        out_specs=[pl.BlockSpec(memory_space=pl.ANY)] * 3,
+        scratch_shapes=[pltpu.SemaphoreType.DMA((6,))],
+    )(up, down, across_opposite)
+    return together(
         shift(far, dx=1),
         shift(far, dx=-1),
-        shift(across_near[1::2], dz=1),
-        shift(across_near[2:], dz=-1),
-    )
-    return jnp.stack([left, right, jnp.concatenate([up, down])])
+        shift(up_out, dz=1),
+        shift(down_out, dz=-1),
+    )
 
 
 NEAR = (0, -1, 1, 4)
@@ -206,16 +230,15 @@
                     z_sum[group * 8 + w, at, tile] = re[:, lanes] + im[:, lanes]
 
 
-def add_cross(turn, block, high_at, group_at, place, z_re, z_im, z_sum, total):
-    tile, n = turn // 4, turn % 4
+def add_cross(tile, block, high, group, rows, total):
+    z_re, z_im, z_sum = rows
     lane = pl.ds(pl.multiple_of(tile * 128, 128), 128)
     lane_im = pl.ds(pl.multiple_of(tile * 128 + BINS, 128), 128)
-    high, group = place[high_at + n], place[group_at + n]
     for core, base in ((0, 0), (0, 4), (1, 0), (1, 4)):
         sums = [None] * 12
         for w in range(8):
-            yr = block[0, n, w, :, lane].astype(jnp.float32)
-            yi = block[0, n, w, :, lane_im].astype(jnp.float32)
+            yr = block[w, :, lane].astype(jnp.float32)
+            yi = block[w, :, lane_im].astype(jnp.float32)
             dif = yr - yi
             window = group * 8 + w
             for i in range(4):
@@ -234,106 +257,107 @@
             total[high, core * 8 + base + i, :, lane_im] += r - p + q
 
 
-def near_kernel(place, block, mine, other, total, z_re, z_im, z_sum):
-    step = pl.program_id(0)
-
-    @pl.when(step == 0)
-    def _():
-        load_rows(place, mine, other, z_re, z_im, z_sum)
-
-    @pl.when(step != 1)
-    def _():
-        total[...] = jnp.zeros_like(total)
-
-    high_at = jnp.where(step == 1, HIGH_FAR, HIGH_NEAR)
-    group_at = jnp.where(step == 1, GROUP_FAR, GROUP_NEAR)
-
-    def turn(at, carry):
-        add_cross(at, block, high_at, group_at, place, z_re, z_im, z_sum, total.at[0])
+def add_blocks(blocks, place, high_at, group_at, rows, total):
+    def tile_step(tile, carry):
+        for n, block in enumerate(blocks):
+            add_cross(tile, block, place[high_at + n], place[group_at + n], rows, total)
         return carry
 
-    lax.fori_loop(0, 16, turn, 0)
+    lax.fori_loop(0, 4, tile_step, 0)
+
+
+def settle(source, target):
+    for i in range(16):
+        rows = jnp.concatenate([source[0, i], source[1, i]], axis=0)
+        target[pl.ds(i * 16, 16), :] = rows.astype(jnp.bfloat16)
+
+
+def near_kernel(
+    place, near, up, down, left, right, across, across_opposite, mine, other, own, total, z_re, z_im, z_sum, sums
+):
+    rows = (z_re, z_im, z_sum)
+    load_rows(place, mine, other, *rows)
+    sums[...] = jnp.zeros_like(sums)
+    total[...] = jnp.zeros_like(total)
+    add_blocks([near.at[n] for n in range(4)], place, HIGH_NEAR, GROUP_NEAR, rows, sums)
+    far = [up.at[0], up.at[1], down.at[0], down.at[1]]
+    add_blocks(far, place, HIGH_FAR, GROUP_FAR, rows, sums)
+    settle(sums, own)
+    sides = (
+        [left.at[n] for n in range(4)],
+        [right.at[n] for n in range(4)],
+        [across, up.at[2], down.at[2], across_opposite],
+    )
+    for n, blocks in enumerate(sides):
+        add_blocks(blocks, place, HIGH_NEAR, GROUP_NEAR, rows, total.at[n])
 
 
 WHOLE = pl.BlockSpec(memory_space=pltpu.VMEM)
-BLOCK = (1, 4, 8, 8, 2 * BINS)
-TOTAL = (1, 2, 16, 8, 2 * BINS)
+SCALARS = pl.BlockSpec(memory_space=pltpu.SMEM)
+TOTAL = (2, 16, 8, 2 * BINS)
+OWN = jax.ShapeDtypeStruct((256, 2 * BINS), jnp.bfloat16)
 ROW_SCRATCH = [pltpu.VMEM((32, 2, 4, 8, 128), jnp.float32)] * 3
 
 
-def near_totals(place, blocks, mine, other):
+def near_totals(place, *blocks):
     return pl.pallas_call(
         near_kernel,
-        out_shape=jax.ShapeDtypeStruct((4, *TOTAL[1:]), jnp.float32),
-        grid_spec=pltpu.PrefetchScalarGridSpec(
-            num_scalar_prefetch=1,
-            grid=(5,),
-            in_specs=[
-                pl.BlockSpec(BLOCK, lambda j, place: (j, 0, 0, 0, 0)),
-                WHOLE,
-                WHOLE,
-            ],
-            out_specs=pl.BlockSpec(TOTAL, lambda j, place: (jnp.maximum(j - 1, 0), 0, 0, 0, 0)),
-            scratch_shapes=ROW_SCRATCH,
-        ),
-        compiler_params=pltpu.CompilerParams(vmem_limit_bytes=32 * 1024 * 1024),
+        out_shape=(OWN, jax.ShapeDtypeStruct((3, *TOTAL), jnp.float32)),
+        in_specs=[SCALARS] + [WHOLE] * len(blocks),
+        out_specs=(WHOLE, WHOLE),
+        scratch_shapes=[*ROW_SCRATCH, pltpu.VMEM(TOTAL, jnp.float32)],
+        compiler_params=pltpu.CompilerParams(vmem_limit_bytes=24 * 1024 * 1024),
         cost_estimate=pl.CostEstimate(
             flops=12 * 10**9, bytes_accessed=8 * 2**20, transcendentals=0
         ),
-    )(place, blocks, mine, other)
+    )(place, *blocks)
 
 
 def far_kernel(
-    place, block, before, mine, other, source, out, z_re, z_im, z_sum, total, now, later, table, ready
+    place, left, right, up, down, own, before, mine, other, source, out, z_re, z_im, z_sum, total, now, later, table, ready
 ):
     step = pl.program_id(0)
     fetch = pltpu.make_async_copy(source, table, ready)
-
-    def settle(source, target):
-        for i in range(16):
-            rows = jnp.concatenate([source[0, i], source[1, i]], axis=0)
-            target[pl.ds(i * 16, 16), :] = rows.astype(jnp.bfloat16)
+    rows = (z_re, z_im, z_sum)
 
     @pl.when(step == 0)
     def _():
         fetch.start()
-        load_rows(place, mine, other, z_re, z_im, z_sum)
-        settle(before.at[0], now)
-
-    def lag_all():
-        for tile in range(8):
-            start = tile * 512
-            keep = min(512, LAGS - start)
-            value = jnp.dot(
-                now[...], table[:, start : start + 512], preferred_element_type=jnp.float32
-            )
-            value = value.reshape(16, 2, 1, 8, 512).astype(jnp.bfloat16)
-            out[:, :, :, :, start : start + keep] = value[..., :keep]
-
-    @pl.when(step < 3)
-    def _():
-        total[...] = before[step + 1]
-
-        def turn(at, carry):
-            add_cross(at, block, HIGH_FAR, GROUP_FAR, place, z_re, z_im, z_sum, total)
-            return carry
-
-        lax.fori_loop(0, 16, turn, 0)
-        settle(total, later)
+        load_rows(place, mine, other, *rows)
+        now[...] = own[...]
+
+    chunks = (
+        [left.at[n] for n in range(4)],
+        [right.at[n] for n in range(4)],
+        [up.at[0], up.at[1], down.at[0], down.at[1]],
+    )
+    for n, blocks in enumerate(chunks):
+
+        @pl.when(step == n)
+        def _():
+            total[...] = before[0]
+            add_blocks(blocks, place, HIGH_FAR, GROUP_FAR, rows, total)
+            settle(total, later)
 
     @pl.when(step == 0)
     def _():
         fetch.wait()
 
-    lag_all()
+    for tile in range(8):
+        start = tile * 512
+        keep = min(512, LAGS - start)
+        value = jnp.dot(
+            now[...], table[:, start : start + 512], preferred_element_type=jnp.float32
+        )
+        value = value.reshape(16, 2, 1, 8, 512).astype(jnp.bfloat16)
+        out[:, :, :, :, start : start + keep] = value[..., :keep]
 
     @pl.when(step < 3)
     def _():
         now[...] = later[...]
 
 
-def correlations(place, blocks, before, mine, other):
-    last = lambda j: jnp.minimum(j, 2)
+def correlations(place, left, right, up, down, own, before, mine, other):
     return pl.pallas_call(
         far_kernel,
         out_shape=jax.ShapeDtypeStruct((16, 2, 4, 8, LAGS), jnp.bfloat16),
@@ -341,8 +365,12 @@
             num_scalar_prefetch=1,
             grid=(4,),
             in_specs=[
-                pl.BlockSpec(BLOCK, lambda j, place: (last(j), 0, 0, 0, 0)),
-                pl.BlockSpec((4, *TOTAL[1:]), lambda j, place: (0, 0, 0, 0, 0)),
+                WHOLE,
+                WHOLE,
+                WHOLE,
+                WHOLE,
+                WHOLE,
+                pl.BlockSpec((1, *TOTAL), lambda j, place: (jnp.minimum(j, 2), 0, 0, 0, 0)),
                 WHOLE,
                 WHOLE,
                 pl.BlockSpec(memory_space=pl.ANY),
@@ -350,18 +378,18 @@
             out_specs=pl.BlockSpec((16, 2, 1, 8, LAGS), lambda j, place: (0, 0, place[j], 0, 0)),
             scratch_shapes=[
                 *ROW_SCRATCH,
-                pltpu.VMEM(TOTAL[1:], jnp.float32),
+                pltpu.VMEM(TOTAL, jnp.float32),
                 pltpu.VMEM((256, 2 * BINS), jnp.bfloat16),
                 pltpu.VMEM((256, 2 * BINS), jnp.bfloat16),
                 pltpu.VMEM((2 * BINS, LAGS_PAD), jnp.bfloat16),
                 pltpu.SemaphoreType.DMA(()),
             ],
         ),
-        compiler_params=pltpu.CompilerParams(vmem_limit_bytes=48 * 1024 * 1024),
+        compiler_params=pltpu.CompilerParams(vmem_limit_bytes=32 * 1024 * 1024),
         cost_estimate=pl.CostEstimate(
             flops=2 * 1024 * 1024 * LAGS, bytes_accessed=24 * 2**20, transcendentals=0
         ),
-    )(place, blocks, before, mine, other, lag_table())
+    )(place, left, right, up, down, own, before, mine, other, lag_table())
 
 
 def shards(record, window_weight):
@@ -384,11 +412,13 @@
         ]
     ).astype(jnp.int32)
     arrived = first_step(plain, weighted)
-    near, far, left, right, across, mine = second_step(plain, weighted, arrived, col // 2, z_low)
-    other = shift(mine, dcore=1)
-    rest = third_step(far, across)
-    before = near_totals(place, jnp.stack([near, far, left, right, across]), mine, other)
-    corr = correlations(place, rest, before, mine, other)
+    near, sent = second_step(plain, weighted, arrived, col // 2, z_low)
+    mine, other, left, right, up, down, across_opposite = sent
+    rest = third_step(up, down, across_opposite)
+    own, before = near_totals(
+        place, near, up, down, left, right, arrived[1], across_opposite, mine, other
+    )
+    corr = correlations(place, *rest, own, before, mine, other)
     return corr.reshape(1, 1, 16, 8, 8, LAGS)
 
 

time: 112 us -> 142 us (1.27)
  the two profiles are of different devices: /device:TPU:64 before, /device:TPU:6 now
where the time goes in v4:
time: 142 us; the launch traced here: 140 us
  Pallas kernels  68.8 us (48%)
  starting transfers between devices  37.7 us (27%)
  waiting for transfers between devices  16.8 us (12%)
  other arithmetic  6.7 us (5%)
  local copies, waits for them, and re-layouts  5.74 us (4%)
  matrix products  3.72 us (3%)
    ppermute x17, starting transfers between devices, shift(): return lax.ppermute(value, AXES, pairs)  33.4 us
    pallas_call x1, Pallas kernels, third_step(): pl.pallas_call(repack_kernel, out_shape=[jax.ShapeDtypeStruct((n, *block)...  32.9 us
    pallas_call x1, Pallas kernels, correlations(): pl.pallas_call(far_kernel, out_shape=jax.ShapeDtypeStruct((16, 2, 4, 8, L...  20.7 us
    pallas_call x1, Pallas kernels, near_totals(): pl.pallas_call(near_kernel, out_shape=(OWN, jax.ShapeDtypeStruct((3, *TOT...  15.2 us
    ppermute x17, waiting for transfers between devices, shift(): return lax.ppermute(value, AXES, pairs)  14.8 us
    unnamed x34, local copies, waits for them, and re-layouts  4.88 us
    ppermute x3, starting transfers between devices, own_only(): return lax.ppermute(value, 'win', [(i, (i + k) % 4) for i in range(4)])  4.36 us
    dot_general x4, matrix products, product(): return jnp.dot(left, table, preferred_element_type=jnp.float32)  2.94 us
  transfers between devices with their start and end apart: 20, of which 4 were waited for; matrix products, arithmetic and copies ran while one was open for 3% of the time, Pallas kernels for 11%

profile of v4, /device:TPU:6, one launch (start us, length us, event | category | flops | bytes accessed | tf_op | source)
XLA Modules:
  0.0 140.0 jit_solution(15044531699555730400)
XLA Ops:
  0.0 1.8 %convert_reduce_fusion = f32[8,8]{1,0:T(8,128)S(1)} fusion(bf16[8,8,12000]{2,1,0:T(8,128)(2,1)} %param.12), kind=kLoop, calls=%fused_computation | loop fusion | flops 1535936 | bytes 1536256 | tf_op jit(solution)/shard_map/reduce_sum | solution.py:83
  1.9 0.1 div.68
  1.9 1.9 %fusion.3 = f32[64,12000]{1,0:T(8,128)S(1)} fusion(bf16[8,8,12000]{2,1,0:T(8,128)(2,1)} %param.12, f32[12000]{0:T(1024)} %constant.173, f32[64]{0:T(128)S(1)} %div.68), kind=kLoop, calls=%fused_computation.5 | loop fusion | flops 3840000 | bytes 4656256 | tf_op jit(solution)/shard_map/convert_element_type | solution.py:84
  3.8 0.0 copy-start.8
  3.8 0.9 fusion.7
  4.7 0.0 copy-done.15
  4.7 0.0 copy-start.7
  4.7 0.9 fusion.6
  5.6 0.1 copy-done.8
  5.7 0.6 fusion.8
  6.3 0.5 copy-done.7
  6.9 0.0 copy-start.14
  6.9 0.6 convolution_add_fusion.1
  7.5 0.6 copy-done.9
  8.1 0.8 fusion.14
  8.9 0.0 copy-start.12
  8.9 0.1 fusion.9
  9.0 3.1 %collective-permute-start.6 = (bf16[8,8,1024]{2,1,0:T(8,128)(2,1)S(1)}, bf16[8,8,1024]{2,1,0:T(8,128)(2,1)S(1)}, u32[]{:S(2)}, u32[]{:S(2)}) collective-permute-start(bf16[8,8,1024]{2,1,0:T(8,128)(2,1)S(1)} %fusion.9), channel_id=1, source_target_pairs={{0,6},{1,7},{64,70},{65,71},{128,134},{129,135},{192,198},{193,199... | collective-permute-start | bytes 393224 | tf_op jit(solution)/shard_map/ppermute | solution.py:131
  12.1 0.6 collective-permute-start.5
  12.7 1.0 collective-permute-start.4
  13.7 5.9 %collective-permute-start.3 = (bf16[8,8,1024]{2,1,0:T(8,128)(2,1)S(1)}, bf16[8,8,1024]{2,1,0:T(8,128)(2,1)S(1)}, u32[]{:S(2)}, u32[]{:S(2)}) collective-permute-start(bf16[8,8,1024]{2,1,0:T(8,128)(2,1)S(1)} %get-tuple-element.62), channel_id=1, source_target_pairs={{0,224},{1,225},{64,0},{65,1},{128,64},{129,65},{192,128},{193,129... | collective-permute-start | bytes 393224 | tf_op jit(solution)/shard_map/ppermute | solution.py:131
  19.7 0.0 collective-permute-start.2
  19.7 0.0 collective-permute-done.6
  19.7 1.4 %collective-permute-start.1 = (bf16[8,8,1024]{2,1,0:T(8,128)(2,1)S(1)}, bf16[8,8,1024]{2,1,0:T(8,128)(2,1)S(1)}, u32[]{:S(2)}, u32[]{:S(2)}) collective-permute-start(bf16[8,8,1024]{2,1,0:T(8,128)(2,1)S(1)} %get-tuple-element.62), channel_id=1, source_target_pairs={{0,16},{1,17},{64,80},{65,81},{128,144},{129,145},{192,208},{193,2... | collective-permute-start | bytes 393224 | tf_op jit(solution)/shard_map/ppermute | solution.py:131
  21.1 0.0 collective-permute-done.5
  21.1 6.1 %collective-permute-start = (bf16[8,8,1024]{2,1,0:T(8,128)(2,1)S(1)}, bf16[8,8,1024]{2,1,0:T(8,128)(2,1)S(1)}, u32[]{:S(2)}, u32[]{:S(2)}) collective-permute-start(bf16[8,8,1024]{2,1,0:T(8,128)(2,1)S(1)} %get-tuple-element.62), channel_id=1, source_target_pairs={{0,32},{1,33},{64,96},{65,97},{128,160},{129,161},{192,224},{193,2... | collective-permute-start | bytes 393224 | tf_op jit(solution)/shard_map/ppermute | solution.py:131
  27.2 0.0 collective-permute-done.4
  27.2 0.0 collective-permute-done.3
  27.2 4.2 %collective-permute-done.2 = bf16[8,8,1024]{2,1,0:T(8,128)(2,1)S(1)} collective-permute-done((bf16[8,8,1024]{2,1,0:T(8,128)(2,1)S(1)}, bf16[8,8,1024]{2,1,0:T(8,128)(2,1)S(1)}, u32[]{:S(2)}, u32[]{:S(2)}) %collective-permute-start.2) | collective-permute-done | bytes 131104 | tf_op jit(solution)/shard_map/ppermute | solution.py:131
  31.4 0.0 collective-permute-done.1.across
  31.5 0.0 collective-permute-done
  31.5 0.1 select_bitcast_fusion
  31.6 3.2 %collective-permute-start.9 = (bf16[8,8,1024]{2,1,0:T(8,128)(2,1)S(1)}, bf16[8,8,1024]{2,1,0:T(8,128)(2,1)S(1)}, u32[]{:S(2)}, u32[]{:S(2)}) collective-permute-start(bf16[8,8,1024]{2,1,0:T(8,128)(2,1)S(1)} %get-tuple-element.56), channel_id=1, source_target_pairs={{0,192},{64,0},{128,64},{192,128},{1,193},{65,1},{129,65},{193,129... | collective-permute-start | bytes 393224 | tf_op jit(solution)/shard_map/ppermute | solution.py:135
  34.8 1.2 collective-permute-start.7
  35.9 0.6 and_select_fusion.2
  36.5 1.7 %collective-permute-start.15 = (bf16[8,8,1024]{2,1,0:T(8,128)(2,1)S(1)}, bf16[8,8,1024]{2,1,0:T(8,128)(2,1)S(1)}, u32[]{:S(2)}, u32[]{:S(2)}) collective-permute-start(bf16[8,8,1024]{2,1,0:T(8,128)(2,1)S(1)} %collective-permute-done), channel_id=1, source_target_pairs={{0,16},{1,17},{64,80},{65,81},{128,144},{129,145},{192,208},{193,2... | collective-permute-start | bytes 393224 | tf_op jit(solution)/shard_map/ppermute | solution.py:131
  38.2 0.1 pad_maximum_fusion.1.near
  38.3 1.1 collective-permute-start.12
  39.4 2.4 %collective-permute-start.11 = (bf16[4,8,8,1024]{3,2,1,0:T(8,128)(2,1)S(1)}, bf16[4,8,8,1024]{3,2,1,0:T(8,128)(2,1)}, u32[]{:S(2)}, u32[]{:S(2)}) collective-permute-start(bf16[4,8,8,1024]{3,2,1,0:T(8,128)(2,1)S(1)} %pad_maximum_fusion.1.near), channel_id=1, source_target_pairs={{0,8},{1,9},{64,72},{65,73},{128,136},{129,137},{192,200},{193,201... | collective-permute-start | bytes 1572872 | tf_op jit(solution)/shard_map/ppermute | solution.py:131
  41.8 2.0 %collective-permute-done.8 = bf16[8,8,1024]{2,1,0:T(8,128)(2,1)S(1)} collective-permute-done((bf16[8,8,1024]{2,1,0:T(8,128)(2,1)S(1)}, bf16[8,8,1024]{2,1,0:T(8,128)(2,1)S(1)}, u32[]{:S(2)}, u32[]{:S(2)}) %collective-permute-start.8) | collective-permute-done | bytes 131104 | tf_op jit(solution)/shard_map/ppermute | solution.py:135
  43.8 0.0 collective-permute-done.7
  43.8 0.1 pad_maximum_fusion.mine
  43.9 0.1 collective-permute-start.10
  44.0 0.8 pad_maximum_fusion.2
  44.8 3.4 %collective-permute-start.14 = (bf16[3,8,8,1024]{3,2,1,0:T(8,128)(2,1)}, bf16[3,8,8,1024]{3,2,1,0:T(8,128)(2,1)S(1)}, u32[]{:S(2)}, u32[]{:S(2)}) collective-permute-start(bf16[3,8,8,1024]{3,2,1,0:T(8,128)(2,1)} %get-tuple-element.59), channel_id=1, source_target_pairs={{0,224},{1,225},{64,0},{65,1},{128,64},{129,65},{192,128},{193,129... | collective-permute-start | bytes 1179656 | tf_op jit(solution)/shard_map/ppermute | solution.py:131
  48.3 0.6 and_select_fusion.5
  48.9 0.6 and_select_fusion
  49.5 0.8 concatenate.16.place
  50.2 7.4 %collective-permute-done.14.down = bf16[3,8,8,1024]{3,2,1,0:T(8,128)(2,1)S(1)} collective-permute-done((bf16[3,8,8,1024]{3,2,1,0:T(8,128)(2,1)}, bf16[3,8,8,1024]{3,2,1,0:T(8,128)(2,1)S(1)}, u32[]{:S(2)}, u32[]{:S(2)}) %collective-permute-start.14) | collective-permute-done | bytes 393248 | tf_op jit(solution)/shard_map/ppermute | solution.py:131
  57.6 3.1 %collective-permute-done.13.up = bf16[3,8,8,1024]{3,2,1,0:T(8,128)(2,1)S(1)} collective-permute-done((bf16[3,8,8,1024]{3,2,1,0:T(8,128)(2,1)S(1)}, bf16[3,8,8,1024]{3,2,1,0:T(8,128)(2,1)S(1)}, u32[]{:S(2)}, u32[]{:S(2)}) %collective-permute-start.13) | collective-permute-done | bytes 393248 | tf_op jit(solution)/shard_map/ppermute | solution.py:131
  60.7 0.0 collective-permute-done.10.other
  60.8 0.7 copy-done.2
  61.5 32.9 %shard_map.118 = (bf16[4,8,8,1024]{3,2,1,0:T(8,128)(2,1)}, bf16[2,8,8,1024]{3,2,1,0:T(8,128)(2,1)}, bf16[2,8,8,1024]{3,2,1,0:T(8,128)(2,1)}) custom-call(bf16[3,8,8,1024]{3,2,1,0:T(8,128)(2,1)} %copy-done.2, bf16[3,8,8,1024]{3,2,1,0:T(8,128)(2,1)} %copy-done, bf16[8,8,1024]{2,1,0:T(8,128)(2,1)} %copy-done.4), custom_call_target="tpu_custom_call" | custom-call | tf_op jit(solution)/shard_map/pallas_call | solution.py:198
  94.4 0.1 collective-permute-start.17
  94.5 3.2 %collective-permute-start.16 = (bf16[4,8,8,1024]{3,2,1,0:T(8,128)(2,1)}, bf16[4,8,8,1024]{3,2,1,0:T(8,128)(2,1)S(1)}, u32[]{:S(2)}, u32[]{:S(2)}) collective-permute-start(bf16[4,8,8,1024]{3,2,1,0:T(8,128)(2,1)} %get-tuple-element.38), channel_id=1, source_target_pairs={{0,8},{1,9},{64,72},{65,73},{128,136},{129,137},{192,200},{193,201... | collective-permute-start | bytes 1572872 | tf_op jit(solution)/shard_map/ppermute | solution.py:131
  97.7 3.2 %collective-permute-start.19 = (bf16[2,8,8,1024]{3,2,1,0:T(8,128)(2,1)}, bf16[2,8,8,1024]{3,2,1,0:T(8,128)(2,1)S(1)}, u32[]{:S(2)}, u32[]{:S(2)}) collective-permute-start(bf16[2,8,8,1024]{3,2,1,0:T(8,128)(2,1)} %get-tuple-element.40), channel_id=1, source_target_pairs={{0,224},{1,225},{64,0},{65,1},{128,64},{129,65},{192,128},{193,129... | collective-permute-start | bytes 786440 | tf_op jit(solution)/shard_map/ppermute | solution.py:131
  101.0 1.0 copy-done.1
  102.0 1.0 copy-done.3
  103.0 0.9 copy-done.5
  103.9 15.2 %shard_map.119 = (bf16[256,1024]{1,0:T(8,128)(2,1)S(1)}, f32[3,2,16,8,1024]{4,3,2,1,0:T(8,128)S(1)}) custom-call(s32[25]{0:T(128)S(1)} %concatenate.16.place, bf16[4,8,8,1024]{3,2,1,0:T(8,128)(2,1)S(1)} %pad_maximum_fusion.1.near, bf16[3,8,8,1024]{3,2,1,0:T(8,128)(2,1)S(1)} %copy-done.3, bf16[3,8,8,1024]{3,2,1,0:T(8,128)(2,1)S(1)} %copy-done.1, ...), custom_call_target="tpu_custom_call" | custom-call | flops 12000000000 | bytes 8388608 | tf_op jit(solution)/shard_map/pallas_call | solution.py:303
  119.1 0.0 collective-permute-done.18.up
  119.1 0.0 collective-permute-done.17.right
  119.1 0.0 collective-permute-done.16.left
  119.1 20.7 %shard_map.120 = bf16[16,2,4,8,4000]{4,3,2,1,0:T(8,128)(2,1)} custom-call(s32[25]{0:T(128)S(1)} %concatenate.16.place, bf16[4,8,8,1024]{3,2,1,0:T(8,128)(2,1)S(1)} %collective-permute-done.16.left, bf16[4,8,8,1024]{3,2,1,0:T(8,128)(2,1)S(1)} %collective-permute-done.17.right, bf16[2,8,8,1024]{3,2,1,0:T(8,128)(2,1)S(1)} %collective-permute-done.18.up, ...), custom_call_target="tpu_custom_call" | custom-call | flops 8388608000 | bytes 25165824 | tf_op jit(solution)/shard_map/pallas_call | solution.py:361
  (35 shorter events, 0.1 us)
Async XLA Ops:
  0.0 3.8 %copy-start.16 = (bf16[3000,256]{1,0:T(8,128)(2,1)S(1)}, bf16[3000,256]{1,0:T(8,128)(2,1)}, u32[]{:S(2)}) copy-start(bf16[3000,256]{1,0:T(8,128)(2,1)} %constant.164.clone) | copy-start | bytes 4608004
  1.9 2.8 %copy-start.15 = (bf16[3000,256]{1,0:T(8,128)(2,1)S(1)}, bf16[3000,256]{1,0:T(8,128)(2,1)}, u32[]{:S(2)}) copy-start(bf16[3000,256]{1,0:T(8,128)(2,1)} %constant.163.clone) | copy-start | bytes 4608004
  3.8 1.9 %copy-start.8 = (bf16[3000,512]{1,0:T(8,128)(2,1)S(1)}, bf16[3000,512]{1,0:T(8,128)(2,1)}, u32[]{:S(2)}) copy-start(bf16[3000,512]{1,0:T(8,128)(2,1)} %constant.174) | copy-start | bytes 9216004
  4.7 2.1 %copy-start.7 = (bf16[3000,512]{1,0:T(8,128)(2,1)S(1)}, bf16[3000,512]{1,0:T(8,128)(2,1)}, u32[]{:S(2)}) copy-start(bf16[3000,512]{1,0:T(8,128)(2,1)} %constant.175) | copy-start | bytes 9216004
  6.9 1.2 copy-start.9
  6.9 1.2 copy-start.11
  6.9 2.0 %copy-start.10 = (f32[8]{0:T(128)S(1)}, f32[8]{0:T(128)}, u32[]{:S(2)}) copy-start(f32[8]{0:T(128)} %param.13) | copy-start | bytes 100
  6.9 20.3 %copy-start.13 = (s32[4]{0:T(128)S(1)}, s32[4]{0:T(128)}, u32[]{:S(2)}) copy-start(s32[4]{0:T(128)} %constant.169.clone) | copy-start | bytes 52
  6.9 20.3 %copy-start.14 = (s32[4]{0:T(128)S(1)}, s32[4]{0:T(128)}, u32[]{:S(2)}) copy-start(s32[4]{0:T(128)} %constant.168.clone) | copy-start | bytes 52
  8.9 40.0 %copy-start.12 = (s32[4]{0:T(128)S(1)}, s32[4]{0:T(128)}, u32[]{:S(2)}) copy-start(s32[4]{0:T(128)} %constant.170.clone) | copy-start | bytes 52
  9.0 10.7 %collective-permute-start.6 = (bf16[8,8,1024]{2,1,0:T(8,128)(2,1)S(1)}, bf16[8,8,1024]{2,1,0:T(8,128)(2,1)S(1)}, u32[]{:S(2)}, u32[]{:S(2)}) collective-permute-start(bf16[8,8,1024]{2,1,0:T(8,128)(2,1)S(1)} %fusion.9), channel_id=1, source_target_pairs={{0,6},{1,7},{64,70},{65,71},{128,134},{129,135},{192,198},{193,199... | collective-permute-start | bytes 393224 | tf_op jit(solution)/shard_map/ppermute | solution.py:131
  12.1 9.0 %collective-permute-start.5 = (bf16[8,8,1024]{2,1,0:T(8,128)(2,1)S(1)}, bf16[8,8,1024]{2,1,0:T(8,128)(2,1)S(1)}, u32[]{:S(2)}, u32[]{:S(2)}) collective-permute-start(bf16[8,8,1024]{2,1,0:T(8,128)(2,1)S(1)} %fusion.9), channel_id=1, source_target_pairs={{0,4},{1,5},{64,68},{65,69},{128,132},{129,133},{192,196},{193,197... | collective-permute-start | bytes 393224 | tf_op jit(solution)/shard_map/ppermute | solution.py:131
  12.7 14.5 %collective-permute-start.4 = (bf16[8,8,1024]{2,1,0:T(8,128)(2,1)S(1)}, bf16[8,8,1024]{2,1,0:T(8,128)(2,1)S(1)}, u32[]{:S(2)}, u32[]{:S(2)}) collective-permute-start(bf16[8,8,1024]{2,1,0:T(8,128)(2,1)S(1)} %fusion.9), channel_id=1, source_target_pairs={{0,2},{1,3},{64,66},{65,67},{128,130},{129,131},{192,194},{193,195... | collective-permute-start | bytes 393224 | tf_op jit(solution)/shard_map/ppermute | solution.py:131
  13.7 13.5 %collective-permute-start.3 = (bf16[8,8,1024]{2,1,0:T(8,128)(2,1)S(1)}, bf16[8,8,1024]{2,1,0:T(8,128)(2,1)S(1)}, u32[]{:S(2)}, u32[]{:S(2)}) collective-permute-start(bf16[8,8,1024]{2,1,0:T(8,128)(2,1)S(1)} %get-tuple-element.62), channel_id=1, source_target_pairs={{0,224},{1,225},{64,0},{65,1},{128,64},{129,65},{192,128},{193,129... | collective-permute-start | bytes 393224 | tf_op jit(solution)/shard_map/ppermute | solution.py:131
  19.7 11.8 %collective-permute-start.2 = (bf16[8,8,1024]{2,1,0:T(8,128)(2,1)S(1)}, bf16[8,8,1024]{2,1,0:T(8,128)(2,1)S(1)}, u32[]{:S(2)}, u32[]{:S(2)}) collective-permute-start(bf16[8,8,1024]{2,1,0:T(8,128)(2,1)S(1)} %get-tuple-element.62), channel_id=1, source_target_pairs={{0,64},{1,65},{64,128},{65,129},{128,192},{129,193},{192,32},{193,... | collective-permute-start | bytes 393224 | tf_op jit(solution)/shard_map/ppermute | solution.py:131
  19.7 11.8 %collective-permute-start.1 = (bf16[8,8,1024]{2,1,0:T(8,128)(2,1)S(1)}, bf16[8,8,1024]{2,1,0:T(8,128)(2,1)S(1)}, u32[]{:S(2)}, u32[]{:S(2)}) collective-permute-start(bf16[8,8,1024]{2,1,0:T(8,128)(2,1)S(1)} %get-tuple-element.62), channel_id=1, source_target_pairs={{0,16},{1,17},{64,80},{65,81},{128,144},{129,145},{192,208},{193,2... | collective-permute-start | bytes 393224 | tf_op jit(solution)/shard_map/ppermute | solution.py:131
  21.1 10.4 %collective-permute-start = (bf16[8,8,1024]{2,1,0:T(8,128)(2,1)S(1)}, bf16[8,8,1024]{2,1,0:T(8,128)(2,1)S(1)}, u32[]{:S(2)}, u32[]{:S(2)}) collective-permute-start(bf16[8,8,1024]{2,1,0:T(8,128)(2,1)S(1)} %get-tuple-element.62), channel_id=1, source_target_pairs={{0,32},{1,33},{64,96},{65,97},{128,160},{129,161},{192,224},{193,2... | collective-permute-start | bytes 393224 | tf_op jit(solution)/shard_map/ppermute | solution.py:131
  31.6 7.8 %collective-permute-start.9 = (bf16[8,8,1024]{2,1,0:T(8,128)(2,1)S(1)}, bf16[8,8,1024]{2,1,0:T(8,128)(2,1)S(1)}, u32[]{:S(2)}, u32[]{:S(2)}) collective-permute-start(bf16[8,8,1024]{2,1,0:T(8,128)(2,1)S(1)} %get-tuple-element.56), channel_id=1, source_target_pairs={{0,192},{64,0},{128,64},{192,128},{1,193},{65,1},{129,65},{193,129... | collective-permute-start | bytes 393224 | tf_op jit(solution)/shard_map/ppermute | solution.py:135
  34.8 9.1 %collective-permute-start.8 = (bf16[8,8,1024]{2,1,0:T(8,128)(2,1)S(1)}, bf16[8,8,1024]{2,1,0:T(8,128)(2,1)S(1)}, u32[]{:S(2)}, u32[]{:S(2)}) collective-permute-start(bf16[8,8,1024]{2,1,0:T(8,128)(2,1)S(1)} %get-tuple-element.57), channel_id=1, source_target_pairs={{0,128},{64,192},{128,0},{192,64},{1,129},{65,193},{129,1},{193,65... | collective-permute-start | bytes 393224 | tf_op jit(solution)/shard_map/ppermute | solution.py:135
  34.8 9.1 %collective-permute-start.7 = (bf16[8,8,1024]{2,1,0:T(8,128)(2,1)S(1)}, bf16[8,8,1024]{2,1,0:T(8,128)(2,1)S(1)}, u32[]{:S(2)}, u32[]{:S(2)}) collective-permute-start(bf16[8,8,1024]{2,1,0:T(8,128)(2,1)S(1)} %get-tuple-element.58), channel_id=1, source_target_pairs={{0,64},{64,128},{128,192},{192,0},{1,65},{65,129},{129,193},{193,1... | collective-permute-start | bytes 393224 | tf_op jit(solution)/shard_map/ppermute | solution.py:135
  36.5 11.7 %collective-permute-start.15 = (bf16[8,8,1024]{2,1,0:T(8,128)(2,1)S(1)}, bf16[8,8,1024]{2,1,0:T(8,128)(2,1)S(1)}, u32[]{:S(2)}, u32[]{:S(2)}) collective-permute-start(bf16[8,8,1024]{2,1,0:T(8,128)(2,1)S(1)} %collective-permute-done), channel_id=1, source_target_pairs={{0,16},{1,17},{64,80},{65,81},{128,144},{129,145},{192,208},{193,2... | collective-permute-start | bytes 393224 | tf_op jit(solution)/shard_map/ppermute | solution.py:131
  38.3 22.4 %collective-permute-start.12 = (bf16[4,8,8,1024]{3,2,1,0:T(8,128)(2,1)S(1)}, bf16[4,8,8,1024]{3,2,1,0:T(8,128)(2,1)S(1)}, u32[]{:S(2)}, u32[]{:S(2)}) collective-permute-start(bf16[4,8,8,1024]{3,2,1,0:T(8,128)(2,1)S(1)} %pad_maximum_fusion.1.near), channel_id=1, source_target_pairs={{0,24},{1,25},{64,88},{65,89},{128,152},{129,153},{192,216},{193,2... | collective-permute-start | bytes 1572872 | tf_op jit(solution)/shard_map/ppermute | solution.py:131
  39.4 21.3 %collective-permute-start.11 = (bf16[4,8,8,1024]{3,2,1,0:T(8,128)(2,1)S(1)}, bf16[4,8,8,1024]{3,2,1,0:T(8,128)(2,1)}, u32[]{:S(2)}, u32[]{:S(2)}) collective-permute-start(bf16[4,8,8,1024]{3,2,1,0:T(8,128)(2,1)S(1)} %pad_maximum_fusion.1.near), channel_id=1, source_target_pairs={{0,8},{1,9},{64,72},{65,73},{128,136},{129,137},{192,200},{193,201... | collective-permute-start | bytes 1572872 | tf_op jit(solution)/shard_map/ppermute | solution.py:131
  43.9 16.8 %collective-permute-start.10 = (bf16[4,8,8,1024]{3,2,1,0:T(8,128)(2,1)S(1)}, bf16[4,8,8,1024]{3,2,1,0:T(8,128)(2,1)S(1)}, u32[]{:S(2)}, u32[]{:S(2)}) collective-permute-start(bf16[4,8,8,1024]{3,2,1,0:T(8,128)(2,1)S(1)} %pad_maximum_fusion.mine), channel_id=1, source_target_pairs={{0,1},{1,0},{64,65},{65,64},{128,129},{129,128},{192,193},{193,192... | collective-permute-start | bytes 1572872 | tf_op jit(solution)/shard_map/ppermute | solution.py:131
  44.8 12.8 %collective-permute-start.14 = (bf16[3,8,8,1024]{3,2,1,0:T(8,128)(2,1)}, bf16[3,8,8,1024]{3,2,1,0:T(8,128)(2,1)S(1)}, u32[]{:S(2)}, u32[]{:S(2)}) collective-permute-start(bf16[3,8,8,1024]{3,2,1,0:T(8,128)(2,1)} %get-tuple-element.59), channel_id=1, source_target_pairs={{0,224},{1,225},{64,0},{65,1},{128,64},{129,65},{192,128},{193,129... | collective-permute-start | bytes 1179656 | tf_op jit(solution)/shard_map/ppermute | solution.py:131
  48.3 12.5 %copy-start.4 = (bf16[8,8,1024]{2,1,0:T(8,128)(2,1)}, bf16[8,8,1024]{2,1,0:T(8,128)(2,1)S(1)}, u32[]{:S(2)}) copy-start(bf16[8,8,1024]{2,1,0:T(8,128)(2,1)S(1)} %collective-permute-done.15.across_opposite) | copy-start | bytes 393220
  48.3 12.4 %collective-permute-start.13 = (bf16[3,8,8,1024]{3,2,1,0:T(8,128)(2,1)S(1)}, bf16[3,8,8,1024]{3,2,1,0:T(8,128)(2,1)S(1)}, u32[]{:S(2)}, u32[]{:S(2)}) collective-permute-start(bf16[3,8,8,1024]{3,2,1,0:T(8,128)(2,1)S(1)} %get-tuple-element.60), channel_id=1, source_target_pairs={{0,64},{1,65},{64,128},{65,129},{128,192},{129,193},{192,32},{193,... | collective-permute-start | bytes 1179656 | tf_op jit(solution)/shard_map/ppermute | solution.py:131
  57.6 3.1 %copy-start = (bf16[3,8,8,1024]{3,2,1,0:T(8,128)(2,1)}, bf16[3,8,8,1024]{3,2,1,0:T(8,128)(2,1)S(1)}, u32[]{:S(2)}) copy-start(bf16[3,8,8,1024]{3,2,1,0:T(8,128)(2,1)S(1)} %collective-permute-done.14.down) | copy-start | bytes 1179652
  60.7 0.8 copy-start.2
  94.4 24.7 %collective-permute-start.17 = (bf16[4,8,8,1024]{3,2,1,0:T(8,128)(2,1)}, bf16[4,8,8,1024]{3,2,1,0:T(8,128)(2,1)S(1)}, u32[]{:S(2)}, u32[]{:S(2)}) collective-permute-start(bf16[4,8,8,1024]{3,2,1,0:T(8,128)(2,1)} %get-tuple-element.38), channel_id=1, source_target_pairs={{0,24},{1,25},{64,88},{65,89},{128,152},{129,153},{192,216},{193,2... | collective-permute-start | bytes 1572872 | tf_op jit(solution)/shard_map/ppermute | solution.py:131
  94.5 24.6 %collective-permute-start.16 = (bf16[4,8,8,1024]{3,2,1,0:T(8,128)(2,1)}, bf16[4,8,8,1024]{3,2,1,0:T(8,128)(2,1)S(1)}, u32[]{:S(2)}, u32[]{:S(2)}) collective-permute-start(bf16[4,8,8,1024]{3,2,1,0:T(8,128)(2,1)} %get-tuple-element.38), channel_id=1, source_target_pairs={{0,8},{1,9},{64,72},{65,73},{128,136},{129,137},{192,200},{193,201... | collective-permute-start | bytes 1572872 | tf_op jit(solution)/shard_map/ppermute | solution.py:131
  97.7 21.3 %collective-permute-start.18 = (bf16[2,8,8,1024]{3,2,1,0:T(8,128)(2,1)}, bf16[2,8,8,1024]{3,2,1,0:T(8,128)(2,1)S(1)}, u32[]{:S(2)}, u32[]{:S(2)}) collective-permute-start(bf16[2,8,8,1024]{3,2,1,0:T(8,128)(2,1)} %get-tuple-element.39), channel_id=1, source_target_pairs={{0,64},{1,65},{64,128},{65,129},{128,192},{129,193},{192,32},{193,... | collective-permute-start | bytes 786440 | tf_op jit(solution)/shard_map/ppermute | solution.py:131
  97.7 21.3 %collective-permute-start.19 = (bf16[2,8,8,1024]{3,2,1,0:T(8,128)(2,1)}, bf16[2,8,8,1024]{3,2,1,0:T(8,128)(2,1)S(1)}, u32[]{:S(2)}, u32[]{:S(2)}) collective-permute-start(bf16[2,8,8,1024]{3,2,1,0:T(8,128)(2,1)} %get-tuple-element.40), channel_id=1, source_target_pairs={{0,224},{1,225},{64,0},{65,1},{128,64},{129,65},{192,128},{193,129... | collective-permute-start | bytes 786440 | tf_op jit(solution)/shard_map/ppermute | solution.py:131
  101.0 1.0 copy-start.1
  102.0 1.0 copy-start.3
  103.0 0.9 copy-start.5
  103.9 15.2 %copy-start.6 = (bf16[1024,4096]{1,0:T(8,128)(2,1)S(1)}, bf16[1024,4096]{1,0:T(8,128)(2,1)}, u32[]{:S(2)}) copy-start(bf16[1024,4096]{1,0:T(8,128)(2,1)} %constant.171.clone.source) | copy-start | bytes 25165828

commit v5 on v4

--- a/solution.py
+++ b/solution.py
@@ -141,10 +141,9 @@
 
 def first_step(plain, weighted):
     return together(
-        shift(plain, dz=4),
+        shift(plain, dz=-3),
+        shift(plain, dz=2),
         shift(plain, dx=2),
-        shift(plain, dz=1),
-        shift(plain, dz=-1),
         shift(weighted, dy=1),
         shift(weighted, dy=2),
         shift(weighted, dy=3),
@@ -152,8 +151,8 @@
 
 
 def second_step(plain, weighted, arrived, y, z_low):
-    opposite, across, below, above, *sides = arrived
-    near = jnp.stack([plain, below, above, opposite])
+    ahead, behind, across, *sides = arrived
+    near = jnp.stack([plain, ahead, behind])
     held = [weighted, *sides]
 
     def for_offset(k):
@@ -168,51 +167,25 @@
         shift(mine, dcore=1),
         shift(near, dx=1),
         shift(near, dx=-1),
-        shift(jnp.stack([below, opposite, across]), dz=1),
-        shift(jnp.stack([above, opposite, across]), dz=-1),
-        shift(opposite, dx=2),
-    )
-
-
-def repack_kernel(up, down, across_opposite, far, up_out, down_out, done):
-    pairs = (
-        (up.at[0:2], far.at[0:2]),
-        (down.at[0:2], far.at[2:4]),
-        (up.at[2], up_out.at[0]),
-        (across_opposite, up_out.at[1]),
-        (down.at[2], down_out.at[0]),
-        (across_opposite, down_out.at[1]),
-    )
-    copies = [
-        pltpu.make_async_copy(source, target, done.at[n])
-        for n, (source, target) in enumerate(pairs)
-    ]
-    for copy in copies:
-        copy.start()
-    for copy in copies:
-        copy.wait()
-
-
-def third_step(up, down, across_opposite):
-    block = up.shape[1:]
-    far, up_out, down_out = pl.pallas_call(
-        repack_kernel,
-        out_shape=[jax.ShapeDtypeStruct((n, *block), jnp.bfloat16) for n in (4, 2, 2)],
-        in_specs=[pl.BlockSpec(memory_space=pl.ANY)] * 3,
-        out_specs=[pl.BlockSpec(memory_space=pl.ANY)] * 3,
-        scratch_shapes=[pltpu.SemaphoreType.DMA((6,))],
-    )(up, down, across_opposite)
+        shift(near, dz=1),
+        shift(jnp.stack([plain, ahead]), dz=-1),
+        shift(jnp.stack([ahead, behind]), dx=2),
+    )
+
+
+def third_step(up, down, across, across_near):
+    far = jnp.concatenate([up, down])
     return together(
         shift(far, dx=1),
         shift(far, dx=-1),
-        shift(up_out, dz=1),
-        shift(down_out, dz=-1),
-    )
-
-
-NEAR = (0, -1, 1, 4)
-FAR = (-2, 3, 2, -3)
-XS, HIGH_NEAR, GROUP_NEAR, HIGH_FAR, GROUP_FAR, ROWS, CORE = 0, 4, 8, 12, 16, 20, 24
+        shift(jnp.concatenate([across[None], across_near]), dz=1),
+        shift(jnp.stack([across, across_near[0]]), dz=-1),
+    )
+
+
+NEAR = (0, 3, -2)
+FAR = (-1, 2, -3, 1, 4)
+XS, HIGH, GROUP, ROWS, CORE = 0, 4, 12, 20, 24
 
 
 def load_rows(place, mine, other, z_re, z_im, z_sum):
@@ -257,10 +230,10 @@
             total[high, core * 8 + base + i, :, lane_im] += r - p + q
 
 
-def add_blocks(blocks, place, high_at, group_at, rows, total):
+def add_blocks(blocks, place, first, rows, total):
     def tile_step(tile, carry):
-        for n, block in enumerate(blocks):
-            add_cross(tile, block, place[high_at + n], place[group_at + n], rows, total)
+        for n, block in enumerate(blocks, first):
+            add_cross(tile, block, place[HIGH + n], place[GROUP + n], rows, total)
         return carry
 
     lax.fori_loop(0, 4, tile_step, 0)
@@ -272,41 +245,48 @@
         target[pl.ds(i * 16, 16), :] = rows.astype(jnp.bfloat16)
 
 
+def parts_of(*refs):
+    return [ref.at[n] for ref in refs for n in range(ref.shape[0])]
+
+
 def near_kernel(
-    place, near, up, down, left, right, across, across_opposite, mine, other, own, total, z_re, z_im, z_sum, sums
+    place, near, up, down, left, right, across, across_near, mine, other, own, total, z_re, z_im, z_sum, sums
 ):
     rows = (z_re, z_im, z_sum)
     load_rows(place, mine, other, *rows)
     sums[...] = jnp.zeros_like(sums)
     total[...] = jnp.zeros_like(total)
-    add_blocks([near.at[n] for n in range(4)], place, HIGH_NEAR, GROUP_NEAR, rows, sums)
-    far = [up.at[0], up.at[1], down.at[0], down.at[1]]
-    add_blocks(far, place, HIGH_FAR, GROUP_FAR, rows, sums)
+    add_blocks(parts_of(near, up, down), place, 0, rows, sums)
     settle(sums, own)
-    sides = (
-        [left.at[n] for n in range(4)],
-        [right.at[n] for n in range(4)],
-        [across, up.at[2], down.at[2], across_opposite],
-    )
+    sides = (parts_of(left), parts_of(right), [across, *parts_of(across_near)])
     for n, blocks in enumerate(sides):
-        add_blocks(blocks, place, HIGH_NEAR, GROUP_NEAR, rows, total.at[n])
-
-
-WHOLE = pl.BlockSpec(memory_space=pltpu.VMEM)
-SCALARS = pl.BlockSpec(memory_space=pltpu.SMEM)
+        add_blocks(blocks, place, 0, rows, total.at[n])
+
+
 TOTAL = (2, 16, 8, 2 * BINS)
-OWN = jax.ShapeDtypeStruct((256, 2 * BINS), jnp.bfloat16)
+OWN = (256, 2 * BINS)
 ROW_SCRATCH = [pltpu.VMEM((32, 2, 4, 8, 128), jnp.float32)] * 3
+
+
+def whole(shape):
+    return pl.BlockSpec(shape, lambda j, place: (0,) * len(shape))
 
 
 def near_totals(place, *blocks):
     return pl.pallas_call(
         near_kernel,
-        out_shape=(OWN, jax.ShapeDtypeStruct((3, *TOTAL), jnp.float32)),
-        in_specs=[SCALARS] + [WHOLE] * len(blocks),
-        out_specs=(WHOLE, WHOLE),
-        scratch_shapes=[*ROW_SCRATCH, pltpu.VMEM(TOTAL, jnp.float32)],
-        compiler_params=pltpu.CompilerParams(vmem_limit_bytes=24 * 1024 * 1024),
+        out_shape=(
+            jax.ShapeDtypeStruct(OWN, jnp.bfloat16),
+            jax.ShapeDtypeStruct((3, *TOTAL), jnp.float32),
+        ),
+        grid_spec=pltpu.PrefetchScalarGridSpec(
+            num_scalar_prefetch=1,
+            grid=(1,),
+            in_specs=[whole(block.shape) for block in blocks],
+            out_specs=(whole(OWN), whole((3, *TOTAL))),
+            scratch_shapes=[*ROW_SCRATCH, pltpu.VMEM(TOTAL, jnp.float32)],
+        ),
+        compiler_params=pltpu.CompilerParams(vmem_limit_bytes=28 * 1024 * 1024),
         cost_estimate=pl.CostEstimate(
             flops=12 * 10**9, bytes_accessed=8 * 2**20, transcendentals=0
         ),
@@ -326,17 +306,13 @@
         load_rows(place, mine, other, *rows)
         now[...] = own[...]
 
-    chunks = (
-        [left.at[n] for n in range(4)],
-        [right.at[n] for n in range(4)],
-        [up.at[0], up.at[1], down.at[0], down.at[1]],
-    )
+    chunks = (parts_of(left), parts_of(right), parts_of(up, down))
     for n, blocks in enumerate(chunks):
 
         @pl.when(step == n)
         def _():
             total[...] = before[0]
-            add_blocks(blocks, place, HIGH_FAR, GROUP_FAR, rows, total)
+            add_blocks(blocks, place, 3, rows, total)
             settle(total, later)
 
     @pl.when(step == 0)
@@ -365,14 +341,9 @@
             num_scalar_prefetch=1,
             grid=(4,),
             in_specs=[
-                WHOLE,
-                WHOLE,
-                WHOLE,
-                WHOLE,
-                WHOLE,
+                *[whole(block.shape) for block in (left, right, up, down, own)],
                 pl.BlockSpec((1, *TOTAL), lambda j, place: (jnp.minimum(j, 2), 0, 0, 0, 0)),
-                WHOLE,
-                WHOLE,
+                *[whole(block.shape) for block in (mine, other)],
                 pl.BlockSpec(memory_space=pl.ANY),
             ],
             out_specs=pl.BlockSpec((16, 2, 1, 8, LAGS), lambda j, place: (0, 0, place[j], 0, 0)),
@@ -385,7 +356,7 @@
                 pltpu.SemaphoreType.DMA(()),
             ],
         ),
-        compiler_params=pltpu.CompilerParams(vmem_limit_bytes=32 * 1024 * 1024),
+        compiler_params=pltpu.CompilerParams(vmem_limit_bytes=36 * 1024 * 1024),
         cost_estimate=pl.CostEstimate(
             flops=2 * 1024 * 1024 * LAGS, bytes_accessed=24 * 2**20, transcendentals=0
         ),
@@ -398,25 +369,23 @@
     row = lax.axis_index("row")
     col = lax.axis_index("col")
     x, z = row % 4, (row // 4) * 4 + z_low
-    near_z = (z + jnp.array(NEAR)) % 8
-    far_z = (z + jnp.array(FAR)) % 8
+    where = (z + jnp.array(NEAR + FAR)) % 8
     place = jnp.concatenate(
         [
             (x + jnp.array([0, -1, 1, 2])) % 4,
-            near_z // 4,
-            near_z % 4,
-            far_z // 4,
-            far_z % 4,
+            where // 4,
+            where % 4,
             (z_low - jnp.arange(4)) % 4,
             jnp.stack([col % 2]),
         ]
     ).astype(jnp.int32)
     arrived = first_step(plain, weighted)
     near, sent = second_step(plain, weighted, arrived, col // 2, z_low)
-    mine, other, left, right, up, down, across_opposite = sent
-    rest = third_step(up, down, across_opposite)
+    mine, other, left, right, up, down, across_near = sent
+    across = arrived[2]
+    rest = third_step(up, down, across, across_near)
     own, before = near_totals(
-        place, near, up, down, left, right, arrived[1], across_opposite, mine, other
+        place, near, up, down, left, right, across, across_near, mine, other
     )
     corr = correlations(place, *rest, own, before, mine, other)
     return corr.reshape(1, 1, 16, 8, 8, LAGS)

time: 142 us -> 105 us (0.74)
  the two profiles are of different devices: /device:TPU:6 before, /device:TPU:120 now
where the time goes in v5:
time: 105 us
  Pallas kernels  35.2 us (34%)
  starting transfers between devices  33 us (31%)
  waiting for transfers between devices  25.8 us (25%)
  other arithmetic  4.73 us (5%)
  matrix products  3.82 us (4%)
  local copies, waits for them, and re-layouts  2.09 us (2%)
    ppermute x16, starting transfers between devices, shift(): return lax.ppermute(value, AXES, pairs)  28.4 us
    pallas_call x1, Pallas kernels, correlations(): pl.pallas_call(far_kernel, out_shape=jax.ShapeDtypeStruct((16, 2, 4, 8, L...  22.7 us
    ppermute x16, waiting for transfers between devices, shift(): return lax.ppermute(value, AXES, pairs)  21.5 us
    pallas_call x1, Pallas kernels, near_totals(): pl.pallas_call(near_kernel, out_shape=(jax.ShapeDtypeStruct(OWN, jnp.bflo...  12.5 us
    ppermute x3, starting transfers between devices, own_only(): return lax.ppermute(value, 'win', [(i, (i + k) % 4) for i in range(4)])  4.56 us
    ppermute x3, waiting for transfers between devices, own_only(): return lax.ppermute(value, 'win', [(i, (i + k) % 4) for i in range(4)])  4.35 us
    dot_general x4, matrix products, product(): return jnp.dot(left, table, preferred_element_type=jnp.float32)  3.02 us
  transfers between devices with their start and end apart: 19, of which 6 were waited for; matrix products, arithmetic and copies ran while one was open for 1% of the time, Pallas kernels for 12%

profile of v5, /device:TPU:120, one launch (start us, length us, event | category | flops | bytes accessed | tf_op | source)
XLA Modules:
  0.0 105.1 jit_solution(12106013148648613689)
XLA Ops:
  0.0 1.8 %convert_reduce_fusion = f32[8,8]{1,0:T(8,128)S(1)} fusion(bf16[8,8,12000]{2,1,0:T(8,128)(2,1)} %param.11), kind=kLoop, calls=%fused_computation | loop fusion | flops 1535936 | bytes 1536256 | tf_op jit(solution)/shard_map/reduce_sum | solution.py:83
  1.9 0.1 div.57
  1.9 1.9 %fusion.3 = f32[64,12000]{1,0:T(8,128)S(1)} fusion(bf16[8,8,12000]{2,1,0:T(8,128)(2,1)} %param.11, f32[12000]{0:T(1024)} %constant.156, f32[64]{0:T(128)S(1)} %div.57), kind=kLoop, calls=%fused_computation.5 | loop fusion | flops 3840000 | bytes 4656256 | tf_op jit(solution)/shard_map/convert_element_type | solution.py:84
  3.8 0.0 copy-start.1
  3.8 0.9 fusion.7
  4.8 0.0 copy-done.7
  4.8 0.0 copy-start
  4.8 0.9 fusion.6
  5.7 0.0 copy-done.1
  5.7 0.6 fusion.8
  6.3 0.6 copy-done
  6.9 0.6 convolution_add_fusion.1
  7.5 0.0 copy-start.6
  7.5 0.6 copy-done.2
  8.1 0.8 fusion.14
  8.9 0.0 copy-done.3
  8.9 0.1 fusion.9
  9.0 0.8 collective-permute-start.5
  9.8 0.9 collective-permute-start.4
  10.8 2.2 %collective-permute-start.3 = (bf16[8,8,1024]{2,1,0:T(8,128)(2,1)S(1)}, bf16[8,8,1024]{2,1,0:T(8,128)(2,1)S(1)}, u32[]{:S(2)}, u32[]{:S(2)}) collective-permute-start(bf16[8,8,1024]{2,1,0:T(8,128)(2,1)S(1)} %fusion.9), channel_id=1, source_target_pairs={{0,2},{1,3},{64,66},{65,67},{128,130},{129,131},{192,194},{193,195... | collective-permute-start | bytes 393224 | tf_op jit(solution)/shard_map/ppermute | solution.py:131
  13.0 3.1 %collective-permute-start.2 = (bf16[8,8,1024]{2,1,0:T(8,128)(2,1)S(1)}, bf16[8,8,1024]{2,1,0:T(8,128)(2,1)S(1)}, u32[]{:S(2)}, u32[]{:S(2)}) collective-permute-start(bf16[8,8,1024]{2,1,0:T(8,128)(2,1)S(1)} %get-tuple-element.50), channel_id=1, source_target_pairs={{0,16},{1,17},{64,80},{65,81},{128,144},{129,145},{192,208},{193,2... | collective-permute-start | bytes 393224 | tf_op jit(solution)/shard_map/ppermute | solution.py:131
  16.1 3.6 %collective-permute-start.1 = (bf16[8,8,1024]{2,1,0:T(8,128)(2,1)S(1)}, bf16[8,8,1024]{2,1,0:T(8,128)(2,1)S(1)}, u32[]{:S(2)}, u32[]{:S(2)}) collective-permute-start(bf16[8,8,1024]{2,1,0:T(8,128)(2,1)S(1)} %get-tuple-element.50), channel_id=1, source_target_pairs={{0,128},{1,129},{64,192},{65,193},{128,32},{129,33},{192,96},{193,... | collective-permute-start | bytes 393224 | tf_op jit(solution)/shard_map/ppermute | solution.py:131
  19.7 0.0 collective-permute-done.5
  19.7 0.0 collective-permute-start
  19.7 0.0 collective-permute-done.4
  19.7 0.0 collective-permute-done.3
  19.7 0.0 collective-permute-done.2.across
  19.7 4.4 %collective-permute-done.1 = bf16[8,8,1024]{2,1,0:T(8,128)(2,1)S(1)} collective-permute-done((bf16[8,8,1024]{2,1,0:T(8,128)(2,1)S(1)}, bf16[8,8,1024]{2,1,0:T(8,128)(2,1)S(1)}, u32[]{:S(2)}, u32[]{:S(2)}) %collective-permute-start.1) | collective-permute-done | bytes 131104 | tf_op jit(solution)/shard_map/ppermute | solution.py:131
  24.2 6.1 %collective-permute-done = bf16[8,8,1024]{2,1,0:T(8,128)(2,1)S(1)} collective-permute-done((bf16[8,8,1024]{2,1,0:T(8,128)(2,1)S(1)}, bf16[8,8,1024]{2,1,0:T(8,128)(2,1)S(1)}, u32[]{:S(2)}, u32[]{:S(2)}) %collective-permute-start) | collective-permute-done | bytes 131104 | tf_op jit(solution)/shard_map/ppermute | solution.py:131
  30.3 0.1 select_bitcast_fusion
  30.4 2.1 %collective-permute-start.8 = (bf16[8,8,1024]{2,1,0:T(8,128)(2,1)S(1)}, bf16[8,8,1024]{2,1,0:T(8,128)(2,1)S(1)}, u32[]{:S(2)}, u32[]{:S(2)}) collective-permute-start(bf16[8,8,1024]{2,1,0:T(8,128)(2,1)S(1)} %get-tuple-element.46), channel_id=1, source_target_pairs={{0,192},{64,0},{128,64},{192,128},{1,193},{65,1},{129,65},{193,129... | collective-permute-start | bytes 393224 | tf_op jit(solution)/shard_map/ppermute | solution.py:135
  32.5 0.3 collective-permute-start.7
  32.8 2.2 %collective-permute-start.6 = (bf16[8,8,1024]{2,1,0:T(8,128)(2,1)S(1)}, bf16[8,8,1024]{2,1,0:T(8,128)(2,1)S(1)}, u32[]{:S(2)}, u32[]{:S(2)}) collective-permute-start(bf16[8,8,1024]{2,1,0:T(8,128)(2,1)S(1)} %get-tuple-element.48), channel_id=1, source_target_pairs={{0,64},{64,128},{128,192},{192,0},{1,65},{65,129},{129,193},{193,1... | collective-permute-start | bytes 393224 | tf_op jit(solution)/shard_map/ppermute | solution.py:135
  35.0 2.8 %collective-permute-start.14 = (bf16[2,8,8,1024]{3,2,1,0:T(8,128)(2,1)S(1)}, bf16[2,8,8,1024]{3,2,1,0:T(8,128)(2,1)S(1)}, u32[]{:S(2)}, u32[]{:S(2)}) collective-permute-start(bf16[2,8,8,1024]{3,2,1,0:T(8,128)(2,1)S(1)} %get-tuple-element.51), channel_id=1, source_target_pairs={{0,16},{1,17},{64,80},{65,81},{128,144},{129,145},{192,208},{193,2... | collective-permute-start | bytes 786440 | tf_op jit(solution)/shard_map/ppermute | solution.py:131
  37.8 0.0 copy-done.6
  37.8 0.9 collective-permute-done.8
  38.7 3.4 %collective-permute-done.7 = bf16[8,8,1024]{2,1,0:T(8,128)(2,1)S(1)} collective-permute-done((bf16[8,8,1024]{2,1,0:T(8,128)(2,1)S(1)}, bf16[8,8,1024]{2,1,0:T(8,128)(2,1)S(1)}, u32[]{:S(2)}, u32[]{:S(2)}) %collective-permute-start.7) | collective-permute-done | bytes 131104 | tf_op jit(solution)/shard_map/ppermute | solution.py:135
  42.2 0.0 collective-permute-done.6
  42.2 0.1 pad_maximum_fusion.mine
  42.2 0.1 collective-permute-start.9
  42.4 6.7 %collective-permute-start.12 = (bf16[3,8,8,1024]{3,2,1,0:T(8,128)(2,1)S(1)}, bf16[3,8,8,1024]{3,2,1,0:T(8,128)(2,1)S(1)}, u32[]{:S(2)}, u32[]{:S(2)}) collective-permute-start(bf16[3,8,8,1024]{3,2,1,0:T(8,128)(2,1)S(1)} %pad_maximum_fusion.1.near), channel_id=1, source_target_pairs={{0,64},{1,65},{64,128},{65,129},{128,192},{129,193},{192,32},{193,... | collective-permute-start | bytes 1179656 | tf_op jit(solution)/shard_map/ppermute | solution.py:131
  49.0 2.8 %collective-permute-start.11 = (bf16[3,8,8,1024]{3,2,1,0:T(8,128)(2,1)S(1)}, bf16[3,8,8,1024]{3,2,1,0:T(8,128)(2,1)S(1)}, u32[]{:S(2)}, u32[]{:S(2)}) collective-permute-start(bf16[3,8,8,1024]{3,2,1,0:T(8,128)(2,1)S(1)} %pad_maximum_fusion.1.near), channel_id=1, source_target_pairs={{0,24},{1,25},{64,88},{65,89},{128,152},{129,153},{192,216},{193,2... | collective-permute-start | bytes 1179656 | tf_op jit(solution)/shard_map/ppermute | solution.py:131
  51.9 0.0 collective-permute-start.10
  51.9 0.0 collective-permute-done.14.across_near
  51.9 0.0 collective-permute-start.13
  51.9 0.5 and_select_fusion.2
  52.4 0.7 concatenate.22.place
  53.2 8.1 %collective-permute-done.13.down = bf16[2,8,8,1024]{3,2,1,0:T(8,128)(2,1)S(1)} collective-permute-done((bf16[2,8,8,1024]{3,2,1,0:T(8,128)(2,1)S(1)}, bf16[2,8,8,1024]{3,2,1,0:T(8,128)(2,1)S(1)}, u32[]{:S(2)}, u32[]{:S(2)}) %collective-permute-start.13) | collective-permute-done | bytes 262176 | tf_op jit(solution)/shard_map/ppermute | solution.py:131
  61.2 0.0 collective-permute-done.12.up
  61.2 0.0 collective-permute-done.11.right
  61.2 2.8 %collective-permute-done.10.left = bf16[3,8,8,1024]{3,2,1,0:T(8,128)(2,1)S(1)} collective-permute-done((bf16[3,8,8,1024]{3,2,1,0:T(8,128)(2,1)S(1)}, bf16[3,8,8,1024]{3,2,1,0:T(8,128)(2,1)S(1)}, u32[]{:S(2)}, u32[]{:S(2)}) %collective-permute-start.10) | collective-permute-done | bytes 393248 | tf_op jit(solution)/shard_map/ppermute | solution.py:131
  64.0 0.0 collective-permute-done.9.other
  64.1 0.4 collective-permute-start.16
  64.5 1.7 %collective-permute-start.15 = (bf16[5,8,8,1024]{3,2,1,0:T(8,128)(2,1)S(1)}, bf16[5,8,8,1024]{3,2,1,0:T(8,128)(2,1)S(1)}, u32[]{:S(2)}, u32[]{:S(2)}) collective-permute-start(bf16[5,8,8,1024]{3,2,1,0:T(8,128)(2,1)S(1)} %constant_dynamic-update-slice_fusion), channel_id=1, source_target_pairs={{0,8},{1,9},{64,72},{65,73},{128,136},{129,137},{192,200},{193,201... | collective-permute-start | bytes 1966088 | tf_op jit(solution)/shard_map/ppermute | solution.py:131
  66.3 0.0 slice-start
  66.3 0.0 slice-start.1
  66.3 0.1 collective-permute-start.18
  66.4 3.2 %collective-permute-start.17 = (bf16[3,8,8,1024]{3,2,1,0:T(8,128)(2,1)S(1)}, bf16[3,8,8,1024]{3,2,1,0:T(8,128)(2,1)S(1)}, u32[]{:S(2)}, u32[]{:S(2)}) collective-permute-start(bf16[3,8,8,1024]{3,2,1,0:T(8,128)(2,1)S(1)} %pad_maximum_fusion.2), channel_id=1, source_target_pairs={{0,64},{1,65},{64,128},{65,129},{128,192},{129,193},{192,32},{193,... | collective-permute-start | bytes 1179656 | tf_op jit(solution)/shard_map/ppermute | solution.py:131
  69.6 12.5 %shard_map.109 = (bf16[256,1024]{1,0:T(8,128)(2,1)S(1)}, f32[3,2,16,8,1024]{4,3,2,1,0:T(8,128)S(1)}) custom-call(s32[25]{0:T(128)S(1)} %concatenate.22.place, bf16[3,8,8,1024]{3,2,1,0:T(8,128)(2,1)S(1)} %pad_maximum_fusion.1.near, bf16[3,8,8,1024]{3,2,1,0:T(8,128)(2,1)S(1)} %collective-permute-done.12.up, ...), custom_call_target="tpu_custom_call" | custom-call | flops 12000000000 | bytes 8388608 | tf_op jit(solution)/shard_map/pallas_call | solution.py:276
  82.1 0.0 collective-permute-done.18.down
  82.2 0.0 collective-permute-done.17.up
  82.2 0.0 collective-permute-done.16.right
  82.2 0.0 collective-permute-done.15.left
  82.2 22.7 %shard_map.110 = bf16[16,2,4,8,4000]{4,3,2,1,0:T(8,128)(2,1)} custom-call(s32[25]{0:T(128)S(1)} %concatenate.22.place, bf16[5,8,8,1024]{3,2,1,0:T(8,128)(2,1)S(1)} %collective-permute-done.15.left, bf16[5,8,8,1024]{3,2,1,0:T(8,128)(2,1)S(1)} %collective-permute-done.16.right, bf16[3,8,8,1024]{3,2,1,0:T(8,128)(2,1)S(1)} %collective-permute-done.17.up, ...), custom_call_target="tpu_custom_call" | custom-call | flops 8388608000 | bytes 25165824 | tf_op jit(solution)/shard_map/pallas_call | solution.py:337
  (25 shorter events, 0.3 us)
Async XLA Ops:
  0.0 3.8 %copy-start.8 = (bf16[3000,256]{1,0:T(8,128)(2,1)S(1)}, bf16[3000,256]{1,0:T(8,128)(2,1)}, u32[]{:S(2)}) copy-start(bf16[3000,256]{1,0:T(8,128)(2,1)} %constant.148.clone) | copy-start | bytes 4608004
  1.9 2.8 %copy-start.7 = (bf16[3000,256]{1,0:T(8,128)(2,1)S(1)}, bf16[3000,256]{1,0:T(8,128)(2,1)}, u32[]{:S(2)}) copy-start(bf16[3000,256]{1,0:T(8,128)(2,1)} %constant.147.clone) | copy-start | bytes 4608004
  3.8 1.9 %copy-start.1 = (bf16[3000,512]{1,0:T(8,128)(2,1)S(1)}, bf16[3000,512]{1,0:T(8,128)(2,1)}, u32[]{:S(2)}) copy-start(bf16[3000,512]{1,0:T(8,128)(2,1)} %constant.157) | copy-start | bytes 9216004
  4.8 2.1 %copy-start = (bf16[3000,512]{1,0:T(8,128)(2,1)S(1)}, bf16[3000,512]{1,0:T(8,128)(2,1)}, u32[]{:S(2)}) copy-start(bf16[3000,512]{1,0:T(8,128)(2,1)} %constant.158) | copy-start | bytes 9216004
  6.9 1.2 %copy-start.2 = (f32[512,512]{1,0:T(8,128)S(1)}, f32[512,512]{1,0:T(8,128)}, u32[]{:S(2)}) copy-start(f32[512,512]{1,0:T(8,128)} %constant.150.clone) | copy-start | bytes 3145732
  6.9 1.2 %copy-start.4 = (f32[512]{0:T(512)S(1)}, f32[512]{0:T(512)}, u32[]{:S(2)}) copy-start(f32[512]{0:T(512)} %constant.159) | copy-start | bytes 6148
  6.9 2.0 %copy-start.3 = (f32[8]{0:T(128)S(1)}, f32[8]{0:T(128)}, u32[]{:S(2)}) copy-start(f32[8]{0:T(128)} %param.12) | copy-start | bytes 100
  7.5 30.3 %copy-start.6 = (s32[8]{0:T(128)S(1)}, s32[8]{0:T(128)}, u32[]{:S(2)}) copy-start(s32[8]{0:T(128)} %constant.152.clone) | copy-start | bytes 100
  8.1 44.3 %copy-start.5 = (s32[4]{0:T(128)S(1)}, s32[4]{0:T(128)}, u32[]{:S(2)}) copy-start(s32[4]{0:T(128)} %constant.153.clone) | copy-start | bytes 52
  9.0 10.7 %collective-permute-start.5 = (bf16[8,8,1024]{2,1,0:T(8,128)(2,1)S(1)}, bf16[8,8,1024]{2,1,0:T(8,128)(2,1)S(1)}, u32[]{:S(2)}, u32[]{:S(2)}) collective-permute-start(bf16[8,8,1024]{2,1,0:T(8,128)(2,1)S(1)} %fusion.9), channel_id=1, source_target_pairs={{0,6},{1,7},{64,70},{65,71},{128,134},{129,135},{192,198},{193,199... | collective-permute-start | bytes 393224 | tf_op jit(solution)/shard_map/ppermute | solution.py:131
  9.8 9.8 %collective-permute-start.4 = (bf16[8,8,1024]{2,1,0:T(8,128)(2,1)S(1)}, bf16[8,8,1024]{2,1,0:T(8,128)(2,1)S(1)}, u32[]{:S(2)}, u32[]{:S(2)}) collective-permute-start(bf16[8,8,1024]{2,1,0:T(8,128)(2,1)S(1)} %fusion.9), channel_id=1, source_target_pairs={{0,4},{1,5},{64,68},{65,69},{128,132},{129,133},{192,196},{193,197... | collective-permute-start | bytes 393224 | tf_op jit(solution)/shard_map/ppermute | solution.py:131
  10.8 8.9 %collective-permute-start.3 = (bf16[8,8,1024]{2,1,0:T(8,128)(2,1)S(1)}, bf16[8,8,1024]{2,1,0:T(8,128)(2,1)S(1)}, u32[]{:S(2)}, u32[]{:S(2)}) collective-permute-start(bf16[8,8,1024]{2,1,0:T(8,128)(2,1)S(1)} %fusion.9), channel_id=1, source_target_pairs={{0,2},{1,3},{64,66},{65,67},{128,130},{129,131},{192,194},{193,195... | collective-permute-start | bytes 393224 | tf_op jit(solution)/shard_map/ppermute | solution.py:131
  13.0 6.7 %collective-permute-start.2 = (bf16[8,8,1024]{2,1,0:T(8,128)(2,1)S(1)}, bf16[8,8,1024]{2,1,0:T(8,128)(2,1)S(1)}, u32[]{:S(2)}, u32[]{:S(2)}) collective-permute-start(bf16[8,8,1024]{2,1,0:T(8,128)(2,1)S(1)} %get-tuple-element.50), channel_id=1, source_target_pairs={{0,16},{1,17},{64,80},{65,81},{128,144},{129,145},{192,208},{193,2... | collective-permute-start | bytes 393224 | tf_op jit(solution)/shard_map/ppermute | solution.py:131
  16.1 8.1 %collective-permute-start.1 = (bf16[8,8,1024]{2,1,0:T(8,128)(2,1)S(1)}, bf16[8,8,1024]{2,1,0:T(8,128)(2,1)S(1)}, u32[]{:S(2)}, u32[]{:S(2)}) collective-permute-start(bf16[8,8,1024]{2,1,0:T(8,128)(2,1)S(1)} %get-tuple-element.50), channel_id=1, source_target_pairs={{0,128},{1,129},{64,192},{65,193},{128,32},{129,33},{192,96},{193,... | collective-permute-start | bytes 393224 | tf_op jit(solution)/shard_map/ppermute | solution.py:131
  19.7 10.6 %collective-permute-start = (bf16[8,8,1024]{2,1,0:T(8,128)(2,1)S(1)}, bf16[8,8,1024]{2,1,0:T(8,128)(2,1)S(1)}, u32[]{:S(2)}, u32[]{:S(2)}) collective-permute-start(bf16[8,8,1024]{2,1,0:T(8,128)(2,1)S(1)} %get-tuple-element.50), channel_id=1, source_target_pairs={{0,96},{1,97},{64,160},{65,161},{128,224},{129,225},{192,0},{193,1... | collective-permute-start | bytes 393224 | tf_op jit(solution)/shard_map/ppermute | solution.py:131
  30.4 8.3 %collective-permute-start.8 = (bf16[8,8,1024]{2,1,0:T(8,128)(2,1)S(1)}, bf16[8,8,1024]{2,1,0:T(8,128)(2,1)S(1)}, u32[]{:S(2)}, u32[]{:S(2)}) collective-permute-start(bf16[8,8,1024]{2,1,0:T(8,128)(2,1)S(1)} %get-tuple-element.46), channel_id=1, source_target_pairs={{0,192},{64,0},{128,64},{192,128},{1,193},{65,1},{129,65},{193,129... | collective-permute-start | bytes 393224 | tf_op jit(solution)/shard_map/ppermute | solution.py:135
  32.5 9.7 %collective-permute-start.7 = (bf16[8,8,1024]{2,1,0:T(8,128)(2,1)S(1)}, bf16[8,8,1024]{2,1,0:T(8,128)(2,1)S(1)}, u32[]{:S(2)}, u32[]{:S(2)}) collective-permute-start(bf16[8,8,1024]{2,1,0:T(8,128)(2,1)S(1)} %get-tuple-element.47), channel_id=1, source_target_pairs={{0,128},{64,192},{128,0},{192,64},{1,129},{65,193},{129,1},{193,65... | collective-permute-start | bytes 393224 | tf_op jit(solution)/shard_map/ppermute | solution.py:135
  32.8 9.4 %collective-permute-start.6 = (bf16[8,8,1024]{2,1,0:T(8,128)(2,1)S(1)}, bf16[8,8,1024]{2,1,0:T(8,128)(2,1)S(1)}, u32[]{:S(2)}, u32[]{:S(2)}) collective-permute-start(bf16[8,8,1024]{2,1,0:T(8,128)(2,1)S(1)} %get-tuple-element.48), channel_id=1, source_target_pairs={{0,64},{64,128},{128,192},{192,0},{1,65},{65,129},{129,193},{193,1... | collective-permute-start | bytes 393224 | tf_op jit(solution)/shard_map/ppermute | solution.py:135
  35.0 16.9 %collective-permute-start.14 = (bf16[2,8,8,1024]{3,2,1,0:T(8,128)(2,1)S(1)}, bf16[2,8,8,1024]{3,2,1,0:T(8,128)(2,1)S(1)}, u32[]{:S(2)}, u32[]{:S(2)}) collective-permute-start(bf16[2,8,8,1024]{3,2,1,0:T(8,128)(2,1)S(1)} %get-tuple-element.51), channel_id=1, source_target_pairs={{0,16},{1,17},{64,80},{65,81},{128,144},{129,145},{192,208},{193,2... | collective-permute-start | bytes 786440 | tf_op jit(solution)/shard_map/ppermute | solution.py:131
  42.2 21.8 %collective-permute-start.9 = (bf16[4,8,8,1024]{3,2,1,0:T(8,128)(2,1)S(1)}, bf16[4,8,8,1024]{3,2,1,0:T(8,128)(2,1)S(1)}, u32[]{:S(2)}, u32[]{:S(2)}) collective-permute-start(bf16[4,8,8,1024]{3,2,1,0:T(8,128)(2,1)S(1)} %pad_maximum_fusion.mine), channel_id=1, source_target_pairs={{0,1},{1,0},{64,65},{65,64},{128,129},{129,128},{192,193},{193,192... | collective-permute-start | bytes 1572872 | tf_op jit(solution)/shard_map/ppermute | solution.py:131
  42.4 18.8 %collective-permute-start.12 = (bf16[3,8,8,1024]{3,2,1,0:T(8,128)(2,1)S(1)}, bf16[3,8,8,1024]{3,2,1,0:T(8,128)(2,1)S(1)}, u32[]{:S(2)}, u32[]{:S(2)}) collective-permute-start(bf16[3,8,8,1024]{3,2,1,0:T(8,128)(2,1)S(1)} %pad_maximum_fusion.1.near), channel_id=1, source_target_pairs={{0,64},{1,65},{64,128},{65,129},{128,192},{129,193},{192,32},{193,... | collective-permute-start | bytes 1179656 | tf_op jit(solution)/shard_map/ppermute | solution.py:131
  49.0 12.2 %collective-permute-start.11 = (bf16[3,8,8,1024]{3,2,1,0:T(8,128)(2,1)S(1)}, bf16[3,8,8,1024]{3,2,1,0:T(8,128)(2,1)S(1)}, u32[]{:S(2)}, u32[]{:S(2)}) collective-permute-start(bf16[3,8,8,1024]{3,2,1,0:T(8,128)(2,1)S(1)} %pad_maximum_fusion.1.near), channel_id=1, source_target_pairs={{0,24},{1,25},{64,88},{65,89},{128,152},{129,153},{192,216},{193,2... | collective-permute-start | bytes 1179656 | tf_op jit(solution)/shard_map/ppermute | solution.py:131
  51.9 12.2 %collective-permute-start.10 = (bf16[3,8,8,1024]{3,2,1,0:T(8,128)(2,1)S(1)}, bf16[3,8,8,1024]{3,2,1,0:T(8,128)(2,1)S(1)}, u32[]{:S(2)}, u32[]{:S(2)}) collective-permute-start(bf16[3,8,8,1024]{3,2,1,0:T(8,128)(2,1)S(1)} %pad_maximum_fusion.1.near), channel_id=1, source_target_pairs={{0,8},{1,9},{64,72},{65,73},{128,136},{129,137},{192,200},{193,201... | collective-permute-start | bytes 1179656 | tf_op jit(solution)/shard_map/ppermute | solution.py:131
  51.9 9.4 %collective-permute-start.13 = (bf16[2,8,8,1024]{3,2,1,0:T(8,128)(2,1)S(1)}, bf16[2,8,8,1024]{3,2,1,0:T(8,128)(2,1)S(1)}, u32[]{:S(2)}, u32[]{:S(2)}) collective-permute-start(bf16[2,8,8,1024]{3,2,1,0:T(8,128)(2,1)S(1)} %get-tuple-element.52), channel_id=1, source_target_pairs={{0,224},{1,225},{64,0},{65,1},{128,64},{129,65},{192,128},{193,129... | collective-permute-start | bytes 786440 | tf_op jit(solution)/shard_map/ppermute | solution.py:131
  64.1 18.1 %collective-permute-start.16 = (bf16[5,8,8,1024]{3,2,1,0:T(8,128)(2,1)S(1)}, bf16[5,8,8,1024]{3,2,1,0:T(8,128)(2,1)S(1)}, u32[]{:S(2)}, u32[]{:S(2)}) collective-permute-start(bf16[5,8,8,1024]{3,2,1,0:T(8,128)(2,1)S(1)} %constant_dynamic-update-slice_fusion), channel_id=1, source_target_pairs={{0,24},{1,25},{64,88},{65,89},{128,152},{129,153},{192,216},{193,2... | collective-permute-start | bytes 1966088 | tf_op jit(solution)/shard_map/ppermute | solution.py:131
  64.5 17.7 %collective-permute-start.15 = (bf16[5,8,8,1024]{3,2,1,0:T(8,128)(2,1)S(1)}, bf16[5,8,8,1024]{3,2,1,0:T(8,128)(2,1)S(1)}, u32[]{:S(2)}, u32[]{:S(2)}) collective-permute-start(bf16[5,8,8,1024]{3,2,1,0:T(8,128)(2,1)S(1)} %constant_dynamic-update-slice_fusion), channel_id=1, source_target_pairs={{0,8},{1,9},{64,72},{65,73},{128,136},{129,137},{192,200},{193,201... | collective-permute-start | bytes 1966088 | tf_op jit(solution)/shard_map/ppermute | solution.py:131
  66.3 15.9 %slice-start = ((s8[8388608]{0:T(1024)(128)(4,1)}), s8[4194304]{0:T(1024)(128)(4,1)S(1)}, s32[]{:S(2)}) async-start(s8[8388608]{0:T(1024)(128)(4,1)} %bitcast.36), calls=%async_computation | async-start | bytes 8388608
  66.3 15.9 %slice-start.1 = ((s8[8388608]{0:T(1024)(128)(4,1)}), s8[4194304]{0:T(1024)(128)(4,1)S(1)}, s32[]{:S(2)}) async-start(s8[8388608]{0:T(1024)(128)(4,1)} %bitcast.36), calls=%async_computation.1 | async-start | bytes 8388608
  66.3 15.8 %collective-permute-start.18 = (bf16[2,8,8,1024]{3,2,1,0:T(8,128)(2,1)S(1)}, bf16[2,8,8,1024]{3,2,1,0:T(8,128)(2,1)S(1)}, u32[]{:S(2)}, u32[]{:S(2)}) collective-permute-start(bf16[2,8,8,1024]{3,2,1,0:T(8,128)(2,1)S(1)} %pad_maximum_fusion.6), channel_id=1, source_target_pairs={{0,224},{1,225},{64,0},{65,1},{128,64},{129,65},{192,128},{193,129... | collective-permute-start | bytes 786440 | tf_op jit(solution)/shard_map/ppermute | solution.py:131
  66.4 15.8 %collective-permute-start.17 = (bf16[3,8,8,1024]{3,2,1,0:T(8,128)(2,1)S(1)}, bf16[3,8,8,1024]{3,2,1,0:T(8,128)(2,1)S(1)}, u32[]{:S(2)}, u32[]{:S(2)}) collective-permute-start(bf16[3,8,8,1024]{3,2,1,0:T(8,128)(2,1)S(1)} %pad_maximum_fusion.2), channel_id=1, source_target_pairs={{0,64},{1,65},{64,128},{65,129},{128,192},{129,193},{192,32},{193,... | collective-permute-start | bytes 1179656 | tf_op jit(solution)/shard_map/ppermute | solution.py:131

commit v6 on v5

--- a/solution.py
+++ b/solution.py
@@ -141,19 +141,19 @@
 
 def first_step(plain, weighted):
     return together(
+        shift(weighted, dy=1),
+        shift(weighted, dy=3),
+        shift(weighted, dy=2),
+        shift(plain, dx=2),
+        shift(plain, dz=2),
         shift(plain, dz=-3),
-        shift(plain, dz=2),
-        shift(plain, dx=2),
-        shift(weighted, dy=1),
-        shift(weighted, dy=2),
-        shift(weighted, dy=3),
     )
 
 
 def second_step(plain, weighted, arrived, y, z_low):
-    ahead, behind, across, *sides = arrived
+    left, right, opposite, across, behind, ahead = arrived
     near = jnp.stack([plain, ahead, behind])
-    held = [weighted, *sides]
+    held = [weighted, left, opposite, right]
 
     def for_offset(k):
         at = (y - z_low - k) % 4
@@ -161,26 +161,45 @@
         high = jnp.where(at == 2, held[2], held[3])
         return jnp.where(at < 2, low, high)
 
-    mine = jnp.stack([for_offset(0)] + [own_only(for_offset(k), k) for k in (1, 2, 3)])
-    return near, together(
+    return together(
+        for_offset(0),
+        own_only(for_offset(1), 1),
+        own_only(for_offset(2), 2),
+        own_only(for_offset(3), 3),
+        shift(near, dx=-1),
+        shift(near, dx=1),
+        near,
+        across,
+    )
+
+
+def third_step(arrived):
+    *rows, right, left, near, across = arrived
+    mine = jnp.stack(rows)
+    across_near, other, down, up, *rest = together(
+        shift(near[1:], dx=2),
+        shift(mine, dcore=1),
+        shift(near[:2], dz=-1),
+        shift(near, dz=1),
         mine,
-        shift(mine, dcore=1),
-        shift(near, dx=1),
-        shift(near, dx=-1),
-        shift(near, dz=1),
-        shift(jnp.stack([plain, ahead]), dz=-1),
-        shift(jnp.stack([ahead, behind]), dx=2),
-    )
-
-
-def third_step(up, down, across, across_near):
+        near,
+        left,
+        right,
+        across,
+    )
+    mine, near, left, right, across = rest
+    return near, up, down, left, right, across, across_near, mine, other
+
+
+def fourth_step(up, down, across, across_near):
     far = jnp.concatenate([up, down])
-    return together(
+    down_out, up_out, right, left = together(
+        shift(jnp.stack([across, across_near[0]]), dz=-1),
+        shift(jnp.concatenate([across[None], across_near]), dz=1),
+        shift(far, dx=-1),
         shift(far, dx=1),
-        shift(far, dx=-1),
-        shift(jnp.concatenate([across[None], across_near]), dz=1),
-        shift(jnp.stack([across, across_near[0]]), dz=-1),
-    )
+    )
+    return left, right, up_out, down_out
 
 
 NEAR = (0, 3, -2)
@@ -380,10 +399,9 @@
         ]
     ).astype(jnp.int32)
     arrived = first_step(plain, weighted)
-    near, sent = second_step(plain, weighted, arrived, col // 2, z_low)
-    mine, other, left, right, up, down, across_near = sent
-    across = arrived[2]
-    rest = third_step(up, down, across, across_near)
+    arrived = second_step(plain, weighted, arrived, col // 2, z_low)
+    near, up, down, left, right, across, across_near, mine, other = third_step(arrived)
+    rest = fourth_step(up, down, across, across_near)
     own, before = near_totals(
         place, near, up, down, left, right, across, across_near, mine, other
     )

time: 105 us -> 101 us (0.962)
  the two profiles are of different devices: /device:TPU:120 before, /device:TPU:6 now
where the time goes in v6:
time: 101 us
  Pallas kernels  35.2 us (35%)
  starting transfers between devices  29.3 us (29%)
  waiting for transfers between devices  24.8 us (25%)
  other arithmetic  4.68 us (5%)
  matrix products  3.81 us (4%)
  local copies, waits for them, and re-layouts  2.79 us (3%)
    ppermute x16, starting transfers between devices, shift(): return lax.ppermute(value, AXES, pairs)  26.3 us
    pallas_call x1, Pallas kernels, correlations(): pl.pallas_call(far_kernel, out_shape=jax.ShapeDtypeStruct((16, 2, 4, 8, L...  22.7 us
    ppermute x16, waiting for transfers between devices, shift(): return lax.ppermute(value, AXES, pairs)  15.3 us
    pallas_call x1, Pallas kernels, near_totals(): pl.pallas_call(near_kernel, out_shape=(jax.ShapeDtypeStruct(OWN, jnp.bflo...  12.5 us
    ppermute x3, waiting for transfers between devices, own_only(): return lax.ppermute(value, 'win', [(i, (i + k) % 4) for i in range(4)])  9.52 us
    dot_general x4, matrix products, product(): return jnp.dot(left, table, preferred_element_type=jnp.float32)  3.02 us
    ppermute x3, starting transfers between devices, own_only(): return lax.ppermute(value, 'win', [(i, (i + k) % 4) for i in range(4)])  3.02 us
  transfers between devices with their start and end apart: 19, of which 7 were waited for; matrix products, arithmetic and copies ran while one was open for 2% of the time, Pallas kernels for 12%

profile of v6, /device:TPU:6, one launch (start us, length us, event | category | flops | bytes accessed | tf_op | source)
XLA Modules:
  0.0 101.0 jit_solution(5019568186318587955)
XLA Ops:
  0.0 1.8 %convert_reduce_fusion = f32[8,8]{1,0:T(8,128)S(1)} fusion(bf16[8,8,12000]{2,1,0:T(8,128)(2,1)} %param.11), kind=kLoop, calls=%fused_computation | loop fusion | flops 1535936 | bytes 1536256 | tf_op jit(solution)/shard_map/reduce_sum | solution.py:83
  1.9 0.1 div.57
  1.9 1.9 %fusion.3 = f32[64,12000]{1,0:T(8,128)S(1)} fusion(bf16[8,8,12000]{2,1,0:T(8,128)(2,1)} %param.11, f32[12000]{0:T(1024)} %constant.156, f32[64]{0:T(128)S(1)} %div.57), kind=kLoop, calls=%fused_computation.5 | loop fusion | flops 3840000 | bytes 4656256 | tf_op jit(solution)/shard_map/convert_element_type | solution.py:84
  3.8 0.0 copy-start.1
  3.8 0.9 fusion.7
  4.8 0.0 copy-done.7
  4.8 0.0 copy-start
  4.8 0.9 fusion.6
  5.7 0.0 copy-done.1
  5.7 0.6 fusion.8
  6.3 0.6 copy-done
  6.9 0.6 convolution_add_fusion.1
  7.5 0.0 copy-start.6
  7.5 0.6 copy-done.2
  8.1 0.8 fusion.14
  8.9 0.0 copy-start.5
  8.9 0.1 fusion.9
  9.0 3.3 %collective-permute-start.2 = (bf16[8,8,1024]{2,1,0:T(8,128)(2,1)S(1)}, bf16[8,8,1024]{2,1,0:T(8,128)(2,1)S(1)}, u32[]{:S(2)}, u32[]{:S(2)}) collective-permute-start(bf16[8,8,1024]{2,1,0:T(8,128)(2,1)S(1)} %fusion.9), channel_id=1, source_target_pairs={{0,4},{1,5},{64,68},{65,69},{128,132},{129,133},{192,196},{193,197... | collective-permute-start | bytes 393224 | tf_op jit(solution)/shard_map/ppermute | solution.py:131
  12.3 1.1 %collective-permute-start.1 = (bf16[8,8,1024]{2,1,0:T(8,128)(2,1)S(1)}, bf16[8,8,1024]{2,1,0:T(8,128)(2,1)S(1)}, u32[]{:S(2)}, u32[]{:S(2)}) collective-permute-start(bf16[8,8,1024]{2,1,0:T(8,128)(2,1)S(1)} %fusion.9), channel_id=1, source_target_pairs={{0,6},{1,7},{64,70},{65,71},{128,134},{129,135},{192,198},{193,199... | collective-permute-start | bytes 393224 | tf_op jit(solution)/shard_map/ppermute | solution.py:131
  13.4 1.0 collective-permute-start
  14.4 6.8 %collective-permute-start.5 = (bf16[8,8,1024]{2,1,0:T(8,128)(2,1)S(1)}, bf16[8,8,1024]{2,1,0:T(8,128)(2,1)S(1)}, u32[]{:S(2)}, u32[]{:S(2)}) collective-permute-start(bf16[8,8,1024]{2,1,0:T(8,128)(2,1)S(1)} %get-tuple-element.72), channel_id=1, source_target_pairs={{0,96},{1,97},{64,160},{65,161},{128,224},{129,225},{192,0},{193,1... | collective-permute-start | bytes 393224 | tf_op jit(solution)/shard_map/ppermute | solution.py:131
  21.2 1.5 %collective-permute-start.4 = (bf16[8,8,1024]{2,1,0:T(8,128)(2,1)S(1)}, bf16[8,8,1024]{2,1,0:T(8,128)(2,1)S(1)}, u32[]{:S(2)}, u32[]{:S(2)}) collective-permute-start(bf16[8,8,1024]{2,1,0:T(8,128)(2,1)S(1)} %get-tuple-element.72), channel_id=1, source_target_pairs={{0,128},{1,129},{64,192},{65,193},{128,32},{129,33},{192,96},{193,... | collective-permute-start | bytes 393224 | tf_op jit(solution)/shard_map/ppermute | solution.py:131
  22.6 0.0 collective-permute-done.2
  22.7 1.4 %collective-permute-start.3 = (bf16[8,8,1024]{2,1,0:T(8,128)(2,1)S(1)}, bf16[8,8,1024]{2,1,0:T(8,128)(2,1)S(1)}, u32[]{:S(2)}, u32[]{:S(2)}) collective-permute-start(bf16[8,8,1024]{2,1,0:T(8,128)(2,1)S(1)} %get-tuple-element.72), channel_id=1, source_target_pairs={{0,16},{1,17},{64,80},{65,81},{128,144},{129,145},{192,208},{193,2... | collective-permute-start | bytes 393224 | tf_op jit(solution)/shard_map/ppermute | solution.py:131
  24.1 0.0 collective-permute-done.1
  24.1 0.0 collective-permute-done
  24.1 4.6 %collective-permute-done.5 = bf16[8,8,1024]{2,1,0:T(8,128)(2,1)S(1)} collective-permute-done((bf16[8,8,1024]{2,1,0:T(8,128)(2,1)S(1)}, bf16[8,8,1024]{2,1,0:T(8,128)(2,1)S(1)}, u32[]{:S(2)}, u32[]{:S(2)}) %collective-permute-start.5) | collective-permute-done | bytes 131104 | tf_op jit(solution)/shard_map/ppermute | solution.py:131
  28.7 1.4 %collective-permute-done.4 = bf16[8,8,1024]{2,1,0:T(8,128)(2,1)S(1)} collective-permute-done((bf16[8,8,1024]{2,1,0:T(8,128)(2,1)S(1)}, bf16[8,8,1024]{2,1,0:T(8,128)(2,1)S(1)}, u32[]{:S(2)}, u32[]{:S(2)}) %collective-permute-start.4) | collective-permute-done | bytes 131104 | tf_op jit(solution)/shard_map/ppermute | solution.py:131
  30.1 0.0 collective-permute-done.3.across
  30.2 0.6 collective-permute-start.10
  30.7 1.5 %collective-permute-start.9 = (bf16[3,8,8,1024]{3,2,1,0:T(8,128)(2,1)S(1)}, bf16[3,8,8,1024]{3,2,1,0:T(8,128)(2,1)S(1)}, u32[]{:S(2)}, u32[]{:S(2)}) collective-permute-start(bf16[3,8,8,1024]{3,2,1,0:T(8,128)(2,1)S(1)} %pad_maximum_fusion.1.near), channel_id=1, source_target_pairs={{0,24},{1,25},{64,88},{65,89},{128,152},{129,153},{192,216},{193,2... | collective-permute-start | bytes 1179656 | tf_op jit(solution)/shard_map/ppermute | solution.py:131
  32.3 0.1 select_select_fusion
  32.4 0.2 collective-permute-start.8
  32.6 2.8 %collective-permute-start.7 = (bf16[8,8,1024]{2,1,0:T(8,128)(2,1)S(1)}, bf16[8,8,1024]{2,1,0:T(8,128)(2,1)S(1)}, u32[]{:S(2)}, u32[]{:S(2)}) collective-permute-start(bf16[8,8,1024]{2,1,0:T(8,128)(2,1)S(1)} %get-tuple-element.66), channel_id=1, source_target_pairs={{0,128},{64,192},{128,0},{192,64},{1,129},{65,193},{129,1},{193,65... | collective-permute-start | bytes 393224 | tf_op jit(solution)/shard_map/ppermute | solution.py:135
  35.4 0.0 collective-permute-start.6
  35.5 2.9 %collective-permute-done.8 = bf16[8,8,1024]{2,1,0:T(8,128)(2,1)S(1)} collective-permute-done((bf16[8,8,1024]{2,1,0:T(8,128)(2,1)S(1)}, bf16[8,8,1024]{2,1,0:T(8,128)(2,1)S(1)}, u32[]{:S(2)}, u32[]{:S(2)}) %collective-permute-start.8) | collective-permute-done | bytes 131104 | tf_op jit(solution)/shard_map/ppermute | solution.py:135
  38.3 6.7 %collective-permute-done.7 = bf16[8,8,1024]{2,1,0:T(8,128)(2,1)S(1)} collective-permute-done((bf16[8,8,1024]{2,1,0:T(8,128)(2,1)S(1)}, bf16[8,8,1024]{2,1,0:T(8,128)(2,1)S(1)}, u32[]{:S(2)}, u32[]{:S(2)}) %collective-permute-start.7) | collective-permute-done | bytes 131104 | tf_op jit(solution)/shard_map/ppermute | solution.py:135
  45.0 0.0 collective-permute-done.6
  45.0 0.0 collective-permute-done.10.left
  45.0 0.0 collective-permute-done.9.right
  45.0 0.3 collective-permute-start.14
  45.3 0.1 pad_maximum_fusion.mine
  45.3 0.1 collective-permute-start.12
  45.4 0.8 fusion.21
  46.2 3.2 %collective-permute-start.13 = (bf16[2,8,8,1024]{3,2,1,0:T(8,128)(2,1)}, bf16[2,8,8,1024]{3,2,1,0:T(8,128)(2,1)S(1)}, u32[]{:S(2)}, u32[]{:S(2)}) collective-permute-start(bf16[2,8,8,1024]{3,2,1,0:T(8,128)(2,1)} %get-tuple-element.69), channel_id=1, source_target_pairs={{0,224},{1,225},{64,0},{65,1},{128,64},{129,65},{192,128},{193,129... | collective-permute-start | bytes 786440 | tf_op jit(solution)/shard_map/ppermute | solution.py:131
  49.4 1.4 %collective-permute-start.11 = (bf16[2,8,8,1024]{3,2,1,0:T(8,128)(2,1)S(1)}, bf16[2,8,8,1024]{3,2,1,0:T(8,128)(2,1)S(1)}, u32[]{:S(2)}, u32[]{:S(2)}) collective-permute-start(bf16[2,8,8,1024]{3,2,1,0:T(8,128)(2,1)S(1)} %get-tuple-element.70), channel_id=1, source_target_pairs={{0,16},{1,17},{64,80},{65,81},{128,144},{129,145},{192,208},{193,2... | collective-permute-start | bytes 786440 | tf_op jit(solution)/shard_map/ppermute | solution.py:131
  50.8 0.5 and_select_fusion.2
  51.3 0.7 concatenate.22.place
  52.0 3.9 %collective-permute-done.13.down = bf16[2,8,8,1024]{3,2,1,0:T(8,128)(2,1)S(1)} collective-permute-done((bf16[2,8,8,1024]{3,2,1,0:T(8,128)(2,1)}, bf16[2,8,8,1024]{3,2,1,0:T(8,128)(2,1)S(1)}, u32[]{:S(2)}, u32[]{:S(2)}) %collective-permute-start.13) | collective-permute-done | bytes 262176 | tf_op jit(solution)/shard_map/ppermute | solution.py:131
  56.0 3.4 %collective-permute-done.11.across_near = bf16[2,8,8,1024]{3,2,1,0:T(8,128)(2,1)S(1)} collective-permute-done((bf16[2,8,8,1024]{3,2,1,0:T(8,128)(2,1)S(1)}, bf16[2,8,8,1024]{3,2,1,0:T(8,128)(2,1)S(1)}, u32[]{:S(2)}, u32[]{:S(2)}) %collective-permute-start.11) | collective-permute-done | bytes 262176 | tf_op jit(solution)/shard_map/ppermute | solution.py:131
  59.3 0.0 collective-permute-done.14.up
  59.3 0.0 collective-permute-done.12.other
  59.4 1.8 %collective-permute-start.18 = (bf16[5,8,8,1024]{3,2,1,0:T(8,128)(2,1)S(1)}, bf16[5,8,8,1024]{3,2,1,0:T(8,128)(2,1)S(1)}, u32[]{:S(2)}, u32[]{:S(2)}) collective-permute-start(bf16[5,8,8,1024]{3,2,1,0:T(8,128)(2,1)S(1)} %constant_dynamic-update-slice_fusion), channel_id=1, source_target_pairs={{0,8},{1,9},{64,72},{65,73},{128,136},{129,137},{192,200},{193,201... | collective-permute-start | bytes 1966088 | tf_op jit(solution)/shard_map/ppermute | solution.py:131
  61.2 0.3 collective-permute-start.17
  61.6 0.0 slice-start
  61.6 0.0 slice-start.1
  61.6 0.4 collective-permute-start.15
  62.0 1.7 %collective-permute-start.16 = (bf16[3,8,8,1024]{3,2,1,0:T(8,128)(2,1)S(1)}, bf16[3,8,8,1024]{3,2,1,0:T(8,128)(2,1)S(1)}, u32[]{:S(2)}, u32[]{:S(2)}) collective-permute-start(bf16[3,8,8,1024]{3,2,1,0:T(8,128)(2,1)S(1)} %pad_maximum_fusion.2), channel_id=1, source_target_pairs={{0,64},{1,65},{64,128},{65,129},{128,192},{129,193},{192,32},{193,... | collective-permute-start | bytes 1179656 | tf_op jit(solution)/shard_map/ppermute | solution.py:131
  63.7 12.5 %shard_map.109 = (bf16[256,1024]{1,0:T(8,128)(2,1)S(1)}, f32[3,2,16,8,1024]{4,3,2,1,0:T(8,128)S(1)}) custom-call(s32[25]{0:T(128)S(1)} %concatenate.22.place, bf16[3,8,8,1024]{3,2,1,0:T(8,128)(2,1)S(1)} %pad_maximum_fusion.1.near, bf16[3,8,8,1024]{3,2,1,0:T(8,128)(2,1)S(1)} %collective-permute-done.14.up, ...), custom_call_target="tpu_custom_call" | custom-call | flops 12000000000 | bytes 8388608 | tf_op jit(solution)/shard_map/pallas_call | solution.py:295
  76.3 0.0 collective-permute-done.15.down
  76.3 0.0 collective-permute-done.16.up
  76.3 0.0 collective-permute-done.18.left
  76.3 1.8 %collective-permute-done.17.right = bf16[5,8,8,1024]{3,2,1,0:T(8,128)(2,1)S(1)} collective-permute-done((bf16[5,8,8,1024]{3,2,1,0:T(8,128)(2,1)S(1)}, bf16[5,8,8,1024]{3,2,1,0:T(8,128)(2,1)S(1)}, u32[]{:S(2)}, u32[]{:S(2)}) %collective-permute-start.17) | collective-permute-done | bytes 655392 | tf_op jit(solution)/shard_map/ppermute | solution.py:131
  78.1 22.7 %shard_map.110 = bf16[16,2,4,8,4000]{4,3,2,1,0:T(8,128)(2,1)} custom-call(s32[25]{0:T(128)S(1)} %concatenate.22.place, bf16[5,8,8,1024]{3,2,1,0:T(8,128)(2,1)S(1)} %collective-permute-done.18.left, bf16[5,8,8,1024]{3,2,1,0:T(8,128)(2,1)S(1)} %collective-permute-done.17.right, bf16[3,8,8,1024]{3,2,1,0:T(8,128)(2,1)S(1)} %collective-permute-done.16.up, ...), custom_call_target="tpu_custom_call" | custom-call | flops 8388608000 | bytes 25165824 | tf_op jit(solution)/shard_map/pallas_call | solution.py:356
  (25 shorter events, 0.3 us)
Async XLA Ops:
  0.0 3.8 %copy-start.8 = (bf16[3000,256]{1,0:T(8,128)(2,1)S(1)}, bf16[3000,256]{1,0:T(8,128)(2,1)}, u32[]{:S(2)}) copy-start(bf16[3000,256]{1,0:T(8,128)(2,1)} %constant.148.clone) | copy-start | bytes 4608004
  1.9 2.8 %copy-start.7 = (bf16[3000,256]{1,0:T(8,128)(2,1)S(1)}, bf16[3000,256]{1,0:T(8,128)(2,1)}, u32[]{:S(2)}) copy-start(bf16[3000,256]{1,0:T(8,128)(2,1)} %constant.147.clone) | copy-start | bytes 4608004
  3.8 1.9 %copy-start.1 = (bf16[3000,512]{1,0:T(8,128)(2,1)S(1)}, bf16[3000,512]{1,0:T(8,128)(2,1)}, u32[]{:S(2)}) copy-start(bf16[3000,512]{1,0:T(8,128)(2,1)} %constant.157) | copy-start | bytes 9216004
  4.8 2.1 %copy-start = (bf16[3000,512]{1,0:T(8,128)(2,1)S(1)}, bf16[3000,512]{1,0:T(8,128)(2,1)}, u32[]{:S(2)}) copy-start(bf16[3000,512]{1,0:T(8,128)(2,1)} %constant.158) | copy-start | bytes 9216004
  6.9 1.2 %copy-start.2 = (f32[512,512]{1,0:T(8,128)S(1)}, f32[512,512]{1,0:T(8,128)}, u32[]{:S(2)}) copy-start(f32[512,512]{1,0:T(8,128)} %constant.150.clone) | copy-start | bytes 3145732
  6.9 1.2 %copy-start.4 = (f32[512]{0:T(512)S(1)}, f32[512]{0:T(512)}, u32[]{:S(2)}) copy-start(f32[512]{0:T(512)} %constant.159) | copy-start | bytes 6148
  6.9 2.0 %copy-start.3 = (f32[8]{0:T(128)S(1)}, f32[8]{0:T(128)}, u32[]{:S(2)}) copy-start(f32[8]{0:T(128)} %param.12) | copy-start | bytes 100
  7.5 27.9 %copy-start.6 = (s32[8]{0:T(128)S(1)}, s32[8]{0:T(128)}, u32[]{:S(2)}) copy-start(s32[8]{0:T(128)} %constant.152.clone) | copy-start | bytes 100
  8.9 42.4 %copy-start.5 = (s32[4]{0:T(128)S(1)}, s32[4]{0:T(128)}, u32[]{:S(2)}) copy-start(s32[4]{0:T(128)} %constant.153.clone) | copy-start | bytes 52
  9.0 13.6 %collective-permute-start.2 = (bf16[8,8,1024]{2,1,0:T(8,128)(2,1)S(1)}, bf16[8,8,1024]{2,1,0:T(8,128)(2,1)S(1)}, u32[]{:S(2)}, u32[]{:S(2)}) collective-permute-start(bf16[8,8,1024]{2,1,0:T(8,128)(2,1)S(1)} %fusion.9), channel_id=1, source_target_pairs={{0,4},{1,5},{64,68},{65,69},{128,132},{129,133},{192,196},{193,197... | collective-permute-start | bytes 393224 | tf_op jit(solution)/shard_map/ppermute | solution.py:131
  12.3 11.8 %collective-permute-start.1 = (bf16[8,8,1024]{2,1,0:T(8,128)(2,1)S(1)}, bf16[8,8,1024]{2,1,0:T(8,128)(2,1)S(1)}, u32[]{:S(2)}, u32[]{:S(2)}) collective-permute-start(bf16[8,8,1024]{2,1,0:T(8,128)(2,1)S(1)} %fusion.9), channel_id=1, source_target_pairs={{0,6},{1,7},{64,70},{65,71},{128,134},{129,135},{192,198},{193,199... | collective-permute-start | bytes 393224 | tf_op jit(solution)/shard_map/ppermute | solution.py:131
  13.4 10.7 %collective-permute-start = (bf16[8,8,1024]{2,1,0:T(8,128)(2,1)S(1)}, bf16[8,8,1024]{2,1,0:T(8,128)(2,1)S(1)}, u32[]{:S(2)}, u32[]{:S(2)}) collective-permute-start(bf16[8,8,1024]{2,1,0:T(8,128)(2,1)S(1)} %fusion.9), channel_id=1, source_target_pairs={{0,2},{1,3},{64,66},{65,67},{128,130},{129,131},{192,194},{193,195... | collective-permute-start | bytes 393224 | tf_op jit(solution)/shard_map/ppermute | solution.py:131
  14.4 14.4 %collective-permute-start.5 = (bf16[8,8,1024]{2,1,0:T(8,128)(2,1)S(1)}, bf16[8,8,1024]{2,1,0:T(8,128)(2,1)S(1)}, u32[]{:S(2)}, u32[]{:S(2)}) collective-permute-start(bf16[8,8,1024]{2,1,0:T(8,128)(2,1)S(1)} %get-tuple-element.72), channel_id=1, source_target_pairs={{0,96},{1,97},{64,160},{65,161},{128,224},{129,225},{192,0},{193,1... | collective-permute-start | bytes 393224 | tf_op jit(solution)/shard_map/ppermute | solution.py:131
  21.2 8.9 %collective-permute-start.4 = (bf16[8,8,1024]{2,1,0:T(8,128)(2,1)S(1)}, bf16[8,8,1024]{2,1,0:T(8,128)(2,1)S(1)}, u32[]{:S(2)}, u32[]{:S(2)}) collective-permute-start(bf16[8,8,1024]{2,1,0:T(8,128)(2,1)S(1)} %get-tuple-element.72), channel_id=1, source_target_pairs={{0,128},{1,129},{64,192},{65,193},{128,32},{129,33},{192,96},{193,... | collective-permute-start | bytes 393224 | tf_op jit(solution)/shard_map/ppermute | solution.py:131
  22.7 7.5 %collective-permute-start.3 = (bf16[8,8,1024]{2,1,0:T(8,128)(2,1)S(1)}, bf16[8,8,1024]{2,1,0:T(8,128)(2,1)S(1)}, u32[]{:S(2)}, u32[]{:S(2)}) collective-permute-start(bf16[8,8,1024]{2,1,0:T(8,128)(2,1)S(1)} %get-tuple-element.72), channel_id=1, source_target_pairs={{0,16},{1,17},{64,80},{65,81},{128,144},{129,145},{192,208},{193,2... | collective-permute-start | bytes 393224 | tf_op jit(solution)/shard_map/ppermute | solution.py:131
  30.2 14.8 %collective-permute-start.10 = (bf16[3,8,8,1024]{3,2,1,0:T(8,128)(2,1)S(1)}, bf16[3,8,8,1024]{3,2,1,0:T(8,128)(2,1)S(1)}, u32[]{:S(2)}, u32[]{:S(2)}) collective-permute-start(bf16[3,8,8,1024]{3,2,1,0:T(8,128)(2,1)S(1)} %pad_maximum_fusion.1.near), channel_id=1, source_target_pairs={{0,8},{1,9},{64,72},{65,73},{128,136},{129,137},{192,200},{193,201... | collective-permute-start | bytes 1179656 | tf_op jit(solution)/shard_map/ppermute | solution.py:131
  30.7 14.2 %collective-permute-start.9 = (bf16[3,8,8,1024]{3,2,1,0:T(8,128)(2,1)S(1)}, bf16[3,8,8,1024]{3,2,1,0:T(8,128)(2,1)S(1)}, u32[]{:S(2)}, u32[]{:S(2)}) collective-permute-start(bf16[3,8,8,1024]{3,2,1,0:T(8,128)(2,1)S(1)} %pad_maximum_fusion.1.near), channel_id=1, source_target_pairs={{0,24},{1,25},{64,88},{65,89},{128,152},{129,153},{192,216},{193,2... | collective-permute-start | bytes 1179656 | tf_op jit(solution)/shard_map/ppermute | solution.py:131
  32.4 5.9 %collective-permute-start.8 = (bf16[8,8,1024]{2,1,0:T(8,128)(2,1)S(1)}, bf16[8,8,1024]{2,1,0:T(8,128)(2,1)S(1)}, u32[]{:S(2)}, u32[]{:S(2)}) collective-permute-start(bf16[8,8,1024]{2,1,0:T(8,128)(2,1)S(1)} %get-tuple-element.65), channel_id=1, source_target_pairs={{0,192},{64,0},{128,64},{192,128},{1,193},{65,1},{129,65},{193,129... | collective-permute-start | bytes 393224 | tf_op jit(solution)/shard_map/ppermute | solution.py:135
  32.6 12.3 %collective-permute-start.7 = (bf16[8,8,1024]{2,1,0:T(8,128)(2,1)S(1)}, bf16[8,8,1024]{2,1,0:T(8,128)(2,1)S(1)}, u32[]{:S(2)}, u32[]{:S(2)}) collective-permute-start(bf16[8,8,1024]{2,1,0:T(8,128)(2,1)S(1)} %get-tuple-element.66), channel_id=1, source_target_pairs={{0,128},{64,192},{128,0},{192,64},{1,129},{65,193},{129,1},{193,65... | collective-permute-start | bytes 393224 | tf_op jit(solution)/shard_map/ppermute | solution.py:135
  35.4 9.5 %collective-permute-start.6 = (bf16[8,8,1024]{2,1,0:T(8,128)(2,1)S(1)}, bf16[8,8,1024]{2,1,0:T(8,128)(2,1)S(1)}, u32[]{:S(2)}, u32[]{:S(2)}) collective-permute-start(bf16[8,8,1024]{2,1,0:T(8,128)(2,1)S(1)} %get-tuple-element.67), channel_id=1, source_target_pairs={{0,64},{64,128},{128,192},{192,0},{1,65},{65,129},{129,193},{193,1... | collective-permute-start | bytes 393224 | tf_op jit(solution)/shard_map/ppermute | solution.py:135
  45.0 14.4 %collective-permute-start.14 = (bf16[3,8,8,1024]{3,2,1,0:T(8,128)(2,1)S(1)}, bf16[3,8,8,1024]{3,2,1,0:T(8,128)(2,1)S(1)}, u32[]{:S(2)}, u32[]{:S(2)}) collective-permute-start(bf16[3,8,8,1024]{3,2,1,0:T(8,128)(2,1)S(1)} %pad_maximum_fusion.1.near), channel_id=1, source_target_pairs={{0,64},{1,65},{64,128},{65,129},{128,192},{129,193},{192,32},{193,... | collective-permute-start | bytes 1179656 | tf_op jit(solution)/shard_map/ppermute | solution.py:131
  45.3 14.0 %collective-permute-start.12 = (bf16[4,8,8,1024]{3,2,1,0:T(8,128)(2,1)S(1)}, bf16[4,8,8,1024]{3,2,1,0:T(8,128)(2,1)S(1)}, u32[]{:S(2)}, u32[]{:S(2)}) collective-permute-start(bf16[4,8,8,1024]{3,2,1,0:T(8,128)(2,1)S(1)} %pad_maximum_fusion.mine), channel_id=1, source_target_pairs={{0,1},{1,0},{64,65},{65,64},{128,129},{129,128},{192,193},{193,192... | collective-permute-start | bytes 1572872 | tf_op jit(solution)/shard_map/ppermute | solution.py:131
  46.2 9.8 %collective-permute-start.13 = (bf16[2,8,8,1024]{3,2,1,0:T(8,128)(2,1)}, bf16[2,8,8,1024]{3,2,1,0:T(8,128)(2,1)S(1)}, u32[]{:S(2)}, u32[]{:S(2)}) collective-permute-start(bf16[2,8,8,1024]{3,2,1,0:T(8,128)(2,1)} %get-tuple-element.69), channel_id=1, source_target_pairs={{0,224},{1,225},{64,0},{65,1},{128,64},{129,65},{192,128},{193,129... | collective-permute-start | bytes 786440 | tf_op jit(solution)/shard_map/ppermute | solution.py:131
  49.4 9.9 %collective-permute-start.11 = (bf16[2,8,8,1024]{3,2,1,0:T(8,128)(2,1)S(1)}, bf16[2,8,8,1024]{3,2,1,0:T(8,128)(2,1)S(1)}, u32[]{:S(2)}, u32[]{:S(2)}) collective-permute-start(bf16[2,8,8,1024]{3,2,1,0:T(8,128)(2,1)S(1)} %get-tuple-element.70), channel_id=1, source_target_pairs={{0,16},{1,17},{64,80},{65,81},{128,144},{129,145},{192,208},{193,2... | collective-permute-start | bytes 786440 | tf_op jit(solution)/shard_map/ppermute | solution.py:131
  59.4 16.9 %collective-permute-start.18 = (bf16[5,8,8,1024]{3,2,1,0:T(8,128)(2,1)S(1)}, bf16[5,8,8,1024]{3,2,1,0:T(8,128)(2,1)S(1)}, u32[]{:S(2)}, u32[]{:S(2)}) collective-permute-start(bf16[5,8,8,1024]{3,2,1,0:T(8,128)(2,1)S(1)} %constant_dynamic-update-slice_fusion), channel_id=1, source_target_pairs={{0,8},{1,9},{64,72},{65,73},{128,136},{129,137},{192,200},{193,201... | collective-permute-start | bytes 1966088 | tf_op jit(solution)/shard_map/ppermute | solution.py:131
  61.2 17.0 %collective-permute-start.17 = (bf16[5,8,8,1024]{3,2,1,0:T(8,128)(2,1)S(1)}, bf16[5,8,8,1024]{3,2,1,0:T(8,128)(2,1)S(1)}, u32[]{:S(2)}, u32[]{:S(2)}) collective-permute-start(bf16[5,8,8,1024]{3,2,1,0:T(8,128)(2,1)S(1)} %constant_dynamic-update-slice_fusion), channel_id=1, source_target_pairs={{0,24},{1,25},{64,88},{65,89},{128,152},{129,153},{192,216},{193,2... | collective-permute-start | bytes 1966088 | tf_op jit(solution)/shard_map/ppermute | solution.py:131
  61.6 16.6 %slice-start = ((s8[8388608]{0:T(1024)(128)(4,1)}), s8[4194304]{0:T(1024)(128)(4,1)S(1)}, s32[]{:S(2)}) async-start(s8[8388608]{0:T(1024)(128)(4,1)} %bitcast.35), calls=%async_computation | async-start | bytes 8388608
  61.6 16.5 %slice-start.1 = ((s8[8388608]{0:T(1024)(128)(4,1)}), s8[4194304]{0:T(1024)(128)(4,1)S(1)}, s32[]{:S(2)}) async-start(s8[8388608]{0:T(1024)(128)(4,1)} %bitcast.35), calls=%async_computation.1 | async-start | bytes 8388608
  61.6 14.6 %collective-permute-start.15 = (bf16[2,8,8,1024]{3,2,1,0:T(8,128)(2,1)S(1)}, bf16[2,8,8,1024]{3,2,1,0:T(8,128)(2,1)S(1)}, u32[]{:S(2)}, u32[]{:S(2)}) collective-permute-start(bf16[2,8,8,1024]{3,2,1,0:T(8,128)(2,1)S(1)} %pad_maximum_fusion.4), channel_id=1, source_target_pairs={{0,224},{1,225},{64,0},{65,1},{128,64},{129,65},{192,128},{193,129... | collective-permute-start | bytes 786440 | tf_op jit(solution)/shard_map/ppermute | solution.py:131
  62.0 14.3 %collective-permute-start.16 = (bf16[3,8,8,1024]{3,2,1,0:T(8,128)(2,1)S(1)}, bf16[3,8,8,1024]{3,2,1,0:T(8,128)(2,1)S(1)}, u32[]{:S(2)}, u32[]{:S(2)}) collective-permute-start(bf16[3,8,8,1024]{3,2,1,0:T(8,128)(2,1)S(1)} %pad_maximum_fusion.2), channel_id=1, source_target_pairs={{0,64},{1,65},{64,128},{65,129},{128,192},{129,193},{192,32},{193,... | collective-permute-start | bytes 1179656 | tf_op jit(solution)/shard_map/ppermute | solution.py:131

commit v7 on v6

--- a/solution.py
+++ b/solution.py
@@ -11,6 +11,7 @@
 
 SAMPLES = 12000
 QUARTER = 3000
+QUARTER_PAD = 3072
 BINS = 512
 LAGS = 4000
 LAGS_PAD = 4096
@@ -43,6 +44,10 @@
     )
 
 
+def padded(table):
+    return bf16(np.pad(table, ((0, QUARTER_PAD - QUARTER), (0, 0))))
+
+
 def waves(bins):
     angle = PHASE * np.mod(np.arange(QUARTER)[:, None] * (bins + FIRST_BIN)[None, :], SAMPLES)
     return np.cos(angle), np.sin(angle)
@@ -50,7 +55,7 @@
 
 def even_table(bins):
     cos, sin = waves(bins)
-    return bf16(np.concatenate([cos, -sin], axis=1))
+    return padded(np.concatenate([cos, -sin], axis=1))
 
 
 def odd_table(bins):
@@ -58,7 +63,7 @@
     turn = np.where((bins + FIRST_BIN) % 4 == 1, 1.0, -1.0)[None, :]
     first = np.concatenate([cos, -sin], axis=1)
     second = np.concatenate([-turn * sin, -turn * cos], axis=1)
-    return bf16(np.concatenate([first, second], axis=0))
+    return np.concatenate([padded(first), padded(second)], axis=0)
 
 
 def lag_table():
@@ -77,40 +82,99 @@
     return mean[BINS_AT][:, BINS_AT]
 
 
-def whiten(record, weights):
-    windows, channels, length = record.shape
-    values = record.reshape(windows * channels, length).astype(jnp.float32)
-    centered = (values - jnp.mean(values, axis=1, keepdims=True)) * time_taper()[None, :]
-    centered = centered.astype(jnp.bfloat16).astype(jnp.float32)
-    part = [centered[:, QUARTER * q : QUARTER * (q + 1)] for q in range(4)]
-    sum02, dif02 = part[0] + part[2], part[0] - part[2]
-    sum13, dif13 = part[1] + part[3], part[1] - part[3]
-    even0 = (sum02 + sum13).astype(jnp.bfloat16)
-    even2 = (sum02 - sum13).astype(jnp.bfloat16)
-    odd = jnp.concatenate([dif02, dif13], axis=1).astype(jnp.bfloat16)
-
-    def product(left, table):
-        return jnp.dot(left, table, preferred_element_type=jnp.float32)
-
-    spec0 = product(even0, even_table(BINS_AT[:128]))
-    spec2 = product(even2, even_table(BINS_AT[128:256]))
-    spec1 = product(odd, odd_table(BINS_AT[256:]))
-    scale = 1.0 / math.sqrt(length)
+def whiten_kernel(
+    record, weight, taper, band, smooth, even0, even2, odd, plain, weighted, parts, table0, table2, table1, done
+):
+    fetches = [
+        pltpu.make_async_copy(source, target, done.at[n])
+        for n, (source, target) in enumerate(((even0, table0), (even2, table2), (odd, table1)))
+    ]
+    for fetch in fetches:
+        fetch.start()
+    for pair in range(4):
+        value = jnp.concatenate([record[2 * pair], record[2 * pair + 1]], axis=0)
+        value = value.astype(jnp.float32)
+        mean = jnp.sum(value, axis=1, keepdims=True) * (1.0 / SAMPLES)
+        centered = ((value - mean) * taper[...]).astype(jnp.bfloat16).astype(jnp.float32)
+        quarter = [centered[:, QUARTER * q : QUARTER * (q + 1)] for q in range(4)]
+        sum02, dif02 = quarter[0] + quarter[2], quarter[0] - quarter[2]
+        sum13, dif13 = quarter[1] + quarter[3], quarter[1] - quarter[3]
+        rows = slice(pair * 16, pair * 16 + 16)
+        for n, part in enumerate((sum02 + sum13, sum02 - sum13, dif02, dif13)):
+            parts[n, rows, :QUARTER] = part.astype(jnp.bfloat16)
+            parts[n, rows, QUARTER:] = jnp.zeros((16, QUARTER_PAD - QUARTER), jnp.bfloat16)
+
+    def product(n, table):
+        return jnp.dot(parts[n], table, preferred_element_type=jnp.float32)
+
+    fetches[0].wait()
+    spec0 = product(0, table0[...])
+    fetches[1].wait()
+    spec2 = product(1, table2[...])
+    fetches[2].wait()
+    spec1 = product(2, table1[:QUARTER_PAD]) + product(3, table1[QUARTER_PAD:])
+    scale = 1.0 / math.sqrt(SAMPLES)
     real_part = jnp.concatenate([spec0[:, :128], spec2[:, :128], spec1[:, :256]], axis=1) * scale
     imag_part = jnp.concatenate([spec0[:, 128:], spec2[:, 128:], spec1[:, 256:]], axis=1) * scale
     power = real_part * real_part + imag_part * imag_part
     smoothed = jnp.dot(
         power,
-        smoother(),
+        smooth[...],
         precision=lax.Precision.HIGHEST,
         preferred_element_type=jnp.float32,
     )
-    gain = band_taper()[BINS_AT][None, :] / jnp.sqrt(smoothed + 1e-05)
+    gain = band[...] / jnp.sqrt(smoothed + 1e-05)
     whitened = jnp.concatenate([real_part * gain, imag_part * gain], axis=1)
-    whitened = whitened.reshape(windows, channels, 2 * BINS)
-    plain = whitened.astype(jnp.bfloat16)
-    weighted = (whitened * weights[:, None, None]).astype(jnp.bfloat16)
-    return plain, weighted
+    for w in range(8):
+        rows = whitened[8 * w : 8 * w + 8]
+        plain[w] = rows.astype(jnp.bfloat16)
+        weighted[w] = (rows * weight[w]).astype(jnp.bfloat16)
+
+
+def full(shape):
+    return pl.BlockSpec(shape, lambda j: (0,) * len(shape))
+
+
+def whiten(record, weights):
+    windows, channels, length = record.shape
+    anywhere = pl.BlockSpec(memory_space=pltpu.HBM)
+    out = jax.ShapeDtypeStruct((windows, channels, 2 * BINS), jnp.bfloat16)
+    return pl.pallas_call(
+        whiten_kernel,
+        out_shape=(out, out),
+        grid=(1,),
+        in_specs=[
+            full(record.shape),
+            pl.BlockSpec(memory_space=pltpu.SMEM),
+            full((1, SAMPLES)),
+            full((1, BINS)),
+            full((BINS, BINS)),
+            anywhere,
+            anywhere,
+            anywhere,
+        ],
+        out_specs=(full(out.shape), full(out.shape)),
+        scratch_shapes=[
+            pltpu.VMEM((4, windows * channels, QUARTER_PAD), jnp.bfloat16),
+            pltpu.VMEM((QUARTER_PAD, 256), jnp.bfloat16),
+            pltpu.VMEM((QUARTER_PAD, 256), jnp.bfloat16),
+            pltpu.VMEM((2 * QUARTER_PAD, 512), jnp.bfloat16),
+            pltpu.SemaphoreType.DMA((3,)),
+        ],
+        compiler_params=pltpu.CompilerParams(vmem_limit_bytes=62 * 1024 * 1024),
+        cost_estimate=pl.CostEstimate(
+            flops=10**9, bytes_accessed=12 * 2**20, transcendentals=32768
+        ),
+    )(
+        record,
+        weights,
+        time_taper()[None, :],
+        band_taper()[BINS_AT][None, :],
+        smoother(),
+        even_table(BINS_AT[:128]),
+        even_table(BINS_AT[128:256]),
+        odd_table(BINS_AT[256:]),
+    )
 
 
 def device_at(x, y, z, core):
@@ -140,11 +204,12 @@
 
 
 def first_step(plain, weighted):
+    weighted, across = together(weighted, shift(plain, dx=2))
     return together(
         shift(weighted, dy=1),
         shift(weighted, dy=3),
         shift(weighted, dy=2),
-        shift(plain, dx=2),
+        across,
         shift(plain, dz=2),
         shift(plain, dz=-3),
     )

time: 101 us -> 101 us (level)
  Pallas kernels: 35.2 us -> 43.2 us
  matrix products: 3.81 us -> 0 us
  other arithmetic: 4.68 us -> 3.27 us
  local copies, waits for them, and re-layouts: 2.79 us -> 1.51 us
  waiting for transfers between devices: 24.8 us -> 23.6 us
    pallas_call x0 -> x1, Pallas kernels: none -> 8.05 us  [whiten(): pl.pallas_call(whiten_kernel, out_shape=(out, out), grid=(1,), in_specs=[...]
    dot_general x5 -> x0, matrix products: 3.81 us -> none  [the longest x4 3.02 us: product(): return jnp.dot(left, table, preferred_element_type=jnp.float32)]
    convert_element_type x3 -> x0, other arithmetic: 1.99 us -> none  [the longest x1 1.88 us: whiten(): centered = centered.astype(jnp.bfloat16).astype(jnp.float32)]
    reduce_sum x1 -> x0, other arithmetic: 1.84 us -> none  [whiten(): jnp.mean(values, axis=1, keepdims=True)]
    ppermute x16, waiting for transfers between devices: 15.3 us -> 14 us  [shift(): return lax.ppermute(value, AXES, pairs)]
    unnamed x23 -> x7, local copies, waits for them, and re-layouts: 1.22 us -> 0.04 us
  transfers between devices with their start and end apart: 19 -> 19, of which waited for: 7 -> 9; matrix products, arithmetic and copies ran while one was open for 2% -> 4% of each run, Pallas kernels for 12% -> 12%
where the time goes in v7:
time: 101 us
  Pallas kernels  43.2 us (43%)
  starting transfers between devices  29 us (29%)
  waiting for transfers between devices  23.6 us (23%)
  other arithmetic  3.27 us (3%)
  local copies, waits for them, and re-layouts  1.51 us (1%)
    ppermute x16, starting transfers between devices, shift(): return lax.ppermute(value, AXES, pairs)  26.4 us
    pallas_call x1, Pallas kernels, correlations(): pl.pallas_call(far_kernel, out_shape=jax.ShapeDtypeStruct((16, 2, 4, 8, L...  22.7 us
    ppermute x16, waiting for transfers between devices, shift(): return lax.ppermute(value, AXES, pairs)  14 us
    pallas_call x1, Pallas kernels, near_totals(): pl.pallas_call(near_kernel, out_shape=(jax.ShapeDtypeStruct(OWN, jnp.bflo...  12.5 us
    ppermute x3, waiting for transfers between devices, own_only(): return lax.ppermute(value, 'win', [(i, (i + k) % 4) for i in range(4)])  9.55 us
    pallas_call x1, Pallas kernels, whiten(): pl.pallas_call(whiten_kernel, out_shape=(out, out), grid=(1,), in_specs=[...  8.05 us
    ppermute x3, starting transfers between devices, own_only(): return lax.ppermute(value, 'win', [(i, (i + k) % 4) for i in range(4)])  2.61 us
  transfers between devices with their start and end apart: 19, of which 9 were waited for; matrix products, arithmetic and copies ran while one was open for 4% of the time, Pallas kernels for 12%

profile of v7, /device:TPU:6, one launch (start us, length us, event | category | flops | bytes accessed | tf_op | source)
XLA Modules:
  0.0 100.9 jit_solution(17806795684631444581)
XLA Ops:
  0.0 0.0 copy-start
  0.0 8.1 %shard_map.109 = (bf16[8,8,1024]{2,1,0:T(8,128)(2,1)}, bf16[8,8,1024]{2,1,0:T(8,128)(2,1)}) custom-call(bf16[8,8,12000]{2,1,0:T(8,128)(2,1)} %record.1, f32[8]{0:T(128)} %weight.1, f32[1,12000]{1,0:T(1,128)} %constant.137.clone.taper, f32[1,512]{1,0:T(1,128)} %constant.138.clone.band, f32[512,512]{1,0:T(8,128)} %constant.139.clone.smooth, ...), custom_call_target="tpu_custom_call" | custom-call | flops 1000000000 | bytes 12582912 | tf_op jit(solution)/shard_map/pallas_call | solution.py:142
  8.1 1.5 %collective-permute-start = (bf16[8,8,1024]{2,1,0:T(8,128)(2,1)}, bf16[8,8,1024]{2,1,0:T(8,128)(2,1)S(1)}, u32[]{:S(2)}, u32[]{:S(2)}) collective-permute-start(bf16[8,8,1024]{2,1,0:T(8,128)(2,1)} %get-tuple-element.39), channel_id=1, source_target_pairs={{0,16},{1,17},{64,80},{65,81},{128,144},{129,145},{192,208},{193,2... | collective-permute-start | bytes 393224 | tf_op jit(solution)/shard_map/ppermute | solution.py:195
  9.6 6.7 %collective-permute-start.5 = (bf16[8,8,1024]{2,1,0:T(8,128)(2,1)}, bf16[8,8,1024]{2,1,0:T(8,128)(2,1)S(1)}, u32[]{:S(2)}, u32[]{:S(2)}) collective-permute-start(bf16[8,8,1024]{2,1,0:T(8,128)(2,1)} %get-tuple-element.39), channel_id=1, source_target_pairs={{0,96},{1,97},{64,160},{65,161},{128,224},{129,225},{192,0},{193,1... | collective-permute-start | bytes 393224 | tf_op jit(solution)/shard_map/ppermute | solution.py:195
  16.3 1.5 %collective-permute-start.4 = (bf16[8,8,1024]{2,1,0:T(8,128)(2,1)}, bf16[8,8,1024]{2,1,0:T(8,128)(2,1)S(1)}, u32[]{:S(2)}, u32[]{:S(2)}) collective-permute-start(bf16[8,8,1024]{2,1,0:T(8,128)(2,1)} %get-tuple-element.39), channel_id=1, source_target_pairs={{0,128},{1,129},{64,192},{65,193},{128,32},{129,33},{192,96},{193,... | collective-permute-start | bytes 393224 | tf_op jit(solution)/shard_map/ppermute | solution.py:195
  17.8 0.0 collective-permute-done.across
  17.8 3.2 %collective-permute-start.3 = (bf16[8,8,1024]{2,1,0:T(8,128)(2,1)}, bf16[8,8,1024]{2,1,0:T(8,128)(2,1)S(1)}, u32[]{:S(2)}, u32[]{:S(2)}) collective-permute-start(bf16[8,8,1024]{2,1,0:T(8,128)(2,1)} %get-tuple-element.40), channel_id=1, source_target_pairs={{0,4},{1,5},{64,68},{65,69},{128,132},{129,133},{192,196},{193,197... | collective-permute-start | bytes 393224 | tf_op jit(solution)/shard_map/ppermute | solution.py:195
  21.0 1.1 %collective-permute-start.2 = (bf16[8,8,1024]{2,1,0:T(8,128)(2,1)}, bf16[8,8,1024]{2,1,0:T(8,128)(2,1)S(1)}, u32[]{:S(2)}, u32[]{:S(2)}) collective-permute-start(bf16[8,8,1024]{2,1,0:T(8,128)(2,1)} %get-tuple-element.40), channel_id=1, source_target_pairs={{0,6},{1,7},{64,70},{65,71},{128,134},{129,135},{192,198},{193,199... | collective-permute-start | bytes 393224 | tf_op jit(solution)/shard_map/ppermute | solution.py:195
  22.0 1.0 collective-permute-start.1
  23.0 1.7 %collective-permute-done.5 = bf16[8,8,1024]{2,1,0:T(8,128)(2,1)S(1)} collective-permute-done((bf16[8,8,1024]{2,1,0:T(8,128)(2,1)}, bf16[8,8,1024]{2,1,0:T(8,128)(2,1)S(1)}, u32[]{:S(2)}, u32[]{:S(2)}) %collective-permute-start.5) | collective-permute-done | bytes 131104 | tf_op jit(solution)/shard_map/ppermute | solution.py:195
  24.7 1.2 %collective-permute-done.4 = bf16[8,8,1024]{2,1,0:T(8,128)(2,1)S(1)} collective-permute-done((bf16[8,8,1024]{2,1,0:T(8,128)(2,1)}, bf16[8,8,1024]{2,1,0:T(8,128)(2,1)S(1)}, u32[]{:S(2)}, u32[]{:S(2)}) %collective-permute-start.4) | collective-permute-done | bytes 131104 | tf_op jit(solution)/shard_map/ppermute | solution.py:195
  25.9 0.0 collective-permute-done.3
  25.9 1.1 %collective-permute-done.2 = bf16[8,8,1024]{2,1,0:T(8,128)(2,1)S(1)} collective-permute-done((bf16[8,8,1024]{2,1,0:T(8,128)(2,1)}, bf16[8,8,1024]{2,1,0:T(8,128)(2,1)S(1)}, u32[]{:S(2)}, u32[]{:S(2)}) %collective-permute-start.2) | collective-permute-done | bytes 131104 | tf_op jit(solution)/shard_map/ppermute | solution.py:195
  27.0 1.4 %collective-permute-done.1 = bf16[8,8,1024]{2,1,0:T(8,128)(2,1)S(1)} collective-permute-done((bf16[8,8,1024]{2,1,0:T(8,128)(2,1)}, bf16[8,8,1024]{2,1,0:T(8,128)(2,1)S(1)}, u32[]{:S(2)}, u32[]{:S(2)}) %collective-permute-start.1) | collective-permute-done | bytes 131104 | tf_op jit(solution)/shard_map/ppermute | solution.py:195
  28.4 0.9 pad_maximum_fusion.1.near
  29.4 2.2 %collective-permute-start.10 = (bf16[3,8,8,1024]{3,2,1,0:T(8,128)(2,1)S(1)}, bf16[3,8,8,1024]{3,2,1,0:T(8,128)(2,1)S(1)}, u32[]{:S(2)}, u32[]{:S(2)}) collective-permute-start(bf16[3,8,8,1024]{3,2,1,0:T(8,128)(2,1)S(1)} %pad_maximum_fusion.1.near), channel_id=1, source_target_pairs={{0,8},{1,9},{64,72},{65,73},{128,136},{129,137},{192,200},{193,201... | collective-permute-start | bytes 1179656 | tf_op jit(solution)/shard_map/ppermute | solution.py:195
  31.6 0.0 collective-permute-start.9
  31.6 1.0 select_select_fusion
  32.5 1.9 %collective-permute-start.8 = (bf16[8,8,1024]{2,1,0:T(8,128)(2,1)S(1)}, bf16[8,8,1024]{2,1,0:T(8,128)(2,1)S(1)}, u32[]{:S(2)}, u32[]{:S(2)}) collective-permute-start(bf16[8,8,1024]{2,1,0:T(8,128)(2,1)S(1)} %get-tuple-element.73), channel_id=1, source_target_pairs={{0,192},{64,0},{128,64},{192,128},{1,193},{65,1},{129,65},{193,129... | collective-permute-start | bytes 393224 | tf_op jit(solution)/shard_map/ppermute | solution.py:199
  34.5 0.0 collective-permute-start.7
  34.5 0.7 collective-permute-start.6
  35.1 0.0 copy-done
  35.2 4.5 %collective-permute-done.8 = bf16[8,8,1024]{2,1,0:T(8,128)(2,1)S(1)} collective-permute-done((bf16[8,8,1024]{2,1,0:T(8,128)(2,1)S(1)}, bf16[8,8,1024]{2,1,0:T(8,128)(2,1)S(1)}, u32[]{:S(2)}, u32[]{:S(2)}) %collective-permute-start.8) | collective-permute-done | bytes 131104 | tf_op jit(solution)/shard_map/ppermute | solution.py:199
  39.6 5.1 %collective-permute-done.7 = bf16[8,8,1024]{2,1,0:T(8,128)(2,1)S(1)} collective-permute-done((bf16[8,8,1024]{2,1,0:T(8,128)(2,1)S(1)}, bf16[8,8,1024]{2,1,0:T(8,128)(2,1)S(1)}, u32[]{:S(2)}, u32[]{:S(2)}) %collective-permute-start.7) | collective-permute-done | bytes 131104 | tf_op jit(solution)/shard_map/ppermute | solution.py:199
  44.7 0.0 collective-permute-done.6
  44.7 0.0 collective-permute-done.10.left
  44.7 0.0 collective-permute-done.9.right
  44.7 0.3 collective-permute-start.14
  45.0 0.1 pad_maximum_fusion.mine
  45.1 0.1 collective-permute-start.12
  45.2 0.7 fusion.3
  45.9 3.2 %collective-permute-start.13 = (bf16[2,8,8,1024]{3,2,1,0:T(8,128)(2,1)}, bf16[2,8,8,1024]{3,2,1,0:T(8,128)(2,1)S(1)}, u32[]{:S(2)}, u32[]{:S(2)}) collective-permute-start(bf16[2,8,8,1024]{3,2,1,0:T(8,128)(2,1)} %get-tuple-element.77), channel_id=1, source_target_pairs={{0,224},{1,225},{64,0},{65,1},{128,64},{129,65},{192,128},{193,129... | collective-permute-start | bytes 786440 | tf_op jit(solution)/shard_map/ppermute | solution.py:195
  49.1 1.5 %collective-permute-start.11 = (bf16[2,8,8,1024]{3,2,1,0:T(8,128)(2,1)S(1)}, bf16[2,8,8,1024]{3,2,1,0:T(8,128)(2,1)S(1)}, u32[]{:S(2)}, u32[]{:S(2)}) collective-permute-start(bf16[2,8,8,1024]{3,2,1,0:T(8,128)(2,1)S(1)} %get-tuple-element.78), channel_id=1, source_target_pairs={{0,16},{1,17},{64,80},{65,81},{128,144},{129,145},{192,208},{193,2... | collective-permute-start | bytes 786440 | tf_op jit(solution)/shard_map/ppermute | solution.py:195
  50.7 0.5 and_select_fusion.2
  51.2 0.7 and_select_fusion
  51.9 0.7 concatenate.9.place
  52.6 3.1 %collective-permute-done.13.down = bf16[2,8,8,1024]{3,2,1,0:T(8,128)(2,1)S(1)} collective-permute-done((bf16[2,8,8,1024]{3,2,1,0:T(8,128)(2,1)}, bf16[2,8,8,1024]{3,2,1,0:T(8,128)(2,1)S(1)}, u32[]{:S(2)}, u32[]{:S(2)}) %collective-permute-start.13) | collective-permute-done | bytes 262176 | tf_op jit(solution)/shard_map/ppermute | solution.py:195
  55.7 3.4 %collective-permute-done.11.across_near = bf16[2,8,8,1024]{3,2,1,0:T(8,128)(2,1)S(1)} collective-permute-done((bf16[2,8,8,1024]{3,2,1,0:T(8,128)(2,1)S(1)}, bf16[2,8,8,1024]{3,2,1,0:T(8,128)(2,1)S(1)}, u32[]{:S(2)}, u32[]{:S(2)}) %collective-permute-start.11) | collective-permute-done | bytes 262176 | tf_op jit(solution)/shard_map/ppermute | solution.py:195
  59.1 0.0 collective-permute-done.14.up
  59.1 0.0 collective-permute-done.12.other
  59.1 2.0 %collective-permute-start.18 = (bf16[5,8,8,1024]{3,2,1,0:T(8,128)(2,1)S(1)}, bf16[5,8,8,1024]{3,2,1,0:T(8,128)(2,1)S(1)}, u32[]{:S(2)}, u32[]{:S(2)}) collective-permute-start(bf16[5,8,8,1024]{3,2,1,0:T(8,128)(2,1)S(1)} %constant_dynamic-update-slice_fusion), channel_id=1, source_target_pairs={{0,8},{1,9},{64,72},{65,73},{128,136},{129,137},{192,200},{193,201... | collective-permute-start | bytes 1966088 | tf_op jit(solution)/shard_map/ppermute | solution.py:195
  61.1 0.1 collective-permute-start.17
  61.3 0.0 slice-start
  61.3 0.0 slice-start.1
  61.4 1.3 %collective-permute-start.15 = (bf16[2,8,8,1024]{3,2,1,0:T(8,128)(2,1)S(1)}, bf16[2,8,8,1024]{3,2,1,0:T(8,128)(2,1)S(1)}, u32[]{:S(2)}, u32[]{:S(2)}) collective-permute-start(bf16[2,8,8,1024]{3,2,1,0:T(8,128)(2,1)S(1)} %pad_maximum_fusion.3), channel_id=1, source_target_pairs={{0,224},{1,225},{64,0},{65,1},{128,64},{129,65},{192,128},{193,129... | collective-permute-start | bytes 786440 | tf_op jit(solution)/shard_map/ppermute | solution.py:195
  62.7 0.8 collective-permute-start.16
  63.5 12.5 %shard_map.110 = (bf16[256,1024]{1,0:T(8,128)(2,1)S(1)}, f32[3,2,16,8,1024]{4,3,2,1,0:T(8,128)S(1)}) custom-call(s32[25]{0:T(128)S(1)} %concatenate.9.place, bf16[3,8,8,1024]{3,2,1,0:T(8,128)(2,1)S(1)} %pad_maximum_fusion.1.near, bf16[3,8,8,1024]{3,2,1,0:T(8,128)(2,1)S(1)} %collective-permute-done.14.up, ...), custom_call_target="tpu_custom_call" | custom-call | flops 12000000000 | bytes 8388608 | tf_op jit(solution)/shard_map/pallas_call | solution.py:360
  76.0 0.0 collective-permute-done.15.down
  76.0 0.0 collective-permute-done.16.up
  76.0 0.0 collective-permute-done.18.left
  76.0 2.1 %collective-permute-done.17.right = bf16[5,8,8,1024]{3,2,1,0:T(8,128)(2,1)S(1)} collective-permute-done((bf16[5,8,8,1024]{3,2,1,0:T(8,128)(2,1)S(1)}, bf16[5,8,8,1024]{3,2,1,0:T(8,128)(2,1)S(1)}, u32[]{:S(2)}, u32[]{:S(2)}) %collective-permute-start.17) | collective-permute-done | bytes 655392 | tf_op jit(solution)/shard_map/ppermute | solution.py:195
  78.1 0.0 slice-done
  78.1 0.0 slice-done.1
  78.1 22.7 %shard_map.111 = bf16[16,2,4,8,4000]{4,3,2,1,0:T(8,128)(2,1)} custom-call(s32[25]{0:T(128)S(1)} %concatenate.9.place, bf16[5,8,8,1024]{3,2,1,0:T(8,128)(2,1)S(1)} %collective-permute-done.18.left, bf16[5,8,8,1024]{3,2,1,0:T(8,128)(2,1)S(1)} %collective-permute-done.17.right, bf16[3,8,8,1024]{3,2,1,0:T(8,128)(2,1)S(1)} %collective-permute-done.16.up, ...), custom_call_target="tpu_custom_call" | custom-call | flops 8388608000 | bytes 25165824 | tf_op jit(solution)/shard_map/pallas_call | solution.py:421
  (7 shorter events, 0.1 us)
Async XLA Ops:
  0.0 35.1 %copy-start = (s32[8]{0:T(128)S(1)}, s32[8]{0:T(128)}, u32[]{:S(2)}) copy-start(s32[8]{0:T(128)} %constant.143.clone) | copy-start | bytes 100
  8.1 9.7 %collective-permute-start = (bf16[8,8,1024]{2,1,0:T(8,128)(2,1)}, bf16[8,8,1024]{2,1,0:T(8,128)(2,1)S(1)}, u32[]{:S(2)}, u32[]{:S(2)}) collective-permute-start(bf16[8,8,1024]{2,1,0:T(8,128)(2,1)} %get-tuple-element.39), channel_id=1, source_target_pairs={{0,16},{1,17},{64,80},{65,81},{128,144},{129,145},{192,208},{193,2... | collective-permute-start | bytes 393224 | tf_op jit(solution)/shard_map/ppermute | solution.py:195
  9.6 15.2 %collective-permute-start.5 = (bf16[8,8,1024]{2,1,0:T(8,128)(2,1)}, bf16[8,8,1024]{2,1,0:T(8,128)(2,1)S(1)}, u32[]{:S(2)}, u32[]{:S(2)}) collective-permute-start(bf16[8,8,1024]{2,1,0:T(8,128)(2,1)} %get-tuple-element.39), channel_id=1, source_target_pairs={{0,96},{1,97},{64,160},{65,161},{128,224},{129,225},{192,0},{193,1... | collective-permute-start | bytes 393224 | tf_op jit(solution)/shard_map/ppermute | solution.py:195
  16.3 9.6 %collective-permute-start.4 = (bf16[8,8,1024]{2,1,0:T(8,128)(2,1)}, bf16[8,8,1024]{2,1,0:T(8,128)(2,1)S(1)}, u32[]{:S(2)}, u32[]{:S(2)}) collective-permute-start(bf16[8,8,1024]{2,1,0:T(8,128)(2,1)} %get-tuple-element.39), channel_id=1, source_target_pairs={{0,128},{1,129},{64,192},{65,193},{128,32},{129,33},{192,96},{193,... | collective-permute-start | bytes 393224 | tf_op jit(solution)/shard_map/ppermute | solution.py:195
  17.8 8.1 %collective-permute-start.3 = (bf16[8,8,1024]{2,1,0:T(8,128)(2,1)}, bf16[8,8,1024]{2,1,0:T(8,128)(2,1)S(1)}, u32[]{:S(2)}, u32[]{:S(2)}) collective-permute-start(bf16[8,8,1024]{2,1,0:T(8,128)(2,1)} %get-tuple-element.40), channel_id=1, source_target_pairs={{0,4},{1,5},{64,68},{65,69},{128,132},{129,133},{192,196},{193,197... | collective-permute-start | bytes 393224 | tf_op jit(solution)/shard_map/ppermute | solution.py:195
  21.0 6.1 %collective-permute-start.2 = (bf16[8,8,1024]{2,1,0:T(8,128)(2,1)}, bf16[8,8,1024]{2,1,0:T(8,128)(2,1)S(1)}, u32[]{:S(2)}, u32[]{:S(2)}) collective-permute-start(bf16[8,8,1024]{2,1,0:T(8,128)(2,1)} %get-tuple-element.40), channel_id=1, source_target_pairs={{0,6},{1,7},{64,70},{65,71},{128,134},{129,135},{192,198},{193,199... | collective-permute-start | bytes 393224 | tf_op jit(solution)/shard_map/ppermute | solution.py:195
  22.0 6.4 %collective-permute-start.1 = (bf16[8,8,1024]{2,1,0:T(8,128)(2,1)}, bf16[8,8,1024]{2,1,0:T(8,128)(2,1)S(1)}, u32[]{:S(2)}, u32[]{:S(2)}) collective-permute-start(bf16[8,8,1024]{2,1,0:T(8,128)(2,1)} %get-tuple-element.40), channel_id=1, source_target_pairs={{0,2},{1,3},{64,66},{65,67},{128,130},{129,131},{192,194},{193,195... | collective-permute-start | bytes 393224 | tf_op jit(solution)/shard_map/ppermute | solution.py:195
  29.4 15.3 %collective-permute-start.10 = (bf16[3,8,8,1024]{3,2,1,0:T(8,128)(2,1)S(1)}, bf16[3,8,8,1024]{3,2,1,0:T(8,128)(2,1)S(1)}, u32[]{:S(2)}, u32[]{:S(2)}) collective-permute-start(bf16[3,8,8,1024]{3,2,1,0:T(8,128)(2,1)S(1)} %pad_maximum_fusion.1.near), channel_id=1, source_target_pairs={{0,8},{1,9},{64,72},{65,73},{128,136},{129,137},{192,200},{193,201... | collective-permute-start | bytes 1179656 | tf_op jit(solution)/shard_map/ppermute | solution.py:195
  31.6 13.2 %collective-permute-start.9 = (bf16[3,8,8,1024]{3,2,1,0:T(8,128)(2,1)S(1)}, bf16[3,8,8,1024]{3,2,1,0:T(8,128)(2,1)S(1)}, u32[]{:S(2)}, u32[]{:S(2)}) collective-permute-start(bf16[3,8,8,1024]{3,2,1,0:T(8,128)(2,1)S(1)} %pad_maximum_fusion.1.near), channel_id=1, source_target_pairs={{0,24},{1,25},{64,88},{65,89},{128,152},{129,153},{192,216},{193,2... | collective-permute-start | bytes 1179656 | tf_op jit(solution)/shard_map/ppermute | solution.py:195
  32.5 7.1 %collective-permute-start.8 = (bf16[8,8,1024]{2,1,0:T(8,128)(2,1)S(1)}, bf16[8,8,1024]{2,1,0:T(8,128)(2,1)S(1)}, u32[]{:S(2)}, u32[]{:S(2)}) collective-permute-start(bf16[8,8,1024]{2,1,0:T(8,128)(2,1)S(1)} %get-tuple-element.73), channel_id=1, source_target_pairs={{0,192},{64,0},{128,64},{192,128},{1,193},{65,1},{129,65},{193,129... | collective-permute-start | bytes 393224 | tf_op jit(solution)/shard_map/ppermute | solution.py:199
  34.5 10.2 %collective-permute-start.7 = (bf16[8,8,1024]{2,1,0:T(8,128)(2,1)S(1)}, bf16[8,8,1024]{2,1,0:T(8,128)(2,1)S(1)}, u32[]{:S(2)}, u32[]{:S(2)}) collective-permute-start(bf16[8,8,1024]{2,1,0:T(8,128)(2,1)S(1)} %get-tuple-element.74), channel_id=1, source_target_pairs={{0,128},{64,192},{128,0},{192,64},{1,129},{65,193},{129,1},{193,65... | collective-permute-start | bytes 393224 | tf_op jit(solution)/shard_map/ppermute | solution.py:199
  34.5 10.2 %collective-permute-start.6 = (bf16[8,8,1024]{2,1,0:T(8,128)(2,1)S(1)}, bf16[8,8,1024]{2,1,0:T(8,128)(2,1)S(1)}, u32[]{:S(2)}, u32[]{:S(2)}) collective-permute-start(bf16[8,8,1024]{2,1,0:T(8,128)(2,1)S(1)} %get-tuple-element.75), channel_id=1, source_target_pairs={{0,64},{64,128},{128,192},{192,0},{1,65},{65,129},{129,193},{193,1... | collective-permute-start | bytes 393224 | tf_op jit(solution)/shard_map/ppermute | solution.py:199
  44.7 14.3 %collective-permute-start.14 = (bf16[3,8,8,1024]{3,2,1,0:T(8,128)(2,1)S(1)}, bf16[3,8,8,1024]{3,2,1,0:T(8,128)(2,1)S(1)}, u32[]{:S(2)}, u32[]{:S(2)}) collective-permute-start(bf16[3,8,8,1024]{3,2,1,0:T(8,128)(2,1)S(1)} %pad_maximum_fusion.1.near), channel_id=1, source_target_pairs={{0,64},{1,65},{64,128},{65,129},{128,192},{129,193},{192,32},{193,... | collective-permute-start | bytes 1179656 | tf_op jit(solution)/shard_map/ppermute | solution.py:195
  45.1 14.0 %collective-permute-start.12 = (bf16[4,8,8,1024]{3,2,1,0:T(8,128)(2,1)S(1)}, bf16[4,8,8,1024]{3,2,1,0:T(8,128)(2,1)S(1)}, u32[]{:S(2)}, u32[]{:S(2)}) collective-permute-start(bf16[4,8,8,1024]{3,2,1,0:T(8,128)(2,1)S(1)} %pad_maximum_fusion.mine), channel_id=1, source_target_pairs={{0,1},{1,0},{64,65},{65,64},{128,129},{129,128},{192,193},{193,192... | collective-permute-start | bytes 1572872 | tf_op jit(solution)/shard_map/ppermute | solution.py:195
  45.9 9.8 %collective-permute-start.13 = (bf16[2,8,8,1024]{3,2,1,0:T(8,128)(2,1)}, bf16[2,8,8,1024]{3,2,1,0:T(8,128)(2,1)S(1)}, u32[]{:S(2)}, u32[]{:S(2)}) collective-permute-start(bf16[2,8,8,1024]{3,2,1,0:T(8,128)(2,1)} %get-tuple-element.77), channel_id=1, source_target_pairs={{0,224},{1,225},{64,0},{65,1},{128,64},{129,65},{192,128},{193,129... | collective-permute-start | bytes 786440 | tf_op jit(solution)/shard_map/ppermute | solution.py:195
  49.1 9.9 %collective-permute-start.11 = (bf16[2,8,8,1024]{3,2,1,0:T(8,128)(2,1)S(1)}, bf16[2,8,8,1024]{3,2,1,0:T(8,128)(2,1)S(1)}, u32[]{:S(2)}, u32[]{:S(2)}) collective-permute-start(bf16[2,8,8,1024]{3,2,1,0:T(8,128)(2,1)S(1)} %get-tuple-element.78), channel_id=1, source_target_pairs={{0,16},{1,17},{64,80},{65,81},{128,144},{129,145},{192,208},{193,2... | collective-permute-start | bytes 786440 | tf_op jit(solution)/shard_map/ppermute | solution.py:195
  59.1 16.9 %collective-permute-start.18 = (bf16[5,8,8,1024]{3,2,1,0:T(8,128)(2,1)S(1)}, bf16[5,8,8,1024]{3,2,1,0:T(8,128)(2,1)S(1)}, u32[]{:S(2)}, u32[]{:S(2)}) collective-permute-start(bf16[5,8,8,1024]{3,2,1,0:T(8,128)(2,1)S(1)} %constant_dynamic-update-slice_fusion), channel_id=1, source_target_pairs={{0,8},{1,9},{64,72},{65,73},{128,136},{129,137},{192,200},{193,201... | collective-permute-start | bytes 1966088 | tf_op jit(solution)/shard_map/ppermute | solution.py:195
  61.1 17.0 %collective-permute-start.17 = (bf16[5,8,8,1024]{3,2,1,0:T(8,128)(2,1)S(1)}, bf16[5,8,8,1024]{3,2,1,0:T(8,128)(2,1)S(1)}, u32[]{:S(2)}, u32[]{:S(2)}) collective-permute-start(bf16[5,8,8,1024]{3,2,1,0:T(8,128)(2,1)S(1)} %constant_dynamic-update-slice_fusion), channel_id=1, source_target_pairs={{0,24},{1,25},{64,88},{65,89},{128,152},{129,153},{192,216},{193,2... | collective-permute-start | bytes 1966088 | tf_op jit(solution)/shard_map/ppermute | solution.py:195
  61.3 16.8 %slice-start = ((s8[8388608]{0:T(1024)(128)(4,1)}), s8[4194304]{0:T(1024)(128)(4,1)S(1)}, s32[]{:S(2)}) async-start(s8[8388608]{0:T(1024)(128)(4,1)} %bitcast.12), calls=%async_computation | async-start | bytes 8388608
  61.3 16.8 %slice-start.1 = ((s8[8388608]{0:T(1024)(128)(4,1)}), s8[4194304]{0:T(1024)(128)(4,1)S(1)}, s32[]{:S(2)}) async-start(s8[8388608]{0:T(1024)(128)(4,1)} %bitcast.12), calls=%async_computation.1 | async-start | bytes 8388608
  61.4 14.6 %collective-permute-start.15 = (bf16[2,8,8,1024]{3,2,1,0:T(8,128)(2,1)S(1)}, bf16[2,8,8,1024]{3,2,1,0:T(8,128)(2,1)S(1)}, u32[]{:S(2)}, u32[]{:S(2)}) collective-permute-start(bf16[2,8,8,1024]{3,2,1,0:T(8,128)(2,1)S(1)} %pad_maximum_fusion.3), channel_id=1, source_target_pairs={{0,224},{1,225},{64,0},{65,1},{128,64},{129,65},{192,128},{193,129... | collective-permute-start | bytes 786440 | tf_op jit(solution)/shard_map/ppermute | solution.py:195
  62.7 13.3 %collective-permute-start.16 = (bf16[3,8,8,1024]{3,2,1,0:T(8,128)(2,1)S(1)}, bf16[3,8,8,1024]{3,2,1,0:T(8,128)(2,1)S(1)}, u32[]{:S(2)}, u32[]{:S(2)}) collective-permute-start(bf16[3,8,8,1024]{3,2,1,0:T(8,128)(2,1)S(1)} %pad_maximum_fusion.2), channel_id=1, source_target_pairs={{0,64},{1,65},{64,128},{65,129},{128,192},{129,193},{192,32},{193,... | collective-permute-start | bytes 1179656 | tf_op jit(solution)/shard_map/ppermute | solution.py:195

commit v8 on v7

--- a/solution.py
+++ b/solution.py
@@ -241,30 +241,22 @@
 def third_step(arrived):
     *rows, right, left, near, across = arrived
     mine = jnp.stack(rows)
-    across_near, other, down, up, *rest = together(
-        shift(near[1:], dx=2),
-        shift(mine, dcore=1),
-        shift(near[:2], dz=-1),
-        shift(near, dz=1),
-        mine,
-        near,
-        left,
-        right,
-        across,
-    )
-    mine, near, left, right, across = rest
+    across_near = shift(near[1:], dx=2)
+    other = shift(mine, dcore=1)
+    down = shift(near[:2], dz=-1)
+    up = shift(near, dz=1)
     return near, up, down, left, right, across, across_near, mine, other
 
 
-def fourth_step(up, down, across, across_near):
-    far = jnp.concatenate([up, down])
-    down_out, up_out, right, left = together(
-        shift(jnp.stack([across, across_near[0]]), dz=-1),
+def fourth_step(up, down, left, right, across, across_near):
+    far = jnp.concatenate([up, down[1:]])
+    down_out, up_out, right_far, left_far = together(
+        shift(jnp.stack([across, across_near[0], left[0], right[0]]), dz=-1),
         shift(jnp.concatenate([across[None], across_near]), dz=1),
         shift(far, dx=-1),
         shift(far, dx=1),
     )
-    return left, right, up_out, down_out
+    return left_far, right_far, up_out, down_out
 
 
 NEAR = (0, 3, -2)
@@ -314,9 +306,9 @@
             total[high, core * 8 + base + i, :, lane_im] += r - p + q
 
 
-def add_blocks(blocks, place, first, rows, total):
+def add_blocks(blocks, place, rows, total):
     def tile_step(tile, carry):
-        for n, block in enumerate(blocks, first):
+        for n, block in blocks:
             add_cross(tile, block, place[HIGH + n], place[GROUP + n], rows, total)
         return carry
 
@@ -329,56 +321,110 @@
         target[pl.ds(i * 16, 16), :] = rows.astype(jnp.bfloat16)
 
 
-def parts_of(*refs):
-    return [ref.at[n] for ref in refs for n in range(ref.shape[0])]
-
-
-def near_kernel(
-    place, near, up, down, left, right, across, across_near, mine, other, own, total, z_re, z_im, z_sum, sums
-):
+def parts_of(first, *refs):
+    return list(enumerate([ref.at[n] for ref in refs for n in range(ref.shape[0])], first))
+
+
+def lag_product(stack, table, out):
+    for tile in range(8):
+        start = tile * 512
+        keep = min(512, LAGS - start)
+        value = jnp.dot(
+            stack[...], table[:, start : start + 512], preferred_element_type=jnp.float32
+        )
+        value = value.reshape(16, 2, 1, 8, 512).astype(jnp.bfloat16)
+        out[:, :, :, :, start : start + keep] = value[..., :keep]
+
+
+TOTAL = (2, 16, 8, 2 * BINS)
+CORR = (16, 2, 4, 8, LAGS)
+ROW_SCRATCH = [pltpu.VMEM((32, 2, 4, 8, 128), jnp.float32)] * 3
+LAG_SCRATCH = [
+    pltpu.VMEM((256, 2 * BINS), jnp.bfloat16),
+    pltpu.VMEM((2 * BINS, LAGS_PAD), jnp.bfloat16),
+    pltpu.SemaphoreType.DMA(()),
+]
+
+
+def whole(shape):
+    return pl.BlockSpec(shape, lambda j, place: (0,) * len(shape))
+
+
+def near_kernel(place, near, left, right, across, mine, other, kept, sides, z_re, z_im, z_sum):
     rows = (z_re, z_im, z_sum)
     load_rows(place, mine, other, *rows)
-    sums[...] = jnp.zeros_like(sums)
-    total[...] = jnp.zeros_like(total)
-    add_blocks(parts_of(near, up, down), place, 0, rows, sums)
-    settle(sums, own)
-    sides = (parts_of(left), parts_of(right), [across, *parts_of(across_near)])
-    for n, blocks in enumerate(sides):
-        add_blocks(blocks, place, 0, rows, total.at[n])
-
-
-TOTAL = (2, 16, 8, 2 * BINS)
-OWN = (256, 2 * BINS)
-ROW_SCRATCH = [pltpu.VMEM((32, 2, 4, 8, 128), jnp.float32)] * 3
-
-
-def whole(shape):
-    return pl.BlockSpec(shape, lambda j, place: (0,) * len(shape))
+    kept[...] = jnp.zeros_like(kept)
+    sides[...] = jnp.zeros_like(sides)
+    add_blocks(parts_of(0, near), place, rows, kept.at[0])
+    add_blocks([(0, across)], place, rows, kept.at[1])
+    add_blocks(parts_of(0, left), place, rows, sides.at[0])
+    add_blocks(parts_of(0, right), place, rows, sides.at[1])
 
 
 def near_totals(place, *blocks):
+    two = (2, *TOTAL)
     return pl.pallas_call(
         near_kernel,
-        out_shape=(
-            jax.ShapeDtypeStruct(OWN, jnp.bfloat16),
-            jax.ShapeDtypeStruct((3, *TOTAL), jnp.float32),
-        ),
+        out_shape=(jax.ShapeDtypeStruct(two, jnp.float32),) * 2,
         grid_spec=pltpu.PrefetchScalarGridSpec(
             num_scalar_prefetch=1,
             grid=(1,),
             in_specs=[whole(block.shape) for block in blocks],
-            out_specs=(whole(OWN), whole((3, *TOTAL))),
-            scratch_shapes=[*ROW_SCRATCH, pltpu.VMEM(TOTAL, jnp.float32)],
+            out_specs=(whole(two), whole(two)),
+            scratch_shapes=ROW_SCRATCH,
         ),
         compiler_params=pltpu.CompilerParams(vmem_limit_bytes=28 * 1024 * 1024),
         cost_estimate=pl.CostEstimate(
-            flops=12 * 10**9, bytes_accessed=8 * 2**20, transcendentals=0
+            flops=8 * 10**9, bytes_accessed=8 * 2**20, transcendentals=0
         ),
     )(place, *blocks)
 
 
+def own_kernel(
+    place, kept, up, down, across_near, mine, other, source, out, sum_across, z_re, z_im, z_sum, total, now, table, ready
+):
+    fetch = pltpu.make_async_copy(source, table, ready)
+    fetch.start()
+    rows = (z_re, z_im, z_sum)
+    load_rows(place, mine, other, *rows)
+    total[...] = kept[0]
+    add_blocks(parts_of(3, up, down), place, rows, total)
+    settle(total, now)
+    sum_across[...] = kept[1]
+    add_blocks(parts_of(1, across_near), place, rows, sum_across)
+    fetch.wait()
+    lag_product(now, table, out)
+
+
+def own_correlations(place, *blocks):
+    return pl.pallas_call(
+        own_kernel,
+        out_shape=(
+            jax.ShapeDtypeStruct(CORR, jnp.bfloat16),
+            jax.ShapeDtypeStruct(TOTAL, jnp.float32),
+        ),
+        grid_spec=pltpu.PrefetchScalarGridSpec(
+            num_scalar_prefetch=1,
+            grid=(1,),
+            in_specs=[
+                *[whole(block.shape) for block in blocks],
+                pl.BlockSpec(memory_space=pl.ANY),
+            ],
+            out_specs=(
+                pl.BlockSpec((16, 2, 1, 8, LAGS), lambda j, place: (0, 0, place[j], 0, 0)),
+                whole(TOTAL),
+            ),
+            scratch_shapes=[*ROW_SCRATCH, pltpu.VMEM(TOTAL, jnp.float32), *LAG_SCRATCH],
+        ),
+        compiler_params=pltpu.CompilerParams(vmem_limit_bytes=36 * 1024 * 1024),
+        cost_estimate=pl.CostEstimate(
+            flops=10 * 10**9, bytes_accessed=16 * 2**20, transcendentals=0
+        ),
+    )(place, *blocks, lag_table())
+
+
 def far_kernel(
-    place, left, right, up, down, own, before, mine, other, source, out, z_re, z_im, z_sum, total, now, later, table, ready
+    place, left, right, up, down, sides, sum_across, mine, other, begun, source, out, z_re, z_im, z_sum, total, now, table, ready
 ):
     step = pl.program_id(0)
     fetch = pltpu.make_async_copy(source, table, ready)
@@ -388,63 +434,57 @@
     def _():
         fetch.start()
         load_rows(place, mine, other, *rows)
-        now[...] = own[...]
-
-    chunks = (parts_of(left), parts_of(right), parts_of(up, down))
+
+    def of_side(side, extra):
+        return [(3, side.at[0]), (4, side.at[1]), (5, side.at[2]), (7, side.at[3]), (6, extra)]
+
+    chunks = (
+        of_side(left, down.at[2]),
+        of_side(right, down.at[3]),
+        [*parts_of(3, up), (6, down.at[0]), (7, down.at[1])],
+    )
     for n, blocks in enumerate(chunks):
 
         @pl.when(step == n)
         def _():
-            total[...] = before[0]
-            add_blocks(blocks, place, 3, rows, total)
-            settle(total, later)
+            total[...] = sides[0] if n < 2 else sum_across[...]
+            add_blocks(blocks, place, rows, total)
+            settle(total, now)
 
     @pl.when(step == 0)
     def _():
         fetch.wait()
 
-    for tile in range(8):
-        start = tile * 512
-        keep = min(512, LAGS - start)
-        value = jnp.dot(
-            now[...], table[:, start : start + 512], preferred_element_type=jnp.float32
-        )
-        value = value.reshape(16, 2, 1, 8, 512).astype(jnp.bfloat16)
-        out[:, :, :, :, start : start + keep] = value[..., :keep]
-
-    @pl.when(step < 3)
-    def _():
-        now[...] = later[...]
-
-
-def correlations(place, left, right, up, down, own, before, mine, other):
+    lag_product(now, table, out)
+
+
+def correlations(place, begun, *blocks):
+    left, right, up, down, sides, sum_across, mine, other = blocks
+    anywhere = pl.BlockSpec(memory_space=pl.ANY)
     return pl.pallas_call(
         far_kernel,
-        out_shape=jax.ShapeDtypeStruct((16, 2, 4, 8, LAGS), jnp.bfloat16),
+        out_shape=jax.ShapeDtypeStruct(CORR, jnp.bfloat16),
         grid_spec=pltpu.PrefetchScalarGridSpec(
             num_scalar_prefetch=1,
-            grid=(4,),
+            grid=(3,),
             in_specs=[
-                *[whole(block.shape) for block in (left, right, up, down, own)],
-                pl.BlockSpec((1, *TOTAL), lambda j, place: (jnp.minimum(j, 2), 0, 0, 0, 0)),
-                *[whole(block.shape) for block in (mine, other)],
-                pl.BlockSpec(memory_space=pl.ANY),
+                *[whole(block.shape) for block in (left, right, up, down)],
+                pl.BlockSpec((1, *TOTAL), lambda j, place: (jnp.minimum(j, 1), 0, 0, 0, 0)),
+                *[whole(block.shape) for block in (sum_across, mine, other)],
+                anywhere,
+                anywhere,
             ],
-            out_specs=pl.BlockSpec((16, 2, 1, 8, LAGS), lambda j, place: (0, 0, place[j], 0, 0)),
-            scratch_shapes=[
-                *ROW_SCRATCH,
-                pltpu.VMEM(TOTAL, jnp.float32),
-                pltpu.VMEM((256, 2 * BINS), jnp.bfloat16),
-                pltpu.VMEM((256, 2 * BINS), jnp.bfloat16),
-                pltpu.VMEM((2 * BINS, LAGS_PAD), jnp.bfloat16),
-                pltpu.SemaphoreType.DMA(()),
-            ],
-        ),
+            out_specs=pl.BlockSpec(
+                (16, 2, 1, 8, LAGS), lambda j, place: (0, 0, place[j + 1], 0, 0)
+            ),
+            scratch_shapes=[*ROW_SCRATCH, pltpu.VMEM(TOTAL, jnp.float32), *LAG_SCRATCH],
+        ),
+        input_output_aliases={9: 0},
         compiler_params=pltpu.CompilerParams(vmem_limit_bytes=36 * 1024 * 1024),
         cost_estimate=pl.CostEstimate(
             flops=2 * 1024 * 1024 * LAGS, bytes_accessed=24 * 2**20, transcendentals=0
         ),
-    )(place, left, right, up, down, own, before, mine, other, lag_table())
+    )(place, *blocks, begun, lag_table())
 
 
 def shards(record, window_weight):
@@ -466,11 +506,11 @@
     arrived = first_step(plain, weighted)
     arrived = second_step(plain, weighted, arrived, col // 2, z_low)
     near, up, down, left, right, across, across_near, mine, other = third_step(arrived)
-    rest = fourth_step(up, down, across, across_near)
-    own, before = near_totals(
-        place, near, up, down, left, right, across, across_near, mine, other
-    )
-    corr = correlations(place, *rest, own, before, mine, other)
+    kept, sides = near_totals(place, near, left, right, across, mine, other)
+    up, down, across_near, kept, sides = together(up, down, across_near, kept, sides)
+    rest = fourth_step(up, down, left, right, across, across_near)
+    corr, sum_across = own_correlations(place, kept, up, down, across_near, mine, other)
+    corr = correlations(place, corr, *rest, sides, sum_across, mine, other)
     return corr.reshape(1, 1, 16, 8, 8, LAGS)
 
 

time: 101 us -> 98.5 us (0.975)
  the two profiles are of different devices: /device:TPU:6 before, /device:TPU:96 now
where the time goes in v8:
time: 98.5 us; the launch traced here: 98.3 us
  Pallas kernels  45.9 us (47%)
  starting transfers between devices  31.8 us (32%)
  waiting for transfers between devices  17.8 us (18%)
  other arithmetic  2.18 us (2%)
    ppermute x16, starting transfers between devices, shift(): return lax.ppermute(value, AXES, pairs)  27.2 us
    pallas_call x1, Pallas kernels, correlations(): pl.pallas_call(far_kernel, out_shape=jax.ShapeDtypeStruct(CORR, jnp.bfloa...  20.2 us
    ppermute x16, waiting for transfers between devices, shift(): return lax.ppermute(value, AXES, pairs)  11.1 us
    pallas_call x1, Pallas kernels, own_correlations(): pl.pallas_call(own_kernel, out_shape=(jax.ShapeDtypeStruct(CORR, jnp.bflo...  9.88 us
    pallas_call x1, Pallas kernels, whiten(): pl.pallas_call(whiten_kernel, out_shape=(out, out), grid=(1,), in_specs=[...  8.05 us
    pallas_call x1, Pallas kernels, near_totals(): pl.pallas_call(near_kernel, out_shape=(jax.ShapeDtypeStruct(two, jnp.floa...  7.74 us
    ppermute x3, waiting for transfers between devices, own_only(): return lax.ppermute(value, 'win', [(i, (i + k) % 4) for i in range(4)])  6.7 us
    ppermute x3, starting transfers between devices, own_only(): return lax.ppermute(value, 'win', [(i, (i + k) % 4) for i in range(4)])  4.58 us
  transfers between devices with their start and end apart: 19, of which 10 were waited for; matrix products, arithmetic and copies ran while one was open for 1% of the time, Pallas kernels for 18%

profile of v8, /device:TPU:96, one launch (start us, length us, event | category | flops | bytes accessed | tf_op | source)
XLA Modules:
  0.0 98.3 jit_solution(1033022694786214366)
XLA Ops:
  0.0 0.0 copy-start.3
  0.0 8.1 %shard_map.118 = (bf16[8,8,1024]{2,1,0:T(8,128)(2,1)}, bf16[8,8,1024]{2,1,0:T(8,128)(2,1)}) custom-call(bf16[8,8,12000]{2,1,0:T(8,128)(2,1)} %record.1, f32[8]{0:T(128)} %weight.1, f32[1,12000]{1,0:T(1,128)} %constant.137.clone.taper, f32[1,512]{1,0:T(1,128)} %constant.138.clone.band, f32[512,512]{1,0:T(8,128)} %constant.139.clone.smooth, ...), custom_call_target="tpu_custom_call" | custom-call | flops 1000000000 | bytes 12582912 | tf_op jit(solution)/shard_map/pallas_call | solution.py:142
  8.1 0.0 copy-start.2
  8.1 3.1 %collective-permute-start = (bf16[8,8,1024]{2,1,0:T(8,128)(2,1)}, bf16[8,8,1024]{2,1,0:T(8,128)(2,1)S(1)}, u32[]{:S(2)}, u32[]{:S(2)}) collective-permute-start(bf16[8,8,1024]{2,1,0:T(8,128)(2,1)} %get-tuple-element.37), channel_id=1, source_target_pairs={{0,16},{1,17},{64,80},{65,81},{128,144},{129,145},{192,208},{193,2... | collective-permute-start | bytes 393224 | tf_op jit(solution)/shard_map/ppermute | solution.py:195
  11.2 0.0 collective-permute-start.5
  11.2 3.7 %collective-permute-start.4 = (bf16[8,8,1024]{2,1,0:T(8,128)(2,1)}, bf16[8,8,1024]{2,1,0:T(8,128)(2,1)S(1)}, u32[]{:S(2)}, u32[]{:S(2)}) collective-permute-start(bf16[8,8,1024]{2,1,0:T(8,128)(2,1)} %get-tuple-element.37), channel_id=1, source_target_pairs={{0,128},{1,129},{64,192},{65,193},{128,32},{129,33},{192,96},{193,... | collective-permute-start | bytes 393224 | tf_op jit(solution)/shard_map/ppermute | solution.py:195
  14.9 0.2 collective-permute-done.across
  15.1 3.2 %collective-permute-start.3 = (bf16[8,8,1024]{2,1,0:T(8,128)(2,1)}, bf16[8,8,1024]{2,1,0:T(8,128)(2,1)S(1)}, u32[]{:S(2)}, u32[]{:S(2)}) collective-permute-start(bf16[8,8,1024]{2,1,0:T(8,128)(2,1)} %get-tuple-element.38), channel_id=1, source_target_pairs={{0,4},{1,5},{64,68},{65,69},{128,132},{129,133},{192,196},{193,197... | collective-permute-start | bytes 393224 | tf_op jit(solution)/shard_map/ppermute | solution.py:195
  18.3 1.1 %collective-permute-start.2 = (bf16[8,8,1024]{2,1,0:T(8,128)(2,1)}, bf16[8,8,1024]{2,1,0:T(8,128)(2,1)S(1)}, u32[]{:S(2)}, u32[]{:S(2)}) collective-permute-start(bf16[8,8,1024]{2,1,0:T(8,128)(2,1)} %get-tuple-element.38), channel_id=1, source_target_pairs={{0,6},{1,7},{64,70},{65,71},{128,134},{129,135},{192,198},{193,199... | collective-permute-start | bytes 393224 | tf_op jit(solution)/shard_map/ppermute | solution.py:195
  19.4 1.0 collective-permute-start.1
  20.3 2.6 %collective-permute-done.5 = bf16[8,8,1024]{2,1,0:T(8,128)(2,1)S(1)} collective-permute-done((bf16[8,8,1024]{2,1,0:T(8,128)(2,1)}, bf16[8,8,1024]{2,1,0:T(8,128)(2,1)S(1)}, u32[]{:S(2)}, u32[]{:S(2)}) %collective-permute-start.5) | collective-permute-done | bytes 131104 | tf_op jit(solution)/shard_map/ppermute | solution.py:195
  22.9 0.0 collective-permute-done.4
  22.9 0.1 collective-permute-done.3
  23.0 1.3 %collective-permute-done.2 = bf16[8,8,1024]{2,1,0:T(8,128)(2,1)S(1)} collective-permute-done((bf16[8,8,1024]{2,1,0:T(8,128)(2,1)}, bf16[8,8,1024]{2,1,0:T(8,128)(2,1)S(1)}, u32[]{:S(2)}, u32[]{:S(2)}) %collective-permute-start.2) | collective-permute-done | bytes 131104 | tf_op jit(solution)/shard_map/ppermute | solution.py:195
  24.3 1.4 %collective-permute-done.1 = bf16[8,8,1024]{2,1,0:T(8,128)(2,1)S(1)} collective-permute-done((bf16[8,8,1024]{2,1,0:T(8,128)(2,1)}, bf16[8,8,1024]{2,1,0:T(8,128)(2,1)S(1)}, u32[]{:S(2)}, u32[]{:S(2)}) %collective-permute-start.1) | collective-permute-done | bytes 131104 | tf_op jit(solution)/shard_map/ppermute | solution.py:195
  25.8 0.9 pad_maximum_fusion.3.near
  26.7 1.6 %collective-permute-start.10 = (bf16[3,8,8,1024]{3,2,1,0:T(8,128)(2,1)S(1)}, bf16[3,8,8,1024]{3,2,1,0:T(8,128)(2,1)S(1)}, u32[]{:S(2)}, u32[]{:S(2)}) collective-permute-start(bf16[3,8,8,1024]{3,2,1,0:T(8,128)(2,1)S(1)} %pad_maximum_fusion.3.near), channel_id=1, source_target_pairs={{0,8},{1,9},{64,72},{65,73},{128,136},{129,137},{192,200},{193,201... | collective-permute-start | bytes 1179656 | tf_op jit(solution)/shard_map/ppermute | solution.py:195
  28.3 1.7 %collective-permute-start.9 = (bf16[3,8,8,1024]{3,2,1,0:T(8,128)(2,1)S(1)}, bf16[3,8,8,1024]{3,2,1,0:T(8,128)(2,1)S(1)}, u32[]{:S(2)}, u32[]{:S(2)}) collective-permute-start(bf16[3,8,8,1024]{3,2,1,0:T(8,128)(2,1)S(1)} %pad_maximum_fusion.3.near), channel_id=1, source_target_pairs={{0,24},{1,25},{64,88},{65,89},{128,152},{129,153},{192,216},{193,2... | collective-permute-start | bytes 1179656 | tf_op jit(solution)/shard_map/ppermute | solution.py:195
  30.0 1.0 select_select_fusion
  31.0 1.2 %collective-permute-start.8 = (bf16[8,8,1024]{2,1,0:T(8,128)(2,1)S(1)}, bf16[8,8,1024]{2,1,0:T(8,128)(2,1)S(1)}, u32[]{:S(2)}, u32[]{:S(2)}) collective-permute-start(bf16[8,8,1024]{2,1,0:T(8,128)(2,1)S(1)} %get-tuple-element.69), channel_id=1, source_target_pairs={{0,192},{64,0},{128,64},{192,128},{1,193},{65,1},{129,65},{193,129... | collective-permute-start | bytes 393224 | tf_op jit(solution)/shard_map/ppermute | solution.py:199
  32.2 2.9 %collective-permute-start.7 = (bf16[8,8,1024]{2,1,0:T(8,128)(2,1)S(1)}, bf16[8,8,1024]{2,1,0:T(8,128)(2,1)S(1)}, u32[]{:S(2)}, u32[]{:S(2)}) collective-permute-start(bf16[8,8,1024]{2,1,0:T(8,128)(2,1)S(1)} %get-tuple-element.70), channel_id=1, source_target_pairs={{0,128},{64,192},{128,0},{192,64},{1,129},{65,193},{129,1},{193,65... | collective-permute-start | bytes 393224 | tf_op jit(solution)/shard_map/ppermute | solution.py:199
  35.1 0.4 collective-permute-start.6
  35.6 0.0 copy-done.3
  35.6 2.9 %collective-permute-done.8 = bf16[8,8,1024]{2,1,0:T(8,128)(2,1)S(1)} collective-permute-done((bf16[8,8,1024]{2,1,0:T(8,128)(2,1)S(1)}, bf16[8,8,1024]{2,1,0:T(8,128)(2,1)S(1)}, u32[]{:S(2)}, u32[]{:S(2)}) %collective-permute-start.8) | collective-permute-done | bytes 131104 | tf_op jit(solution)/shard_map/ppermute | solution.py:199
  38.5 3.8 %collective-permute-done.7 = bf16[8,8,1024]{2,1,0:T(8,128)(2,1)S(1)} collective-permute-done((bf16[8,8,1024]{2,1,0:T(8,128)(2,1)S(1)}, bf16[8,8,1024]{2,1,0:T(8,128)(2,1)S(1)}, u32[]{:S(2)}, u32[]{:S(2)}) %collective-permute-start.7) | collective-permute-done | bytes 131104 | tf_op jit(solution)/shard_map/ppermute | solution.py:199
  42.3 0.0 collective-permute-done.6
  42.3 0.0 collective-permute-done.10.left
  42.3 0.0 copy-start
  42.3 0.0 collective-permute-done.9.right
  42.3 0.0 copy-start.1
  42.3 0.1 pad_maximum_fusion.mine
  42.4 0.1 collective-permute-start.14
  42.5 0.0 copy-done.2
  42.6 0.1 concatenate.9.place
  42.7 4.8 %collective-permute-start.11 = (bf16[3,8,8,1024]{3,2,1,0:T(8,128)(2,1)S(1)}, bf16[3,8,8,1024]{3,2,1,0:T(8,128)(2,1)S(1)}, u32[]{:S(2)}, u32[]{:S(2)}) collective-permute-start(bf16[3,8,8,1024]{3,2,1,0:T(8,128)(2,1)S(1)} %pad_maximum_fusion.3.near), channel_id=1, source_target_pairs={{0,64},{1,65},{64,128},{65,129},{128,192},{129,193},{192,32},{193,... | collective-permute-start | bytes 1179656 | tf_op jit(solution)/shard_map/ppermute | solution.py:195
  47.5 1.2 %collective-permute-start.13 = (bf16[2,8,8,1024]{3,2,1,0:T(8,128)(2,1)S(1)}, bf16[2,8,8,1024]{3,2,1,0:T(8,128)(2,1)S(1)}, u32[]{:S(2)}, u32[]{:S(2)}) collective-permute-start(bf16[2,8,8,1024]{3,2,1,0:T(8,128)(2,1)S(1)} %get-tuple-element.73), channel_id=1, source_target_pairs={{0,16},{1,17},{64,80},{65,81},{128,144},{129,145},{192,208},{193,2... | collective-permute-start | bytes 786440 | tf_op jit(solution)/shard_map/ppermute | solution.py:195
  48.8 0.0 slice-start
  48.8 0.0 slice-start.1
  48.8 0.0 collective-permute-start.12
  48.8 0.0 collective-permute-done.14.other
  48.8 7.7 %shard_map.119 = (f32[2,2,16,8,1024]{4,3,2,1,0:T(8,128)S(1)}, f32[2,2,16,8,1024]{4,3,2,1,0:T(8,128)S(1)}) custom-call(s32[25]{0:T(128)S(1)} %concatenate.9.place, bf16[3,8,8,1024]{3,2,1,0:T(8,128)(2,1)S(1)} %pad_maximum_fusion.3.near, bf16[3,8,8,1024]{3,2,1,0:T(8,128)(2,1)S(1)} %collective-permute-done.10.left, ...), custom_call_target="tpu_custom_call" | custom-call | flops 8000000000 | bytes 8388608 | tf_op jit(solution)/shard_map/pallas_call | solution.py:366
  56.5 0.0 copy-done
  56.5 0.0 copy-done.1
  56.5 1.0 collective-permute-done.13.across_near
  57.5 0.0 slice-start.2
  57.5 0.0 slice-start.3
  57.5 0.6 collective-permute-done.12.down
  58.1 0.0 collective-permute-done.11.up
  58.2 0.7 collective-permute-start.18
  58.8 2.6 %collective-permute-start.17 = (bf16[4,8,8,1024]{3,2,1,0:T(8,128)(2,1)S(1)}, bf16[4,8,8,1024]{3,2,1,0:T(8,128)(2,1)S(1)}, u32[]{:S(2)}, u32[]{:S(2)}) collective-permute-start(bf16[4,8,8,1024]{3,2,1,0:T(8,128)(2,1)S(1)} %pad_maximum_fusion.2), channel_id=1, source_target_pairs={{0,24},{1,25},{64,88},{65,89},{128,152},{129,153},{192,216},{193,2... | collective-permute-start | bytes 1572872 | tf_op jit(solution)/shard_map/ppermute | solution.py:195
  61.5 2.2 %collective-permute-start.16 = (bf16[3,8,8,1024]{3,2,1,0:T(8,128)(2,1)S(1)}, bf16[3,8,8,1024]{3,2,1,0:T(8,128)(2,1)S(1)}, u32[]{:S(2)}, u32[]{:S(2)}) collective-permute-start(bf16[3,8,8,1024]{3,2,1,0:T(8,128)(2,1)S(1)} %pad_maximum_fusion.4), channel_id=1, source_target_pairs={{0,64},{1,65},{64,128},{65,129},{128,192},{129,193},{192,32},{193,... | collective-permute-start | bytes 1179656 | tf_op jit(solution)/shard_map/ppermute | solution.py:195
  63.7 0.0 slice-done.2
  63.7 0.0 slice-done.3
  63.7 0.1 pad_maximum_fusion.1
  63.8 0.3 collective-permute-start.15
  64.1 0.0 slice-done
  64.1 0.0 slice-done.1
  64.1 9.9 %shard_map.120 = (bf16[16,2,4,8,4000]{4,3,2,1,0:T(8,128)(2,1)}, f32[2,16,8,1024]{3,2,1,0:T(8,128)S(1)}) custom-call(s32[25]{0:T(128)S(1)} %concatenate.9.place, f32[2,2,16,8,1024]{4,3,2,1,0:T(8,128)S(1)} %get-tuple-element.64.kept, bf16[3,8,8,1024]{3,2,1,0:T(8,128)(2,1)S(1)} %collective-permute-done.11.up, ...), custom_call_target="tpu_custom_call" | custom-call | flops 10000000000 | bytes 16777216 | tf_op jit(solution)/shard_map/pallas_call | solution.py:400
  74.0 0.0 collective-permute-done.16.up
  74.0 0.0 collective-permute-done.18.left
  74.0 0.0 collective-permute-done.17.right
  74.0 3.9 %collective-permute-done.15.down = bf16[4,8,8,1024]{3,2,1,0:T(8,128)(2,1)S(1)} collective-permute-done((bf16[4,8,8,1024]{3,2,1,0:T(8,128)(2,1)S(1)}, bf16[4,8,8,1024]{3,2,1,0:T(8,128)(2,1)S(1)}, u32[]{:S(2)}, u32[]{:S(2)}) %collective-permute-start.15) | collective-permute-done | bytes 524320 | tf_op jit(solution)/shard_map/ppermute | solution.py:195
  77.9 20.2 %shard_map.121 = bf16[16,2,4,8,4000]{4,3,2,1,0:T(8,128)(2,1)} custom-call(s32[25]{0:T(128)S(1)} %concatenate.9.place, bf16[4,8,8,1024]{3,2,1,0:T(8,128)(2,1)S(1)} %collective-permute-done.18.left, bf16[4,8,8,1024]{3,2,1,0:T(8,128)(2,1)S(1)} %collective-permute-done.17.right, ...), custom_call_target="tpu_custom_call", output_to_operand_aliasing={{}: (9, {})} | custom-call | flops 8388608000 | bytes 25165824 | tf_op jit(solution)/shard_map/pallas_call | solution.py:464
  (9 shorter events, 0.2 us)
Async XLA Ops:
  0.0 35.6 %copy-start.3 = (s32[8]{0:T(128)S(1)}, s32[8]{0:T(128)}, u32[]{:S(2)}) copy-start(s32[8]{0:T(128)} %constant.143.clone) | copy-start | bytes 100
  8.1 34.5 %copy-start.2 = (s32[4]{0:T(128)S(1)}, s32[4]{0:T(128)}, u32[]{:S(2)}) copy-start(s32[4]{0:T(128)} %constant.144.clone) | copy-start | bytes 52
  8.1 7.0 %collective-permute-start = (bf16[8,8,1024]{2,1,0:T(8,128)(2,1)}, bf16[8,8,1024]{2,1,0:T(8,128)(2,1)S(1)}, u32[]{:S(2)}, u32[]{:S(2)}) collective-permute-start(bf16[8,8,1024]{2,1,0:T(8,128)(2,1)} %get-tuple-element.37), channel_id=1, source_target_pairs={{0,16},{1,17},{64,80},{65,81},{128,144},{129,145},{192,208},{193,2... | collective-permute-start | bytes 393224 | tf_op jit(solution)/shard_map/ppermute | solution.py:195
  11.2 11.7 %collective-permute-start.5 = (bf16[8,8,1024]{2,1,0:T(8,128)(2,1)}, bf16[8,8,1024]{2,1,0:T(8,128)(2,1)S(1)}, u32[]{:S(2)}, u32[]{:S(2)}) collective-permute-start(bf16[8,8,1024]{2,1,0:T(8,128)(2,1)} %get-tuple-element.37), channel_id=1, source_target_pairs={{0,96},{1,97},{64,160},{65,161},{128,224},{129,225},{192,0},{193,1... | collective-permute-start | bytes 393224 | tf_op jit(solution)/shard_map/ppermute | solution.py:195
  11.2 11.7 %collective-permute-start.4 = (bf16[8,8,1024]{2,1,0:T(8,128)(2,1)}, bf16[8,8,1024]{2,1,0:T(8,128)(2,1)S(1)}, u32[]{:S(2)}, u32[]{:S(2)}) collective-permute-start(bf16[8,8,1024]{2,1,0:T(8,128)(2,1)} %get-tuple-element.37), channel_id=1, source_target_pairs={{0,128},{1,129},{64,192},{65,193},{128,32},{129,33},{192,96},{193,... | collective-permute-start | bytes 393224 | tf_op jit(solution)/shard_map/ppermute | solution.py:195
  15.1 7.9 %collective-permute-start.3 = (bf16[8,8,1024]{2,1,0:T(8,128)(2,1)}, bf16[8,8,1024]{2,1,0:T(8,128)(2,1)S(1)}, u32[]{:S(2)}, u32[]{:S(2)}) collective-permute-start(bf16[8,8,1024]{2,1,0:T(8,128)(2,1)} %get-tuple-element.38), channel_id=1, source_target_pairs={{0,4},{1,5},{64,68},{65,69},{128,132},{129,133},{192,196},{193,197... | collective-permute-start | bytes 393224 | tf_op jit(solution)/shard_map/ppermute | solution.py:195
  18.3 6.0 %collective-permute-start.2 = (bf16[8,8,1024]{2,1,0:T(8,128)(2,1)}, bf16[8,8,1024]{2,1,0:T(8,128)(2,1)S(1)}, u32[]{:S(2)}, u32[]{:S(2)}) collective-permute-start(bf16[8,8,1024]{2,1,0:T(8,128)(2,1)} %get-tuple-element.38), channel_id=1, source_target_pairs={{0,6},{1,7},{64,70},{65,71},{128,134},{129,135},{192,198},{193,199... | collective-permute-start | bytes 393224 | tf_op jit(solution)/shard_map/ppermute | solution.py:195
  19.4 6.4 %collective-permute-start.1 = (bf16[8,8,1024]{2,1,0:T(8,128)(2,1)}, bf16[8,8,1024]{2,1,0:T(8,128)(2,1)S(1)}, u32[]{:S(2)}, u32[]{:S(2)}) collective-permute-start(bf16[8,8,1024]{2,1,0:T(8,128)(2,1)} %get-tuple-element.38), channel_id=1, source_target_pairs={{0,2},{1,3},{64,66},{65,67},{128,130},{129,131},{192,194},{193,195... | collective-permute-start | bytes 393224 | tf_op jit(solution)/shard_map/ppermute | solution.py:195
  26.7 15.6 %collective-permute-start.10 = (bf16[3,8,8,1024]{3,2,1,0:T(8,128)(2,1)S(1)}, bf16[3,8,8,1024]{3,2,1,0:T(8,128)(2,1)S(1)}, u32[]{:S(2)}, u32[]{:S(2)}) collective-permute-start(bf16[3,8,8,1024]{3,2,1,0:T(8,128)(2,1)S(1)} %pad_maximum_fusion.3.near), channel_id=1, source_target_pairs={{0,8},{1,9},{64,72},{65,73},{128,136},{129,137},{192,200},{193,201... | collective-permute-start | bytes 1179656 | tf_op jit(solution)/shard_map/ppermute | solution.py:195
  28.3 14.0 %collective-permute-start.9 = (bf16[3,8,8,1024]{3,2,1,0:T(8,128)(2,1)S(1)}, bf16[3,8,8,1024]{3,2,1,0:T(8,128)(2,1)S(1)}, u32[]{:S(2)}, u32[]{:S(2)}) collective-permute-start(bf16[3,8,8,1024]{3,2,1,0:T(8,128)(2,1)S(1)} %pad_maximum_fusion.3.near), channel_id=1, source_target_pairs={{0,24},{1,25},{64,88},{65,89},{128,152},{129,153},{192,216},{193,2... | collective-permute-start | bytes 1179656 | tf_op jit(solution)/shard_map/ppermute | solution.py:195
  31.0 7.5 %collective-permute-start.8 = (bf16[8,8,1024]{2,1,0:T(8,128)(2,1)S(1)}, bf16[8,8,1024]{2,1,0:T(8,128)(2,1)S(1)}, u32[]{:S(2)}, u32[]{:S(2)}) collective-permute-start(bf16[8,8,1024]{2,1,0:T(8,128)(2,1)S(1)} %get-tuple-element.69), channel_id=1, source_target_pairs={{0,192},{64,0},{128,64},{192,128},{1,193},{65,1},{129,65},{193,129... | collective-permute-start | bytes 393224 | tf_op jit(solution)/shard_map/ppermute | solution.py:199
  32.2 10.1 %collective-permute-start.7 = (bf16[8,8,1024]{2,1,0:T(8,128)(2,1)S(1)}, bf16[8,8,1024]{2,1,0:T(8,128)(2,1)S(1)}, u32[]{:S(2)}, u32[]{:S(2)}) collective-permute-start(bf16[8,8,1024]{2,1,0:T(8,128)(2,1)S(1)} %get-tuple-element.70), channel_id=1, source_target_pairs={{0,128},{64,192},{128,0},{192,64},{1,129},{65,193},{129,1},{193,65... | collective-permute-start | bytes 393224 | tf_op jit(solution)/shard_map/ppermute | solution.py:199
  35.1 7.2 %collective-permute-start.6 = (bf16[8,8,1024]{2,1,0:T(8,128)(2,1)S(1)}, bf16[8,8,1024]{2,1,0:T(8,128)(2,1)S(1)}, u32[]{:S(2)}, u32[]{:S(2)}) collective-permute-start(bf16[8,8,1024]{2,1,0:T(8,128)(2,1)S(1)} %get-tuple-element.71), channel_id=1, source_target_pairs={{0,64},{64,128},{128,192},{192,0},{1,65},{65,129},{129,193},{193,1... | collective-permute-start | bytes 393224 | tf_op jit(solution)/shard_map/ppermute | solution.py:199
  42.3 14.2 %copy-start = (bf16[3,8,8,1024]{3,2,1,0:T(8,128)(2,1)}, bf16[3,8,8,1024]{3,2,1,0:T(8,128)(2,1)S(1)}, u32[]{:S(2)}) copy-start(bf16[3,8,8,1024]{3,2,1,0:T(8,128)(2,1)S(1)} %collective-permute-done.10.left) | copy-start | bytes 1179652
  42.3 14.2 %copy-start.1 = (bf16[3,8,8,1024]{3,2,1,0:T(8,128)(2,1)}, bf16[3,8,8,1024]{3,2,1,0:T(8,128)(2,1)S(1)}, u32[]{:S(2)}) copy-start(bf16[3,8,8,1024]{3,2,1,0:T(8,128)(2,1)S(1)} %collective-permute-done.9.right) | copy-start | bytes 1179652
  42.4 6.4 %collective-permute-start.14 = (bf16[4,8,8,1024]{3,2,1,0:T(8,128)(2,1)S(1)}, bf16[4,8,8,1024]{3,2,1,0:T(8,128)(2,1)S(1)}, u32[]{:S(2)}, u32[]{:S(2)}) collective-permute-start(bf16[4,8,8,1024]{3,2,1,0:T(8,128)(2,1)S(1)} %pad_maximum_fusion.mine), channel_id=1, source_target_pairs={{0,1},{1,0},{64,65},{65,64},{128,129},{129,128},{192,193},{193,192... | collective-permute-start | bytes 1572872 | tf_op jit(solution)/shard_map/ppermute | solution.py:195
  42.7 15.4 %collective-permute-start.11 = (bf16[3,8,8,1024]{3,2,1,0:T(8,128)(2,1)S(1)}, bf16[3,8,8,1024]{3,2,1,0:T(8,128)(2,1)S(1)}, u32[]{:S(2)}, u32[]{:S(2)}) collective-permute-start(bf16[3,8,8,1024]{3,2,1,0:T(8,128)(2,1)S(1)} %pad_maximum_fusion.3.near), channel_id=1, source_target_pairs={{0,64},{1,65},{64,128},{65,129},{128,192},{129,193},{192,32},{193,... | collective-permute-start | bytes 1179656 | tf_op jit(solution)/shard_map/ppermute | solution.py:195
  47.5 10.0 %collective-permute-start.13 = (bf16[2,8,8,1024]{3,2,1,0:T(8,128)(2,1)S(1)}, bf16[2,8,8,1024]{3,2,1,0:T(8,128)(2,1)S(1)}, u32[]{:S(2)}, u32[]{:S(2)}) collective-permute-start(bf16[2,8,8,1024]{3,2,1,0:T(8,128)(2,1)S(1)} %get-tuple-element.73), channel_id=1, source_target_pairs={{0,16},{1,17},{64,80},{65,81},{128,144},{129,145},{192,208},{193,2... | collective-permute-start | bytes 786440 | tf_op jit(solution)/shard_map/ppermute | solution.py:195
  48.8 15.3 %slice-start = ((s8[8388608]{0:T(1024)(128)(4,1)}), s8[4194304]{0:T(1024)(128)(4,1)S(1)}, s32[]{:S(2)}) async-start(s8[8388608]{0:T(1024)(128)(4,1)} %bitcast.10), calls=%async_computation | async-start | bytes 8388608
  48.8 15.3 %slice-start.1 = ((s8[8388608]{0:T(1024)(128)(4,1)}), s8[4194304]{0:T(1024)(128)(4,1)S(1)}, s32[]{:S(2)}) async-start(s8[8388608]{0:T(1024)(128)(4,1)} %bitcast.10), calls=%async_computation.1 | async-start | bytes 8388608
  48.8 9.3 %collective-permute-start.12 = (bf16[2,8,8,1024]{3,2,1,0:T(8,128)(2,1)S(1)}, bf16[2,8,8,1024]{3,2,1,0:T(8,128)(2,1)S(1)}, u32[]{:S(2)}, u32[]{:S(2)}) collective-permute-start(bf16[2,8,8,1024]{3,2,1,0:T(8,128)(2,1)S(1)} %get-tuple-element.74), channel_id=1, source_target_pairs={{0,224},{1,225},{64,0},{65,1},{128,64},{129,65},{192,128},{193,129... | collective-permute-start | bytes 786440 | tf_op jit(solution)/shard_map/ppermute | solution.py:195
  57.5 6.2 %slice-start.2 = ((bf16[3,8,8,1024]{3,2,1,0:T(8,128)(2,1)}), bf16[1,8,8,1024]{3,2,1,0:T(8,128)(2,1)S(1)}, s32[]{:S(2)}) async-start(bf16[3,8,8,1024]{3,2,1,0:T(8,128)(2,1)} %copy-done), calls=%async_computation.2 | async-start | bytes 262144 | tf_op jit(solution)/shard_map/slice | solution.py:254
  57.5 6.2 %slice-start.3 = ((bf16[3,8,8,1024]{3,2,1,0:T(8,128)(2,1)}), bf16[1,8,8,1024]{3,2,1,0:T(8,128)(2,1)S(1)}, s32[]{:S(2)}) async-start(bf16[3,8,8,1024]{3,2,1,0:T(8,128)(2,1)} %copy-done.1), calls=%async_computation.3 | async-start | bytes 262144 | tf_op jit(solution)/shard_map/slice | solution.py:254
  58.2 15.8 %collective-permute-start.18 = (bf16[4,8,8,1024]{3,2,1,0:T(8,128)(2,1)S(1)}, bf16[4,8,8,1024]{3,2,1,0:T(8,128)(2,1)S(1)}, u32[]{:S(2)}, u32[]{:S(2)}) collective-permute-start(bf16[4,8,8,1024]{3,2,1,0:T(8,128)(2,1)S(1)} %pad_maximum_fusion.2), channel_id=1, source_target_pairs={{0,8},{1,9},{64,72},{65,73},{128,136},{129,137},{192,200},{193,201... | collective-permute-start | bytes 1572872 | tf_op jit(solution)/shard_map/ppermute | solution.py:195
  58.8 15.2 %collective-permute-start.17 = (bf16[4,8,8,1024]{3,2,1,0:T(8,128)(2,1)S(1)}, bf16[4,8,8,1024]{3,2,1,0:T(8,128)(2,1)S(1)}, u32[]{:S(2)}, u32[]{:S(2)}) collective-permute-start(bf16[4,8,8,1024]{3,2,1,0:T(8,128)(2,1)S(1)} %pad_maximum_fusion.2), channel_id=1, source_target_pairs={{0,24},{1,25},{64,88},{65,89},{128,152},{129,153},{192,216},{193,2... | collective-permute-start | bytes 1572872 | tf_op jit(solution)/shard_map/ppermute | solution.py:195
  61.5 12.5 %collective-permute-start.16 = (bf16[3,8,8,1024]{3,2,1,0:T(8,128)(2,1)S(1)}, bf16[3,8,8,1024]{3,2,1,0:T(8,128)(2,1)S(1)}, u32[]{:S(2)}, u32[]{:S(2)}) collective-permute-start(bf16[3,8,8,1024]{3,2,1,0:T(8,128)(2,1)S(1)} %pad_maximum_fusion.4), channel_id=1, source_target_pairs={{0,64},{1,65},{64,128},{65,129},{128,192},{129,193},{192,32},{193,... | collective-permute-start | bytes 1179656 | tf_op jit(solution)/shard_map/ppermute | solution.py:195
  63.8 14.2 %collective-permute-start.15 = (bf16[4,8,8,1024]{3,2,1,0:T(8,128)(2,1)S(1)}, bf16[4,8,8,1024]{3,2,1,0:T(8,128)(2,1)S(1)}, u32[]{:S(2)}, u32[]{:S(2)}) collective-permute-start(bf16[4,8,8,1024]{3,2,1,0:T(8,128)(2,1)S(1)} %pad_maximum_fusion.1), channel_id=1, source_target_pairs={{0,224},{1,225},{64,0},{65,1},{128,64},{129,65},{192,128},{193,129... | collective-permute-start | bytes 1572872 | tf_op jit(solution)/shard_map/ppermute | solution.py:195

commit v9 on v8

--- a/solution.py
+++ b/solution.py
@@ -204,12 +204,11 @@
 
 
 def first_step(plain, weighted):
-    weighted, across = together(weighted, shift(plain, dx=2))
     return together(
         shift(weighted, dy=1),
         shift(weighted, dy=3),
         shift(weighted, dy=2),
-        across,
+        shift(plain, dx=2),
         shift(plain, dz=2),
         shift(plain, dz=-3),
     )
@@ -307,12 +306,12 @@
 
 
 def add_blocks(blocks, place, rows, total):
-    def tile_step(tile, carry):
-        for n, block in blocks:
+    for n, block in blocks:
+        def tile_step(tile, carry, n=n, block=block):
             add_cross(tile, block, place[HIGH + n], place[GROUP + n], rows, total)
-        return carry
-
-    lax.fori_loop(0, 4, tile_step, 0)
+            return carry
+
+        lax.fori_loop(0, 4, tile_step, 0)
 
 
 def settle(source, target):

time: 98.5 us -> 99.4 us (level)
  starting transfers between devices: 31.8 us -> 36 us
  waiting for transfers between devices: 17.8 us -> 15.6 us
    ppermute x16, starting transfers between devices: 27.2 us -> 29.3 us  [shift(): return lax.ppermute(value, AXES, pairs)]
    ppermute x3, starting transfers between devices: 4.58 us -> 6.63 us  [own_only(): return lax.ppermute(value, 'win', [(i, (i + k) % 4) for i in range(4)])]
    ppermute x3, waiting for transfers between devices: 6.7 us -> 5.49 us  [own_only(): return lax.ppermute(value, 'win', [(i, (i + k) % 4) for i in range(4)])]
    ppermute x16, waiting for transfers between devices: 11.1 us -> 10.1 us  [shift(): return lax.ppermute(value, AXES, pairs)]
  transfers between devices with their start and end apart: 19 -> 19, of which waited for: 10 -> 7; matrix products, arithmetic and copies ran while one was open for 1% -> 1% of each run, Pallas kernels for 18% -> 17%
where the time goes in v9:
time: 99.4 us; the launch traced here: 99.3 us
  Pallas kernels  45 us (45%)
  starting transfers between devices  36 us (36%)
  waiting for transfers between devices  15.6 us (16%)
  other arithmetic  2.18 us (2%)
    ppermute x16, starting transfers between devices, shift(): return lax.ppermute(value, AXES, pairs)  29.3 us
    pallas_call x1, Pallas kernels, correlations(): pl.pallas_call(far_kernel, out_shape=jax.ShapeDtypeStruct(CORR, jnp.bfloa...  19.8 us
    ppermute x16, waiting for transfers between devices, shift(): return lax.ppermute(value, AXES, pairs)  10.1 us
    pallas_call x1, Pallas kernels, own_correlations(): pl.pallas_call(own_kernel, out_shape=(jax.ShapeDtypeStruct(CORR, jnp.bflo...  9.68 us
    pallas_call x1, Pallas kernels, whiten(): pl.pallas_call(whiten_kernel, out_shape=(out, out), grid=(1,), in_specs=[...  8.05 us
    pallas_call x1, Pallas kernels, near_totals(): pl.pallas_call(near_kernel, out_shape=(jax.ShapeDtypeStruct(two, jnp.floa...  7.5 us
    ppermute x3, starting transfers between devices, own_only(): return lax.ppermute(value, 'win', [(i, (i + k) % 4) for i in range(4)])  6.63 us
    ppermute x3, waiting for transfers between devices, own_only(): return lax.ppermute(value, 'win', [(i, (i + k) % 4) for i in range(4)])  5.49 us
  transfers between devices with their start and end apart: 19, of which 7 were waited for; matrix products, arithmetic and copies ran while one was open for 1% of the time, Pallas kernels for 17%

profile of v9, /device:TPU:96, one launch (start us, length us, event | category | flops | bytes accessed | tf_op | source)
XLA Modules:
  0.0 99.3 jit_solution(18192723817924324953)
XLA Ops:
  0.0 0.0 copy-start.3
  0.0 8.1 %shard_map.118 = (bf16[8,8,1024]{2,1,0:T(8,128)(2,1)}, bf16[8,8,1024]{2,1,0:T(8,128)(2,1)}) custom-call(bf16[8,8,12000]{2,1,0:T(8,128)(2,1)} %record.1, f32[8]{0:T(128)} %weight.1, f32[1,12000]{1,0:T(1,128)} %constant.137.clone.taper, f32[1,512]{1,0:T(1,128)} %constant.138.clone.band, f32[512,512]{1,0:T(8,128)} %constant.139.clone.smooth, ...), custom_call_target="tpu_custom_call" | custom-call | flops 1000000000 | bytes 12582912 | tf_op jit(solution)/shard_map/pallas_call | solution.py:142
  8.1 0.0 copy-start.2
  8.1 3.3 %collective-permute-start.2 = (bf16[8,8,1024]{2,1,0:T(8,128)(2,1)}, bf16[8,8,1024]{2,1,0:T(8,128)(2,1)S(1)}, u32[]{:S(2)}, u32[]{:S(2)}) collective-permute-start(bf16[8,8,1024]{2,1,0:T(8,128)(2,1)} %get-tuple-element.34), channel_id=1, source_target_pairs={{0,4},{1,5},{64,68},{65,69},{128,132},{129,133},{192,196},{193,197... | collective-permute-start | bytes 393224 | tf_op jit(solution)/shard_map/ppermute | solution.py:195
  11.4 1.1 %collective-permute-start.1 = (bf16[8,8,1024]{2,1,0:T(8,128)(2,1)}, bf16[8,8,1024]{2,1,0:T(8,128)(2,1)S(1)}, u32[]{:S(2)}, u32[]{:S(2)}) collective-permute-start(bf16[8,8,1024]{2,1,0:T(8,128)(2,1)} %get-tuple-element.34), channel_id=1, source_target_pairs={{0,6},{1,7},{64,70},{65,71},{128,134},{129,135},{192,198},{193,199... | collective-permute-start | bytes 393224 | tf_op jit(solution)/shard_map/ppermute | solution.py:195
  12.4 1.0 collective-permute-start
  13.4 0.0 collective-permute-start.5
  13.4 3.7 %collective-permute-start.4 = (bf16[8,8,1024]{2,1,0:T(8,128)(2,1)}, bf16[8,8,1024]{2,1,0:T(8,128)(2,1)S(1)}, u32[]{:S(2)}, u32[]{:S(2)}) collective-permute-start(bf16[8,8,1024]{2,1,0:T(8,128)(2,1)} %get-tuple-element.35), channel_id=1, source_target_pairs={{0,128},{1,129},{64,192},{65,193},{128,32},{129,33},{192,96},{193,... | collective-permute-start | bytes 393224 | tf_op jit(solution)/shard_map/ppermute | solution.py:195
  17.1 0.0 collective-permute-done.2
  17.1 3.0 %collective-permute-start.3 = (bf16[8,8,1024]{2,1,0:T(8,128)(2,1)}, bf16[8,8,1024]{2,1,0:T(8,128)(2,1)S(1)}, u32[]{:S(2)}, u32[]{:S(2)}) collective-permute-start(bf16[8,8,1024]{2,1,0:T(8,128)(2,1)} %get-tuple-element.35), channel_id=1, source_target_pairs={{0,16},{1,17},{64,80},{65,81},{128,144},{129,145},{192,208},{193,2... | collective-permute-start | bytes 393224 | tf_op jit(solution)/shard_map/ppermute | solution.py:195
  20.1 0.0 collective-permute-done.1
  20.1 0.0 collective-permute-done
  20.1 4.7 %collective-permute-done.5 = bf16[8,8,1024]{2,1,0:T(8,128)(2,1)S(1)} collective-permute-done((bf16[8,8,1024]{2,1,0:T(8,128)(2,1)}, bf16[8,8,1024]{2,1,0:T(8,128)(2,1)S(1)}, u32[]{:S(2)}, u32[]{:S(2)}) %collective-permute-start.5) | collective-permute-done | bytes 131104 | tf_op jit(solution)/shard_map/ppermute | solution.py:195
  24.8 0.0 collective-permute-done.4
  24.8 0.0 collective-permute-done.3.across
  24.8 1.0 pad_maximum_fusion.3.near
  25.7 1.6 %collective-permute-start.10 = (bf16[3,8,8,1024]{3,2,1,0:T(8,128)(2,1)S(1)}, bf16[3,8,8,1024]{3,2,1,0:T(8,128)(2,1)S(1)}, u32[]{:S(2)}, u32[]{:S(2)}) collective-permute-start(bf16[3,8,8,1024]{3,2,1,0:T(8,128)(2,1)S(1)} %pad_maximum_fusion.3.near), channel_id=1, source_target_pairs={{0,8},{1,9},{64,72},{65,73},{128,136},{129,137},{192,200},{193,201... | collective-permute-start | bytes 1179656 | tf_op jit(solution)/shard_map/ppermute | solution.py:195
  27.3 1.7 %collective-permute-start.9 = (bf16[3,8,8,1024]{3,2,1,0:T(8,128)(2,1)S(1)}, bf16[3,8,8,1024]{3,2,1,0:T(8,128)(2,1)S(1)}, u32[]{:S(2)}, u32[]{:S(2)}) collective-permute-start(bf16[3,8,8,1024]{3,2,1,0:T(8,128)(2,1)S(1)} %pad_maximum_fusion.3.near), channel_id=1, source_target_pairs={{0,24},{1,25},{64,88},{65,89},{128,152},{129,153},{192,216},{193,2... | collective-permute-start | bytes 1179656 | tf_op jit(solution)/shard_map/ppermute | solution.py:195
  29.1 1.0 select_select_fusion
  30.0 2.3 %collective-permute-start.8 = (bf16[8,8,1024]{2,1,0:T(8,128)(2,1)S(1)}, bf16[8,8,1024]{2,1,0:T(8,128)(2,1)S(1)}, u32[]{:S(2)}, u32[]{:S(2)}) collective-permute-start(bf16[8,8,1024]{2,1,0:T(8,128)(2,1)S(1)} %get-tuple-element.65), channel_id=1, source_target_pairs={{0,192},{64,0},{128,64},{192,128},{1,193},{65,1},{129,65},{193,129... | collective-permute-start | bytes 393224 | tf_op jit(solution)/shard_map/ppermute | solution.py:199
  32.3 2.0 %collective-permute-start.7 = (bf16[8,8,1024]{2,1,0:T(8,128)(2,1)S(1)}, bf16[8,8,1024]{2,1,0:T(8,128)(2,1)S(1)}, u32[]{:S(2)}, u32[]{:S(2)}) collective-permute-start(bf16[8,8,1024]{2,1,0:T(8,128)(2,1)S(1)} %get-tuple-element.66), channel_id=1, source_target_pairs={{0,128},{64,192},{128,0},{192,64},{1,129},{65,193},{129,1},{193,65... | collective-permute-start | bytes 393224 | tf_op jit(solution)/shard_map/ppermute | solution.py:199
  34.3 2.4 %collective-permute-start.6 = (bf16[8,8,1024]{2,1,0:T(8,128)(2,1)S(1)}, bf16[8,8,1024]{2,1,0:T(8,128)(2,1)S(1)}, u32[]{:S(2)}, u32[]{:S(2)}) collective-permute-start(bf16[8,8,1024]{2,1,0:T(8,128)(2,1)S(1)} %get-tuple-element.67), channel_id=1, source_target_pairs={{0,64},{64,128},{128,192},{192,0},{1,65},{65,129},{129,193},{193,1... | collective-permute-start | bytes 393224 | tf_op jit(solution)/shard_map/ppermute | solution.py:199
  36.7 0.0 copy-done.3
  36.7 1.7 %collective-permute-done.8 = bf16[8,8,1024]{2,1,0:T(8,128)(2,1)S(1)} collective-permute-done((bf16[8,8,1024]{2,1,0:T(8,128)(2,1)S(1)}, bf16[8,8,1024]{2,1,0:T(8,128)(2,1)S(1)}, u32[]{:S(2)}, u32[]{:S(2)}) %collective-permute-start.8) | collective-permute-done | bytes 131104 | tf_op jit(solution)/shard_map/ppermute | solution.py:199
  38.4 3.7 %collective-permute-done.7 = bf16[8,8,1024]{2,1,0:T(8,128)(2,1)S(1)} collective-permute-done((bf16[8,8,1024]{2,1,0:T(8,128)(2,1)S(1)}, bf16[8,8,1024]{2,1,0:T(8,128)(2,1)S(1)}, u32[]{:S(2)}, u32[]{:S(2)}) %collective-permute-start.7) | collective-permute-done | bytes 131104 | tf_op jit(solution)/shard_map/ppermute | solution.py:199
  42.1 0.1 collective-permute-done.6
  42.2 0.0 collective-permute-done.10.left
  42.2 0.0 copy-start
  42.2 0.0 collective-permute-done.9.right
  42.2 0.0 copy-start.1
  42.2 0.1 pad_maximum_fusion.mine
  42.3 0.1 collective-permute-start.14
  42.4 0.0 copy-done.2
  42.4 0.1 concatenate.9.place
  42.5 6.3 %collective-permute-start.11 = (bf16[3,8,8,1024]{3,2,1,0:T(8,128)(2,1)S(1)}, bf16[3,8,8,1024]{3,2,1,0:T(8,128)(2,1)S(1)}, u32[]{:S(2)}, u32[]{:S(2)}) collective-permute-start(bf16[3,8,8,1024]{3,2,1,0:T(8,128)(2,1)S(1)} %pad_maximum_fusion.3.near), channel_id=1, source_target_pairs={{0,64},{1,65},{64,128},{65,129},{128,192},{129,193},{192,32},{193,... | collective-permute-start | bytes 1179656 | tf_op jit(solution)/shard_map/ppermute | solution.py:195
  48.9 1.9 %collective-permute-start.13 = (bf16[2,8,8,1024]{3,2,1,0:T(8,128)(2,1)S(1)}, bf16[2,8,8,1024]{3,2,1,0:T(8,128)(2,1)S(1)}, u32[]{:S(2)}, u32[]{:S(2)}) collective-permute-start(bf16[2,8,8,1024]{3,2,1,0:T(8,128)(2,1)S(1)} %get-tuple-element.69), channel_id=1, source_target_pairs={{0,16},{1,17},{64,80},{65,81},{128,144},{129,145},{192,208},{193,2... | collective-permute-start | bytes 786440 | tf_op jit(solution)/shard_map/ppermute | solution.py:195
  50.8 0.0 slice-start
  50.8 0.0 slice-start.1
  50.8 0.0 collective-permute-start.12
  50.8 0.0 collective-permute-done.14.other
  50.8 7.5 %shard_map.119 = (f32[2,2,16,8,1024]{4,3,2,1,0:T(8,128)S(1)}, f32[2,2,16,8,1024]{4,3,2,1,0:T(8,128)S(1)}) custom-call(s32[25]{0:T(128)S(1)} %concatenate.9.place, bf16[3,8,8,1024]{3,2,1,0:T(8,128)(2,1)S(1)} %pad_maximum_fusion.3.near, bf16[3,8,8,1024]{3,2,1,0:T(8,128)(2,1)S(1)} %collective-permute-done.10.left, ...), custom_call_target="tpu_custom_call" | custom-call | flops 8000000000 | bytes 8388608 | tf_op jit(solution)/shard_map/pallas_call | solution.py:365
  58.3 0.0 copy-done
  58.3 0.0 copy-done.1
  58.3 0.6 collective-permute-done.13.across_near
  58.9 0.0 slice-start.2
  58.9 0.0 slice-start.3
  58.9 1.2 %collective-permute-done.12.down = bf16[2,8,8,1024]{3,2,1,0:T(8,128)(2,1)S(1)} collective-permute-done((bf16[2,8,8,1024]{3,2,1,0:T(8,128)(2,1)S(1)}, bf16[2,8,8,1024]{3,2,1,0:T(8,128)(2,1)S(1)}, u32[]{:S(2)}, u32[]{:S(2)}) %collective-permute-start.12) | collective-permute-done | bytes 262176 | tf_op jit(solution)/shard_map/ppermute | solution.py:195
  60.1 0.0 collective-permute-done.11.up
  60.2 0.7 collective-permute-start.18
  60.9 2.6 %collective-permute-start.17 = (bf16[4,8,8,1024]{3,2,1,0:T(8,128)(2,1)S(1)}, bf16[4,8,8,1024]{3,2,1,0:T(8,128)(2,1)S(1)}, u32[]{:S(2)}, u32[]{:S(2)}) collective-permute-start(bf16[4,8,8,1024]{3,2,1,0:T(8,128)(2,1)S(1)} %pad_maximum_fusion.2), channel_id=1, source_target_pairs={{0,24},{1,25},{64,88},{65,89},{128,152},{129,153},{192,216},{193,2... | collective-permute-start | bytes 1572872 | tf_op jit(solution)/shard_map/ppermute | solution.py:195
  63.6 1.6 %collective-permute-start.16 = (bf16[3,8,8,1024]{3,2,1,0:T(8,128)(2,1)S(1)}, bf16[3,8,8,1024]{3,2,1,0:T(8,128)(2,1)S(1)}, u32[]{:S(2)}, u32[]{:S(2)}) collective-permute-start(bf16[3,8,8,1024]{3,2,1,0:T(8,128)(2,1)S(1)} %pad_maximum_fusion.4), channel_id=1, source_target_pairs={{0,64},{1,65},{64,128},{65,129},{128,192},{129,193},{192,32},{193,... | collective-permute-start | bytes 1179656 | tf_op jit(solution)/shard_map/ppermute | solution.py:195
  65.1 0.0 slice-done.2
  65.1 0.0 slice-done.3
  65.1 0.1 pad_maximum_fusion.1
  65.2 0.8 collective-permute-start.15
  66.0 0.0 slice-done
  66.0 0.0 slice-done.1
  66.1 9.7 %shard_map.120 = (bf16[16,2,4,8,4000]{4,3,2,1,0:T(8,128)(2,1)}, f32[2,16,8,1024]{3,2,1,0:T(8,128)S(1)}) custom-call(s32[25]{0:T(128)S(1)} %concatenate.9.place, f32[2,2,16,8,1024]{4,3,2,1,0:T(8,128)S(1)} %get-tuple-element.60.kept, bf16[3,8,8,1024]{3,2,1,0:T(8,128)(2,1)S(1)} %collective-permute-done.11.up, ...), custom_call_target="tpu_custom_call" | custom-call | flops 10000000000 | bytes 16777216 | tf_op jit(solution)/shard_map/pallas_call | solution.py:399
  75.7 0.0 collective-permute-done.16.up
  75.7 0.0 collective-permute-done.18.left
  75.8 0.0 collective-permute-done.17.right
  75.8 3.6 %collective-permute-done.15.down = bf16[4,8,8,1024]{3,2,1,0:T(8,128)(2,1)S(1)} collective-permute-done((bf16[4,8,8,1024]{3,2,1,0:T(8,128)(2,1)S(1)}, bf16[4,8,8,1024]{3,2,1,0:T(8,128)(2,1)S(1)}, u32[]{:S(2)}, u32[]{:S(2)}) %collective-permute-start.15) | collective-permute-done | bytes 524320 | tf_op jit(solution)/shard_map/ppermute | solution.py:195
  79.3 19.8 %shard_map.121 = bf16[16,2,4,8,4000]{4,3,2,1,0:T(8,128)(2,1)} custom-call(s32[25]{0:T(128)S(1)} %concatenate.9.place, bf16[4,8,8,1024]{3,2,1,0:T(8,128)(2,1)S(1)} %collective-permute-done.18.left, bf16[4,8,8,1024]{3,2,1,0:T(8,128)(2,1)S(1)} %collective-permute-done.17.right, ...), custom_call_target="tpu_custom_call", output_to_operand_aliasing={{}: (9, {})} | custom-call | flops 8388608000 | bytes 25165824 | tf_op jit(solution)/shard_map/pallas_call | solution.py:463
  (9 shorter events, 0.2 us)
Async XLA Ops:
  0.0 36.7 %copy-start.3 = (s32[8]{0:T(128)S(1)}, s32[8]{0:T(128)}, u32[]{:S(2)}) copy-start(s32[8]{0:T(128)} %constant.143.clone) | copy-start | bytes 100
  8.1 34.4 %copy-start.2 = (s32[4]{0:T(128)S(1)}, s32[4]{0:T(128)}, u32[]{:S(2)}) copy-start(s32[4]{0:T(128)} %constant.144.clone) | copy-start | bytes 52
  8.1 9.0 %collective-permute-start.2 = (bf16[8,8,1024]{2,1,0:T(8,128)(2,1)}, bf16[8,8,1024]{2,1,0:T(8,128)(2,1)S(1)}, u32[]{:S(2)}, u32[]{:S(2)}) collective-permute-start(bf16[8,8,1024]{2,1,0:T(8,128)(2,1)} %get-tuple-element.34), channel_id=1, source_target_pairs={{0,4},{1,5},{64,68},{65,69},{128,132},{129,133},{192,196},{193,197... | collective-permute-start | bytes 393224 | tf_op jit(solution)/shard_map/ppermute | solution.py:195
  11.4 8.7 %collective-permute-start.1 = (bf16[8,8,1024]{2,1,0:T(8,128)(2,1)}, bf16[8,8,1024]{2,1,0:T(8,128)(2,1)S(1)}, u32[]{:S(2)}, u32[]{:S(2)}) collective-permute-start(bf16[8,8,1024]{2,1,0:T(8,128)(2,1)} %get-tuple-element.34), channel_id=1, source_target_pairs={{0,6},{1,7},{64,70},{65,71},{128,134},{129,135},{192,198},{193,199... | collective-permute-start | bytes 393224 | tf_op jit(solution)/shard_map/ppermute | solution.py:195
  12.4 7.7 %collective-permute-start = (bf16[8,8,1024]{2,1,0:T(8,128)(2,1)}, bf16[8,8,1024]{2,1,0:T(8,128)(2,1)S(1)}, u32[]{:S(2)}, u32[]{:S(2)}) collective-permute-start(bf16[8,8,1024]{2,1,0:T(8,128)(2,1)} %get-tuple-element.34), channel_id=1, source_target_pairs={{0,2},{1,3},{64,66},{65,67},{128,130},{129,131},{192,194},{193,195... | collective-permute-start | bytes 393224 | tf_op jit(solution)/shard_map/ppermute | solution.py:195
  13.4 11.4 %collective-permute-start.5 = (bf16[8,8,1024]{2,1,0:T(8,128)(2,1)}, bf16[8,8,1024]{2,1,0:T(8,128)(2,1)S(1)}, u32[]{:S(2)}, u32[]{:S(2)}) collective-permute-start(bf16[8,8,1024]{2,1,0:T(8,128)(2,1)} %get-tuple-element.35), channel_id=1, source_target_pairs={{0,96},{1,97},{64,160},{65,161},{128,224},{129,225},{192,0},{193,1... | collective-permute-start | bytes 393224 | tf_op jit(solution)/shard_map/ppermute | solution.py:195
  13.4 11.4 %collective-permute-start.4 = (bf16[8,8,1024]{2,1,0:T(8,128)(2,1)}, bf16[8,8,1024]{2,1,0:T(8,128)(2,1)S(1)}, u32[]{:S(2)}, u32[]{:S(2)}) collective-permute-start(bf16[8,8,1024]{2,1,0:T(8,128)(2,1)} %get-tuple-element.35), channel_id=1, source_target_pairs={{0,128},{1,129},{64,192},{65,193},{128,32},{129,33},{192,96},{193,... | collective-permute-start | bytes 393224 | tf_op jit(solution)/shard_map/ppermute | solution.py:195
  17.1 7.7 %collective-permute-start.3 = (bf16[8,8,1024]{2,1,0:T(8,128)(2,1)}, bf16[8,8,1024]{2,1,0:T(8,128)(2,1)S(1)}, u32[]{:S(2)}, u32[]{:S(2)}) collective-permute-start(bf16[8,8,1024]{2,1,0:T(8,128)(2,1)} %get-tuple-element.35), channel_id=1, source_target_pairs={{0,16},{1,17},{64,80},{65,81},{128,144},{129,145},{192,208},{193,2... | collective-permute-start | bytes 393224 | tf_op jit(solution)/shard_map/ppermute | solution.py:195
  25.7 16.4 %collective-permute-start.10 = (bf16[3,8,8,1024]{3,2,1,0:T(8,128)(2,1)S(1)}, bf16[3,8,8,1024]{3,2,1,0:T(8,128)(2,1)S(1)}, u32[]{:S(2)}, u32[]{:S(2)}) collective-permute-start(bf16[3,8,8,1024]{3,2,1,0:T(8,128)(2,1)S(1)} %pad_maximum_fusion.3.near), channel_id=1, source_target_pairs={{0,8},{1,9},{64,72},{65,73},{128,136},{129,137},{192,200},{193,201... | collective-permute-start | bytes 1179656 | tf_op jit(solution)/shard_map/ppermute | solution.py:195
  27.3 14.8 %collective-permute-start.9 = (bf16[3,8,8,1024]{3,2,1,0:T(8,128)(2,1)S(1)}, bf16[3,8,8,1024]{3,2,1,0:T(8,128)(2,1)S(1)}, u32[]{:S(2)}, u32[]{:S(2)}) collective-permute-start(bf16[3,8,8,1024]{3,2,1,0:T(8,128)(2,1)S(1)} %pad_maximum_fusion.3.near), channel_id=1, source_target_pairs={{0,24},{1,25},{64,88},{65,89},{128,152},{129,153},{192,216},{193,2... | collective-permute-start | bytes 1179656 | tf_op jit(solution)/shard_map/ppermute | solution.py:195
  30.0 8.4 %collective-permute-start.8 = (bf16[8,8,1024]{2,1,0:T(8,128)(2,1)S(1)}, bf16[8,8,1024]{2,1,0:T(8,128)(2,1)S(1)}, u32[]{:S(2)}, u32[]{:S(2)}) collective-permute-start(bf16[8,8,1024]{2,1,0:T(8,128)(2,1)S(1)} %get-tuple-element.65), channel_id=1, source_target_pairs={{0,192},{64,0},{128,64},{192,128},{1,193},{65,1},{129,65},{193,129... | collective-permute-start | bytes 393224 | tf_op jit(solution)/shard_map/ppermute | solution.py:199
  32.3 9.8 %collective-permute-start.7 = (bf16[8,8,1024]{2,1,0:T(8,128)(2,1)S(1)}, bf16[8,8,1024]{2,1,0:T(8,128)(2,1)S(1)}, u32[]{:S(2)}, u32[]{:S(2)}) collective-permute-start(bf16[8,8,1024]{2,1,0:T(8,128)(2,1)S(1)} %get-tuple-element.66), channel_id=1, source_target_pairs={{0,128},{64,192},{128,0},{192,64},{1,129},{65,193},{129,1},{193,65... | collective-permute-start | bytes 393224 | tf_op jit(solution)/shard_map/ppermute | solution.py:199
  34.3 7.9 %collective-permute-start.6 = (bf16[8,8,1024]{2,1,0:T(8,128)(2,1)S(1)}, bf16[8,8,1024]{2,1,0:T(8,128)(2,1)S(1)}, u32[]{:S(2)}, u32[]{:S(2)}) collective-permute-start(bf16[8,8,1024]{2,1,0:T(8,128)(2,1)S(1)} %get-tuple-element.67), channel_id=1, source_target_pairs={{0,64},{64,128},{128,192},{192,0},{1,65},{65,129},{129,193},{193,1... | collective-permute-start | bytes 393224 | tf_op jit(solution)/shard_map/ppermute | solution.py:199
  42.2 16.1 %copy-start = (bf16[3,8,8,1024]{3,2,1,0:T(8,128)(2,1)}, bf16[3,8,8,1024]{3,2,1,0:T(8,128)(2,1)S(1)}, u32[]{:S(2)}) copy-start(bf16[3,8,8,1024]{3,2,1,0:T(8,128)(2,1)S(1)} %collective-permute-done.10.left) | copy-start | bytes 1179652
  42.2 16.1 %copy-start.1 = (bf16[3,8,8,1024]{3,2,1,0:T(8,128)(2,1)}, bf16[3,8,8,1024]{3,2,1,0:T(8,128)(2,1)S(1)}, u32[]{:S(2)}) copy-start(bf16[3,8,8,1024]{3,2,1,0:T(8,128)(2,1)S(1)} %collective-permute-done.9.right) | copy-start | bytes 1179652
  42.3 8.5 %collective-permute-start.14 = (bf16[4,8,8,1024]{3,2,1,0:T(8,128)(2,1)S(1)}, bf16[4,8,8,1024]{3,2,1,0:T(8,128)(2,1)S(1)}, u32[]{:S(2)}, u32[]{:S(2)}) collective-permute-start(bf16[4,8,8,1024]{3,2,1,0:T(8,128)(2,1)S(1)} %pad_maximum_fusion.mine), channel_id=1, source_target_pairs={{0,1},{1,0},{64,65},{65,64},{128,129},{129,128},{192,193},{193,192... | collective-permute-start | bytes 1572872 | tf_op jit(solution)/shard_map/ppermute | solution.py:195
  42.5 17.6 %collective-permute-start.11 = (bf16[3,8,8,1024]{3,2,1,0:T(8,128)(2,1)S(1)}, bf16[3,8,8,1024]{3,2,1,0:T(8,128)(2,1)S(1)}, u32[]{:S(2)}, u32[]{:S(2)}) collective-permute-start(bf16[3,8,8,1024]{3,2,1,0:T(8,128)(2,1)S(1)} %pad_maximum_fusion.3.near), channel_id=1, source_target_pairs={{0,64},{1,65},{64,128},{65,129},{128,192},{129,193},{192,32},{193,... | collective-permute-start | bytes 1179656 | tf_op jit(solution)/shard_map/ppermute | solution.py:195
  48.9 10.0 %collective-permute-start.13 = (bf16[2,8,8,1024]{3,2,1,0:T(8,128)(2,1)S(1)}, bf16[2,8,8,1024]{3,2,1,0:T(8,128)(2,1)S(1)}, u32[]{:S(2)}, u32[]{:S(2)}) collective-permute-start(bf16[2,8,8,1024]{3,2,1,0:T(8,128)(2,1)S(1)} %get-tuple-element.69), channel_id=1, source_target_pairs={{0,16},{1,17},{64,80},{65,81},{128,144},{129,145},{192,208},{193,2... | collective-permute-start | bytes 786440 | tf_op jit(solution)/shard_map/ppermute | solution.py:195
  50.8 15.3 %slice-start = ((s8[8388608]{0:T(1024)(128)(4,1)}), s8[4194304]{0:T(1024)(128)(4,1)S(1)}, s32[]{:S(2)}) async-start(s8[8388608]{0:T(1024)(128)(4,1)} %bitcast.10), calls=%async_computation | async-start | bytes 8388608
  50.8 15.3 %slice-start.1 = ((s8[8388608]{0:T(1024)(128)(4,1)}), s8[4194304]{0:T(1024)(128)(4,1)S(1)}, s32[]{:S(2)}) async-start(s8[8388608]{0:T(1024)(128)(4,1)} %bitcast.10), calls=%async_computation.1 | async-start | bytes 8388608
  50.8 9.3 %collective-permute-start.12 = (bf16[2,8,8,1024]{3,2,1,0:T(8,128)(2,1)S(1)}, bf16[2,8,8,1024]{3,2,1,0:T(8,128)(2,1)S(1)}, u32[]{:S(2)}, u32[]{:S(2)}) collective-permute-start(bf16[2,8,8,1024]{3,2,1,0:T(8,128)(2,1)S(1)} %get-tuple-element.70), channel_id=1, source_target_pairs={{0,224},{1,225},{64,0},{65,1},{128,64},{129,65},{192,128},{193,129... | collective-permute-start | bytes 786440 | tf_op jit(solution)/shard_map/ppermute | solution.py:195
  58.9 6.2 %slice-start.2 = ((bf16[3,8,8,1024]{3,2,1,0:T(8,128)(2,1)}), bf16[1,8,8,1024]{3,2,1,0:T(8,128)(2,1)S(1)}, s32[]{:S(2)}) async-start(bf16[3,8,8,1024]{3,2,1,0:T(8,128)(2,1)} %copy-done), calls=%async_computation.2 | async-start | bytes 262144 | tf_op jit(solution)/shard_map/slice | solution.py:253
  58.9 6.2 %slice-start.3 = ((bf16[3,8,8,1024]{3,2,1,0:T(8,128)(2,1)}), bf16[1,8,8,1024]{3,2,1,0:T(8,128)(2,1)S(1)}, s32[]{:S(2)}) async-start(bf16[3,8,8,1024]{3,2,1,0:T(8,128)(2,1)} %copy-done.1), calls=%async_computation.3 | async-start | bytes 262144 | tf_op jit(solution)/shard_map/slice | solution.py:253
  60.2 15.6 %collective-permute-start.18 = (bf16[4,8,8,1024]{3,2,1,0:T(8,128)(2,1)S(1)}, bf16[4,8,8,1024]{3,2,1,0:T(8,128)(2,1)S(1)}, u32[]{:S(2)}, u32[]{:S(2)}) collective-permute-start(bf16[4,8,8,1024]{3,2,1,0:T(8,128)(2,1)S(1)} %pad_maximum_fusion.2), channel_id=1, source_target_pairs={{0,8},{1,9},{64,72},{65,73},{128,136},{129,137},{192,200},{193,201... | collective-permute-start | bytes 1572872 | tf_op jit(solution)/shard_map/ppermute | solution.py:195
  60.9 14.9 %collective-permute-start.17 = (bf16[4,8,8,1024]{3,2,1,0:T(8,128)(2,1)S(1)}, bf16[4,8,8,1024]{3,2,1,0:T(8,128)(2,1)S(1)}, u32[]{:S(2)}, u32[]{:S(2)}) collective-permute-start(bf16[4,8,8,1024]{3,2,1,0:T(8,128)(2,1)S(1)} %pad_maximum_fusion.2), channel_id=1, source_target_pairs={{0,24},{1,25},{64,88},{65,89},{128,152},{129,153},{192,216},{193,2... | collective-permute-start | bytes 1572872 | tf_op jit(solution)/shard_map/ppermute | solution.py:195
  63.6 12.2 %collective-permute-start.16 = (bf16[3,8,8,1024]{3,2,1,0:T(8,128)(2,1)S(1)}, bf16[3,8,8,1024]{3,2,1,0:T(8,128)(2,1)S(1)}, u32[]{:S(2)}, u32[]{:S(2)}) collective-permute-start(bf16[3,8,8,1024]{3,2,1,0:T(8,128)(2,1)S(1)} %pad_maximum_fusion.4), channel_id=1, source_target_pairs={{0,64},{1,65},{64,128},{65,129},{128,192},{129,193},{192,32},{193,... | collective-permute-start | bytes 1179656 | tf_op jit(solution)/shard_map/ppermute | solution.py:195
  65.2 14.1 %collective-permute-start.15 = (bf16[4,8,8,1024]{3,2,1,0:T(8,128)(2,1)S(1)}, bf16[4,8,8,1024]{3,2,1,0:T(8,128)(2,1)S(1)}, u32[]{:S(2)}, u32[]{:S(2)}) collective-permute-start(bf16[4,8,8,1024]{3,2,1,0:T(8,128)(2,1)S(1)} %pad_maximum_fusion.1), channel_id=1, source_target_pairs={{0,224},{1,225},{64,0},{65,1},{128,64},{129,65},{192,128},{193,129... | collective-permute-start | bytes 1572872 | tf_op jit(solution)/shard_map/ppermute | solution.py:195
